TPU v7x, 32 devices: a whole 2x2x4 slice. The times are simulated.
32 devices in a mesh: pb: 4 (over y, x), ga: 8 (over z, core).
Axes of the slice: x: 2, y: 2, z: 4, core: 2. Of those that a mesh axis runs over, the one named last changes fastest.
Arguments:
- valence: bfloat16 [24, 4, 16, 768], P('pb', None, None, 'ga'), may hold values from -6 to 6
- conduction: bfloat16 [24, 4, 8, 768], P('pb', None, None, 'ga'), may hold values from -6 to 6
- screened: bfloat16 [4, 768, 768], P('pb', 'ga'), as said below
- kq_table: int32 [24, 4], P('pb'), may hold values from 0 to 3, each once within a row
Outputs:
- kernel: float32 [24, 4, 8, 16], P('pb')
Inputs may be any that keep to these rules, and one draw needn't show every extreme that they name: screened is symmetric in its last two dimensions: screened[q, G, H] = screened[q, H, G] exactly. Each row of kq_table names every label of 0 to 3 once.
All inputs are finite; a program needn't handle non-finite values.
Results may differ from a plain program's by a relative error of at most 0.0003.
Values may be sent and summed in bfloat16 or wider, within the bound.
No kernel may reach another device: no remote copies, remote signals or barrier semaphores. Data moves between devices by JAX's collectives and lax.ppermute only.
A program may use at most 128 MiB of HBM per device.

v0:
```python
import jax
import jax.numpy as jnp
from jax import lax
from jax.sharding import PartitionSpec as P


def per_device(valence, conduction, screened, kq_table):
    valence_q, conduction_q = (
        lax.all_to_all(valence, "pb", split_axis=1, concat_axis=0, tiled=True),
        lax.all_to_all(conduction, "pb", split_axis=1, concat_axis=0, tiled=True),
    )
    applied = jnp.einsum(
        "qgh,kqph->qgkp",
        screened,
        lax.all_gather(conduction_q, "ga", axis=3, tiled=True),
        preferred_element_type=jnp.float32,
    )
    partial_value = jnp.einsum(
        "kqvg,qgkc->kqcv", valence_q.astype(jnp.float32), applied, precision=lax.Precision.HIGHEST
    )
    summed = lax.psum(partial_value, "ga")
    returned = lax.all_to_all(summed, "pb", split_axis=0, concat_axis=1, tiled=True)
    q_total = returned.shape[1]
    labels = lax.iota(jnp.int32, q_total)
    onehot = (kq_table[:, :, None] == labels[None, None, :]).astype(jnp.float32)
    kernel = jnp.einsum("kqj,kqcv->kjcv", onehot, returned, precision=lax.Precision.HIGHEST)
    return kernel


def solution(mesh):
    return jax.shard_map(
        per_device,
        mesh=mesh,
        in_specs=(
            P("pb", None, None, "ga"),
            P("pb", None, None, "ga"),
            P("pb", "ga", None),
            P("pb", None),
        ),
        out_specs=P("pb", None, None, None),
        check_vma=False,
    )
```

profile of v0, /device:TPU:0, one launch (start us, length us, event | category | flops | bytes accessed | tf_op | source)
XLA Modules:
  0.0 76.7 jit_solution(12857044515483267820)
XLA Ops:
  0.0 0.0 copy-start
  0.0 1.5 %copy.23 = bf16[6,4,8,96]{3,2,0,1:T(8,128)(2,1)} copy(bf16[6,4,8,96]{3,2,1,0:T(8,128)(2,1)} %param.5) | data formatting | bytes 73728 | tf_op args[1]
  1.5 5.2 %all-to-all-start = ((bf16[6,4,8,96]{3,2,0,1:T(8,128)(2,1)}), bf16[6,4,8,96]{3,2,0,1:T(8,128)(2,1)S(1)}, u32[]{:S(2)}, u32[]{:S(2)}) async-start(bf16[6,4,8,96]{3,2,0,1:T(8,128)(2,1)} %copy.23), calls=%async_computation | async-start | bytes 98304 | tf_op jit(solution)/shard_map/all_to_all | solution.py:10
  6.6 1.5 %copy.26 = bf16[6,4,16,96]{3,2,0,1:T(8,128)(2,1)} copy(bf16[6,4,16,96]{3,2,1,0:T(8,128)(2,1)} %param.4) | data formatting | bytes 147456 | tf_op args[0]
  8.2 3.3 %all-to-all-done = bf16[6,4,8,96]{3,2,0,1:T(8,128)(2,1)S(1)} async-done(((bf16[6,4,8,96]{3,2,0,1:T(8,128)(2,1)}), bf16[6,4,8,96]{3,2,0,1:T(8,128)(2,1)S(1)}, u32[]{:S(2)}, u32[]{:S(2)}) %all-to-all-start) | async-done | bytes 36896 | tf_op jit(solution)/shard_map/all_to_all | solution.py:10
  11.4 3.3 %all-to-all-start.1 = ((bf16[6,4,16,96]{3,2,0,1:T(8,128)(2,1)}), bf16[6,4,16,96]{3,2,0,1:T(8,128)(2,1)S(1)}, u32[]{:S(2)}, u32[]{:S(2)}) async-start(bf16[6,4,16,96]{3,2,0,1:T(8,128)(2,1)} %copy.26), calls=%async_computation.1 | async-start | bytes 196608 | tf_op jit(solution)/shard_map/all_to_all | solution.py:9
  14.7 0.2 copy.24
  14.9 19.9 %all_gather.3 = bf16[24,1,8,768]{0,2,1,3:T(8,128)(2,1)S(1)} all-gather(bf16[24,1,8,96]{0,2,1,3:T(8,128)(2,1)S(1)} %copy.24), channel_id=1, replica_groups=mesh['pb'=4,'ga'=8] {'ga'}, dimensions={3}, use_global_device_ids=true | all-gather | bytes 331776 | tf_op jit(solution)/shard_map/all_gather | solution.py:15
  34.8 0.9 %copy.25 = bf16[24,1,8,768]{3,0,2,1:T(8,128)(2,1)S(1)} copy(bf16[24,1,8,768]{0,2,1,3:T(8,128)(2,1)S(1)} %all_gather.3) | data formatting | bytes 589824 | tf_op jit(solution)/shard_map/all_gather | solution.py:15
  35.7 0.0 copy-done
  35.7 0.2 fusion
  36.0 0.0 all-to-all-done.1
  36.0 0.3 convolution_bitcast_fusion
  36.3 28.6 %psum.7 = f32[24,1,8,16]{3,2,0,1:T(8,128)S(1)} all-reduce(f32[24,1,8,16]{3,2,0,1:T(8,128)S(1)} %convolution_bitcast_fusion), channel_id=1, replica_groups=mesh['pb'=4,'ga'=8] {'ga'}, use_global_device_ids=true, to_apply=%region_0.0 | all-reduce | flops 3072 | bytes 24576 | tf_op jit(solution)/shard_map/psum | solution.py:21
  64.9 0.7 reshape.20
  65.6 4.2 %all-to-all-start.2 = ((f32[4,1,768]{2,1,0:T(1,128)}), f32[4,1,768]{2,1,0:T(1,128)S(1)}, u32[]{:S(2)}, u32[]{:S(2)}) async-start(f32[4,1,768]{2,1,0:T(1,128)} %reshape.20), calls=%async_computation.2 | async-start | bytes 24576 | tf_op jit(solution)/shard_map/all_to_all | solution.py:22
  69.8 0.0 copy-done.1
  69.8 0.1 copy.22
  69.9 4.6 %all-to-all-done.2 = f32[4,1,768]{2,1,0:T(1,128)S(1)} async-done(((f32[4,1,768]{2,1,0:T(1,128)}), f32[4,1,768]{2,1,0:T(1,128)S(1)}, u32[]{:S(2)}, u32[]{:S(2)}) %all-to-all-start.2) | async-done | bytes 12320 | tf_op jit(solution)/shard_map/all_to_all | solution.py:22
  74.5 0.5 broadcast.1
  75.0 0.7 reduce
  75.7 0.1 reshape.21
  75.8 0.2 fusion.3
  76.0 0.6 copy.30
  (1 shorter events, 0.0 us)
Async XLA Ops:
  0.0 35.7 %copy-start = (bf16[1,96,768]{2,1,0:T(8,128)(2,1)S(1)}, bf16[1,96,768]{2,1,0:T(8,128)(2,1)}, u32[]{:S(2)}) copy-start(bf16[1,96,768]{2,1,0:T(8,128)(2,1)} %param.6) | copy-start | bytes 442372
  1.5 10.0 %all-to-all-start = ((bf16[6,4,8,96]{3,2,0,1:T(8,128)(2,1)}), bf16[6,4,8,96]{3,2,0,1:T(8,128)(2,1)S(1)}, u32[]{:S(2)}, u32[]{:S(2)}) async-start(bf16[6,4,8,96]{3,2,0,1:T(8,128)(2,1)} %copy.23), calls=%async_computation | async-start | bytes 98304 | tf_op jit(solution)/shard_map/all_to_all | solution.py:10
  11.4 24.6 %all-to-all-start.1 = ((bf16[6,4,16,96]{3,2,0,1:T(8,128)(2,1)}), bf16[6,4,16,96]{3,2,0,1:T(8,128)(2,1)S(1)}, u32[]{:S(2)}, u32[]{:S(2)}) async-start(bf16[6,4,16,96]{3,2,0,1:T(8,128)(2,1)} %copy.26), calls=%async_computation.1 | async-start | bytes 196608 | tf_op jit(solution)/shard_map/all_to_all | solution.py:9
  34.8 35.0 %copy-start.1 = (s32[6,4]{0,1:T(4,128)S(1)}, s32[6,4]{0,1:T(4,128)}, u32[]{:S(2)}) copy-start(s32[6,4]{0,1:T(4,128)} %param.7) | copy-start | bytes 292
  65.6 8.9 %all-to-all-start.2 = ((f32[4,1,768]{2,1,0:T(1,128)}), f32[4,1,768]{2,1,0:T(1,128)S(1)}, u32[]{:S(2)}, u32[]{:S(2)}) async-start(f32[4,1,768]{2,1,0:T(1,128)} %reshape.20), calls=%async_computation.2 | async-start | bytes 24576 | tf_op jit(solution)/shard_map/all_to_all | solution.py:22
where the time goes:
time: 77.1 us; the launch traced here: 76.7 us
  blocking collectives  48.5 us (63%)
  starting transfers between devices  12.6 us (16%)
  waiting for transfers between devices  7.87 us (10%)
  local copies, waits for them, and re-layouts  6.16 us (8%)
    psum x1, blocking collectives, per_device(): summed = lax.psum(partial_value, 'ga')  28.6 us
    all_gather x1, blocking collectives, per_device(): lax.all_gather(conduction_q, 'ga', axis=3, tiled=True)  19.9 us
    all_to_all x1, starting transfers between devices, per_device(): lax.all_to_all(conduction, 'pb', split_axis=1, concat_axis=0, tiled=True)  5.16 us
    all_to_all x1, waiting for transfers between devices, per_device(): lax.all_to_all(summed, 'pb', split_axis=0, concat_axis=1, tiled=True)  4.61 us
    all_to_all x1, starting transfers between devices, per_device(): lax.all_to_all(summed, 'pb', split_axis=0, concat_axis=1, tiled=True)  4.16 us
    unnamed x9, local copies, waits for them, and re-layouts  3.89 us
    all_to_all x1, starting transfers between devices, per_device(): lax.all_to_all(valence, 'pb', split_axis=1, concat_axis=0, tiled=True)  3.31 us
    all_to_all x1, waiting for transfers between devices, per_device(): lax.all_to_all(conduction, 'pb', split_axis=1, concat_axis=0, tiled=True)  3.26 us
  transfers between devices with their start and end apart: 3, of which 2 were waited for; matrix products, arithmetic and copies ran while one was open for 4% of the time, Pallas kernels for 0%

commit v1 on v0

v1 whole, which is shorter than its diff:
```python
import functools

import jax
import jax.numpy as jnp
from jax import lax
from jax.experimental import pallas as pl
from jax.experimental.pallas import tpu as pltpu
from jax.sharding import PartitionSpec as P

CORES = 2
LANES = 128


def partner(i, s, n):
    return i ^ s if n & (n - 1) == 0 else (i + s) % n


def source(i, s, n):
    return jnp.bitwise_xor(i, s) if n & (n - 1) == 0 else lax.rem(i + (n - s), n)


def send_pb(x, s, npb):
    return lax.ppermute(x, "pb", [(i, partner(i, s, npb)) for i in range(npb)])


def send_chip(x, s, nz):
    return lax.ppermute(
        x,
        "ga",
        [(i * CORES + c, partner(i, s, nz) * CORES + c) for i in range(nz) for c in range(CORES)],
    )


def send_core(x, nz):
    return lax.ppermute(
        x, "ga", [(i * CORES + c, i * CORES + 1 - c) for i in range(nz) for c in range(CORES)]
    )


def dot_nt(a, b):
    return lax.dot_general(a, b, (((1,), (1,)), ((), ())), preferred_element_type=jnp.float32)


def partial_kernel(npb, nz, *refs):
    w_refs, mine_refs = refs[:npb], refs[npb : npb + nz]
    other_ref, val_ref, out_ref, slab_ref, full_ref = refs[npb + nz :]
    nk, nq, nc, ng = mine_refs[0].shape
    nv = val_ref.shape[2]
    per_tile = LANES // nv
    pb, ga = lax.axis_index("pb"), lax.axis_index("ga")
    z, core = lax.div(ga, CORES), lax.rem(ga, CORES)
    for s in range(nz):
        first = source(z, s, nz) * CORES
        slab_ref[first + core] = mine_refs[s][...]
        slab_ref[first + 1 - core] = other_ref[s]
    lane_block = lax.broadcasted_iota(jnp.int32, (nc, LANES), 1) // nv
    tiles = [jnp.zeros((nc, LANES), jnp.float32) for _ in range(out_ref.shape[0])]

    def join(q, _):
        for p in range(nz * CORES):
            piece = slab_ref[p, :, q].astype(jnp.float32).reshape(nk * nc, ng)
            full_ref[q, :, p * ng : (p + 1) * ng] = piece.astype(jnp.bfloat16)

    lax.fori_loop(0, nq, join, None, unroll=min(nq, 4))
    for s in range(npb):
        q = source(pb, s, npb)
        applied = dot_nt(full_ref[q], w_refs[s][0])
        high = applied.astype(jnp.bfloat16)
        low = (applied - high.astype(jnp.float32)).astype(jnp.bfloat16)
        val = val_ref[:, q].astype(jnp.float32).reshape(nk * nv, ng).astype(jnp.bfloat16)
        val = jnp.concatenate([val, jnp.zeros((LANES - nk * nv, ng), jnp.bfloat16)], axis=0)
        product = dot_nt(high, val) + dot_nt(low, val)
        for k in range(nk):
            tile, place = divmod(k * npb + s, per_tile)
            moved = pltpu.roll(
                product[k * nc : (k + 1) * nc], ((place - k) * nv) % LANES, axis=1
            )
            tiles[tile] = jnp.where(lane_block == place, moved, tiles[tile])
    for t, tile in enumerate(tiles):
        out_ref[t] = tile


def place_kernel(npb, nz, *refs):
    share_refs, (kq_ref, out_ref) = refs[:nz], refs[nz:]
    nk, _, _, nv = out_ref.shape
    per_tile = LANES // nv
    pb = lax.axis_index("pb")
    total = share_refs[0][...]
    for share_ref in share_refs[1:]:
        total = total + share_ref[...]
    for s in range(npb):
        q = source(pb, s, npb)
        for k in range(nk):
            tile, place = divmod(k * npb + s, per_tile)
            out_ref[k, kq_ref[k, q]] = total[tile, :, place * nv : (place + 1) * nv]


def per_device(npb, nz, valence, conduction, screened, kq_table):
    nk, nq, nv, ng = valence.shape
    nc = conduction.shape[2]
    vmem = pl.BlockSpec(memory_space=pltpu.VMEM)
    smem = pl.BlockSpec(memory_space=pltpu.SMEM)

    w_parts = [screened] + [send_pb(screened, s, npb) for s in range(1, npb)]
    mine = [conduction] + [send_chip(conduction, s, nz) for s in range(1, nz)]
    other = send_core(jnp.stack(mine), nz)
    n_tiles = -(-nk * nq * nv // LANES)
    partial_value = pl.pallas_call(
        functools.partial(partial_kernel, npb, nz),
        out_shape=jax.ShapeDtypeStruct((n_tiles, nc, LANES), jnp.float32),
        in_specs=[vmem] * (npb + nz + 2),
        out_specs=vmem,
        scratch_shapes=[
            pltpu.VMEM((nz * CORES, nk, nq, nc, ng), jnp.bfloat16),
            pltpu.VMEM((nq, nk * nc, nz * CORES * ng), jnp.bfloat16),
        ],
        compiler_params=pltpu.CompilerParams(vmem_limit_bytes=48 * 2**20),
    )(*w_parts, *mine, other, valence)
    chip_value = partial_value + send_core(partial_value, nz)
    shares = [chip_value] + [send_chip(chip_value, s, nz) for s in range(1, nz)]
    return pl.pallas_call(
        functools.partial(place_kernel, npb, nz),
        out_shape=jax.ShapeDtypeStruct((nk, nq, nc, nv), jnp.float32),
        in_specs=[vmem] * nz + [smem],
        out_specs=vmem,
    )(*shares, kq_table)


def solution(mesh):
    npb, nga = mesh.shape["pb"], mesh.shape["ga"]
    return jax.shard_map(
        functools.partial(per_device, npb, nga // CORES),
        mesh=mesh,
        in_specs=(
            P("pb", None, None, "ga"),
            P("pb", None, None, "ga"),
            P("pb", "ga", None),
            P("pb", None),
        ),
        out_specs=P("pb", None, None, None),
        check_vma=False,
    )
```

time: 77.1 us -> 28.9 us (0.37)
  blocking collectives: 48.5 us -> 0 us
  local copies, waits for them, and re-layouts: 6.16 us -> 1.29 us
  Pallas kernels: 0 us -> 2.85 us
  waiting for transfers between devices: 7.87 us -> 9.93 us
  starting transfers between devices: 12.6 us -> 13.6 us
    psum x1 -> x0, blocking collectives: 28.6 us -> none  [per_device(): summed = lax.psum(partial_value, 'ga')]
    all_gather x1 -> x0, blocking collectives: 19.9 us -> none  [per_device(): lax.all_gather(conduction_q, 'ga', axis=3, tiled=True)]
    ppermute x0 -> x11, starting transfers between devices: none -> 13.6 us  [the longest x6 10 us: send_chip(): lax.ppermute(x, 'ga', [(i * CORES + c, partner(i, s, nz) * CORES + c) for...]
    all_to_all x3 -> x0, starting transfers between devices: 12.6 us -> none  [the longest x1 5.16 us: per_device(): lax.all_to_all(conduction, 'pb', split_axis=1, concat_axis=0, tiled=True)]
    ppermute x0 -> x11, waiting for transfers between devices: none -> 9.93 us  [the longest x6 5.69 us: send_chip(): lax.ppermute(x, 'ga', [(i * CORES + c, partner(i, s, nz) * CORES + c) for...]
    all_to_all x3 -> x0, waiting for transfers between devices: 7.87 us -> none  [the longest x1 4.61 us: per_device(): lax.all_to_all(summed, 'pb', split_axis=0, concat_axis=1, tiled=True)]
    pallas_call x0 -> x2, Pallas kernels: none -> 2.85 us  [the longest x1 1.59 us: per_device(): pl.pallas_call(functools.partial(place_kernel, npb, nz), out_shape=jax.Sh...]
    unnamed x9 -> x17, local copies, waits for them, and re-layouts: 3.89 us -> 1.29 us
  transfers between devices with their start and end apart: 3 -> 11, of which waited for: 2 -> 6; matrix products, arithmetic and copies ran while one was open for 4% -> 6% of each run, Pallas kernels for 0% -> 0%
where the time goes in v1:
time: 28.9 us; the launch traced here: 28.7 us
  starting transfers between devices  13.6 us (47%)
  waiting for transfers between devices  9.93 us (34%)
  Pallas kernels  2.85 us (10%)
  local copies, waits for them, and re-layouts  1.29 us (4%)
  other arithmetic  0.92 us (3%)
    ppermute x6, starting transfers between devices, send_chip(): lax.ppermute(x, 'ga', [(i * CORES + c, partner(i, s, nz) * CORES + c) for...  10 us
    ppermute x6, waiting for transfers between devices, send_chip(): lax.ppermute(x, 'ga', [(i * CORES + c, partner(i, s, nz) * CORES + c) for...  5.69 us
    ppermute x3, starting transfers between devices, send_pb(): return lax.ppermute(x, 'pb', [(i, partner(i, s, npb)) for i in range(npb)])  3.49 us
    ppermute x3, waiting for transfers between devices, send_pb(): return lax.ppermute(x, 'pb', [(i, partner(i, s, npb)) for i in range(npb)])  3.07 us
    pallas_call x1, Pallas kernels, per_device(): pl.pallas_call(functools.partial(place_kernel, npb, nz), out_shape=jax.Sh...  1.59 us
    unnamed x17, local copies, waits for them, and re-layouts  1.29 us
    pallas_call x1, Pallas kernels, per_device(): pl.pallas_call(functools.partial(partial_kernel, npb, nz), out_shape=jax....  1.26 us
    ppermute x2, waiting for transfers between devices, send_core(): lax.ppermute(x, 'ga', [(i * CORES + c, i * CORES + 1 - c) for i in range(...  1.17 us
  transfers between devices with their start and end apart: 11, of which 6 were waited for; matrix products, arithmetic and copies ran while one was open for 6% of the time, Pallas kernels for 0%

profile of v1, /device:TPU:0, one launch (start us, length us, event | category | flops | bytes accessed | tf_op | source)
XLA Modules:
  0.0 28.7 jit_solution(2324167560019724223)
XLA Ops:
  0.0 3.0 %collective-permute-start.3 = (bf16[6,4,8,96]{3,2,1,0:T(8,128)(2,1)}, bf16[6,4,8,96]{3,2,1,0:T(8,128)(2,1)S(1)}, u32[]{:S(2)}, u32[]{:S(2)}) collective-permute-start(bf16[6,4,8,96]{3,2,1,0:T(8,128)(2,1)} %refs_4_.2), channel_id=1, source_target_pairs={{0,2},{1,3},{2,0},{3,1},{4,6},{5,7},{6,4},{7,5},{8,10},{9,11},{10,... | collective-permute-start | bytes 110600 | tf_op jit(solution)/shard_map/ppermute | solution.py:27
  3.0 2.6 %collective-permute-start.4 = (bf16[6,4,8,96]{3,2,1,0:T(8,128)(2,1)}, bf16[6,4,8,96]{3,2,1,0:T(8,128)(2,1)S(1)}, u32[]{:S(2)}, u32[]{:S(2)}) collective-permute-start(bf16[6,4,8,96]{3,2,1,0:T(8,128)(2,1)} %refs_4_.2), channel_id=1, source_target_pairs={{0,4},{1,5},{2,6},{3,7},{4,0},{5,1},{6,2},{7,3},{8,12},{9,13},{10,... | collective-permute-start | bytes 110600 | tf_op jit(solution)/shard_map/ppermute | solution.py:27
  5.6 1.7 %collective-permute-start = (bf16[1,96,768]{2,1,0:T(8,128)(2,1)}, bf16[1,96,768]{2,1,0:T(8,128)(2,1)S(1)}, u32[]{:S(2)}, u32[]{:S(2)}) collective-permute-start(bf16[1,96,768]{2,1,0:T(8,128)(2,1)} %refs_0_.1), channel_id=1, source_target_pairs={{0,8},{8,0},{16,24},{24,16},{1,9},{9,1},{17,25},{25,17},{2,10},{10... | collective-permute-start | bytes 442376 | tf_op jit(solution)/shard_map/ppermute | solution.py:23
  7.3 1.5 %collective-permute-start.1 = (bf16[1,96,768]{2,1,0:T(8,128)(2,1)}, bf16[1,96,768]{2,1,0:T(8,128)(2,1)S(1)}, u32[]{:S(2)}, u32[]{:S(2)}) collective-permute-start(bf16[1,96,768]{2,1,0:T(8,128)(2,1)} %refs_0_.1), channel_id=1, source_target_pairs={{0,16},{8,24},{16,0},{24,8},{1,17},{9,25},{17,1},{25,9},{2,18},{10... | collective-permute-start | bytes 442376 | tf_op jit(solution)/shard_map/ppermute | solution.py:23
  8.8 0.0 collective-permute-done.3.refs_5_
  8.9 0.3 collective-permute-start.2
  9.1 0.0 collective-permute-done.4.refs_6_
  9.2 2.6 %collective-permute-done.5.refs_7_ = bf16[6,4,8,96]{3,2,1,0:T(8,128)(2,1)S(1)} collective-permute-done((bf16[6,4,8,96]{3,2,1,0:T(8,128)(2,1)}, bf16[6,4,8,96]{3,2,1,0:T(8,128)(2,1)S(1)}, u32[]{:S(2)}, u32[]{:S(2)}) %collective-permute-start.5) | collective-permute-done | bytes 36896 | tf_op jit(solution)/shard_map/ppermute | solution.py:27
  11.7 0.9 %pad_maximum_fusion = bf16[4,6,4,8,96]{4,3,2,1,0:T(8,128)(2,1)S(1)} fusion(bf16[1,6,4,8,96]{4,3,2,1,0:T(8,128)(2,1)S(1)} %bitcast.7, bf16[1,6,4,8,96]{4,3,2,1,0:T(8,128)(2,1)S(1)} %bitcast.6, bf16[1,6,4,8,96]{4,3,2,1,0:T(8,128)(2,1)S(1)} %bitcast.5, bf16[1,6,4,8,96]{4,3,2,1,0:T(8,128)(2,1)} %bitcast.4), kind=kLoop, calls=%fused_computation | loop fusion | flops 221184 | bytes 294912 | tf_op jit(solution)/shard_map/stack | solution.py:106
  12.6 0.1 collective-permute-start.6
  12.7 3.1 %collective-permute-done.1.refs_2_ = bf16[1,96,768]{2,1,0:T(8,128)(2,1)S(1)} collective-permute-done((bf16[1,96,768]{2,1,0:T(8,128)(2,1)}, bf16[1,96,768]{2,1,0:T(8,128)(2,1)S(1)}, u32[]{:S(2)}, u32[]{:S(2)}) %collective-permute-start.1) | collective-permute-done | bytes 147488 | tf_op jit(solution)/shard_map/ppermute | solution.py:23
  15.8 0.0 collective-permute-done.2.refs_3_
  15.8 0.0 collective-permute-done.6.refs_8_
  15.8 1.3 %shard_map.46 = f32[3,8,128]{2,1,0:T(8,128)S(1)} custom-call(bf16[1,96,768]{2,1,0:T(8,128)(2,1)S(1)} %copy-done.1, bf16[1,96,768]{2,1,0:T(8,128)(2,1)S(1)} %collective-permute-done.refs_1_, bf16[1,96,768]{2,1,0:T(8,128)(2,1)S(1)} %collective-permute-done.1.refs_2_, bf16[1,96,768]{2,1,0:T(8,128)(2,1)S(1)} %collective-permute-done.2.refs_3_, ...), custom_call_target="tpu_custom_call" | custom-call | tf_op jit(solution)/shard_map/pallas_call | solution.py:108
  17.1 0.1 collective-permute-start.7
  17.2 1.2 %collective-permute-done.7 = f32[3,8,128]{2,1,0:T(8,128)S(1)} collective-permute-done((f32[3,8,128]{2,1,0:T(8,128)S(1)}, f32[3,8,128]{2,1,0:T(8,128)S(1)}, u32[]{:S(2)}, u32[]{:S(2)}) %collective-permute-start.7) | collective-permute-done | bytes 12320 | tf_op jit(solution)/shard_map/ppermute | solution.py:35
  18.3 3.6 %collective-permute-start.10 = (f32[3,8,128]{2,1,0:T(8,128)S(1)}, f32[3,8,128]{2,1,0:T(8,128)S(1)}, u32[]{:S(2)}, u32[]{:S(2)}) collective-permute-start(f32[3,8,128]{2,1,0:T(8,128)S(1)} %add.3.refs_0_), channel_id=1, source_target_pairs={{0,6},{1,7},{2,4},{3,5},{4,2},{5,3},{6,0},{7,1},{8,14},{9,15},{10,... | collective-permute-start | bytes 36872 | tf_op jit(solution)/shard_map/ppermute | solution.py:27
  21.9 0.8 %collective-permute-start.9 = (f32[3,8,128]{2,1,0:T(8,128)S(1)}, f32[3,8,128]{2,1,0:T(8,128)S(1)}, u32[]{:S(2)}, u32[]{:S(2)}) collective-permute-start(f32[3,8,128]{2,1,0:T(8,128)S(1)} %add.3.refs_0_), channel_id=1, source_target_pairs={{0,4},{1,5},{2,6},{3,7},{4,0},{5,1},{6,2},{7,3},{8,12},{9,13},{10,... | collective-permute-start | bytes 36872 | tf_op jit(solution)/shard_map/ppermute | solution.py:27
  22.7 0.7 %copy.5.refs_4_ = s32[6,4]{1,0:T(8,128)} copy(s32[6,4]{0,1:T(4,128)S(1)} %copy-done.7) | data formatting | bytes 192 | tf_op args[3]
  23.4 0.4 %collective-permute-done.10.refs_3_ = f32[3,8,128]{2,1,0:T(8,128)S(1)} collective-permute-done((f32[3,8,128]{2,1,0:T(8,128)S(1)}, f32[3,8,128]{2,1,0:T(8,128)S(1)}, u32[]{:S(2)}, u32[]{:S(2)}) %collective-permute-start.10) | collective-permute-done | bytes 12320 | tf_op jit(solution)/shard_map/ppermute | solution.py:27
  23.8 1.8 %collective-permute-done.8.refs_1_ = f32[3,8,128]{2,1,0:T(8,128)S(1)} collective-permute-done((f32[3,8,128]{2,1,0:T(8,128)S(1)}, f32[3,8,128]{2,1,0:T(8,128)S(1)}, u32[]{:S(2)}, u32[]{:S(2)}) %collective-permute-start.8) | collective-permute-done | bytes 12320 | tf_op jit(solution)/shard_map/ppermute | solution.py:27
  25.6 0.9 %collective-permute-done.9.refs_2_ = f32[3,8,128]{2,1,0:T(8,128)S(1)} collective-permute-done((f32[3,8,128]{2,1,0:T(8,128)S(1)}, f32[3,8,128]{2,1,0:T(8,128)S(1)}, u32[]{:S(2)}, u32[]{:S(2)}) %collective-permute-start.9) | collective-permute-done | bytes 12320 | tf_op jit(solution)/shard_map/ppermute | solution.py:27
  26.5 0.6 %copy-done.6 = f32[3,8,128]{2,1,0:T(8,128)} copy-done((f32[3,8,128]{2,1,0:T(8,128)}, f32[3,8,128]{2,1,0:T(8,128)S(1)}, u32[]{:S(2)}) %copy-start.6) | copy-done | bytes 12312
  27.1 1.6 %shard_map.47 = f32[6,4,8,16]{3,2,1,0:T(8,128)} custom-call(f32[3,8,128]{2,1,0:T(8,128)} %copy-done.3, f32[3,8,128]{2,1,0:T(8,128)} %copy-done.5, f32[3,8,128]{2,1,0:T(8,128)} %copy-done.6, f32[3,8,128]{2,1,0:T(8,128)} %copy-done.4, s32[6,4]{1,0:T(8,128)} %copy.5.refs_4_), custom_call_target="tpu_custom_call" | custom-call | tf_op jit(solution)/shard_map/pallas_call | solution.py:121
  (19 shorter events, 0.0 us)
Async XLA Ops:
  0.0 8.8 %collective-permute-start.3 = (bf16[6,4,8,96]{3,2,1,0:T(8,128)(2,1)}, bf16[6,4,8,96]{3,2,1,0:T(8,128)(2,1)S(1)}, u32[]{:S(2)}, u32[]{:S(2)}) collective-permute-start(bf16[6,4,8,96]{3,2,1,0:T(8,128)(2,1)} %refs_4_.2), channel_id=1, source_target_pairs={{0,2},{1,3},{2,0},{3,1},{4,6},{5,7},{6,4},{7,5},{8,10},{9,11},{10,... | collective-permute-start | bytes 110600 | tf_op jit(solution)/shard_map/ppermute | solution.py:27
  3.0 6.1 %collective-permute-start.4 = (bf16[6,4,8,96]{3,2,1,0:T(8,128)(2,1)}, bf16[6,4,8,96]{3,2,1,0:T(8,128)(2,1)S(1)}, u32[]{:S(2)}, u32[]{:S(2)}) collective-permute-start(bf16[6,4,8,96]{3,2,1,0:T(8,128)(2,1)} %refs_4_.2), channel_id=1, source_target_pairs={{0,4},{1,5},{2,6},{3,7},{4,0},{5,1},{6,2},{7,3},{8,12},{9,13},{10,... | collective-permute-start | bytes 110600 | tf_op jit(solution)/shard_map/ppermute | solution.py:27
  5.6 6.1 %collective-permute-start.5 = (bf16[6,4,8,96]{3,2,1,0:T(8,128)(2,1)}, bf16[6,4,8,96]{3,2,1,0:T(8,128)(2,1)S(1)}, u32[]{:S(2)}, u32[]{:S(2)}) collective-permute-start(bf16[6,4,8,96]{3,2,1,0:T(8,128)(2,1)} %refs_4_.2), channel_id=1, source_target_pairs={{0,6},{1,7},{2,4},{3,5},{4,2},{5,3},{6,0},{7,1},{8,14},{9,15},{10,... | collective-permute-start | bytes 110600 | tf_op jit(solution)/shard_map/ppermute | solution.py:27
  5.6 7.1 %collective-permute-start = (bf16[1,96,768]{2,1,0:T(8,128)(2,1)}, bf16[1,96,768]{2,1,0:T(8,128)(2,1)S(1)}, u32[]{:S(2)}, u32[]{:S(2)}) collective-permute-start(bf16[1,96,768]{2,1,0:T(8,128)(2,1)} %refs_0_.1), channel_id=1, source_target_pairs={{0,8},{8,0},{16,24},{24,16},{1,9},{9,1},{17,25},{25,17},{2,10},{10... | collective-permute-start | bytes 442376 | tf_op jit(solution)/shard_map/ppermute | solution.py:23
  7.3 8.5 %collective-permute-start.1 = (bf16[1,96,768]{2,1,0:T(8,128)(2,1)}, bf16[1,96,768]{2,1,0:T(8,128)(2,1)S(1)}, u32[]{:S(2)}, u32[]{:S(2)}) collective-permute-start(bf16[1,96,768]{2,1,0:T(8,128)(2,1)} %refs_0_.1), channel_id=1, source_target_pairs={{0,16},{8,24},{16,0},{24,8},{1,17},{9,25},{17,1},{25,9},{2,18},{10... | collective-permute-start | bytes 442376 | tf_op jit(solution)/shard_map/ppermute | solution.py:23
  8.9 6.9 %collective-permute-start.2 = (bf16[1,96,768]{2,1,0:T(8,128)(2,1)}, bf16[1,96,768]{2,1,0:T(8,128)(2,1)S(1)}, u32[]{:S(2)}, u32[]{:S(2)}) collective-permute-start(bf16[1,96,768]{2,1,0:T(8,128)(2,1)} %refs_0_.1), channel_id=1, source_target_pairs={{0,24},{8,16},{16,8},{24,0},{1,25},{9,17},{17,9},{25,1},{2,26},{10... | collective-permute-start | bytes 442376 | tf_op jit(solution)/shard_map/ppermute | solution.py:23
  11.7 4.1 %copy-start = (bf16[6,4,8,96]{3,2,1,0:T(8,128)(2,1)S(1)}, bf16[6,4,8,96]{3,2,1,0:T(8,128)(2,1)}, u32[]{:S(2)}) copy-start(bf16[6,4,8,96]{3,2,1,0:T(8,128)(2,1)} %refs_4_.2) | copy-start | bytes 110596
  11.7 4.1 %copy-start.1 = (bf16[1,96,768]{2,1,0:T(8,128)(2,1)S(1)}, bf16[1,96,768]{2,1,0:T(8,128)(2,1)}, u32[]{:S(2)}) copy-start(bf16[1,96,768]{2,1,0:T(8,128)(2,1)} %refs_0_.1) | copy-start | bytes 442372
  11.7 4.1 %copy-start.2 = (bf16[6,4,16,96]{3,2,1,0:T(8,128)(2,1)S(1)}, bf16[6,4,16,96]{3,2,1,0:T(8,128)(2,1)}, u32[]{:S(2)}) copy-start(bf16[6,4,16,96]{3,2,1,0:T(8,128)(2,1)} %refs_9_.1) | copy-start | bytes 221188
  12.6 3.2 %collective-permute-start.6 = (bf16[4,6,4,8,96]{4,3,2,1,0:T(8,128)(2,1)S(1)}, bf16[4,6,4,8,96]{4,3,2,1,0:T(8,128)(2,1)S(1)}, u32[]{:S(2)}, u32[]{:S(2)}) collective-permute-start(bf16[4,6,4,8,96]{4,3,2,1,0:T(8,128)(2,1)S(1)} %pad_maximum_fusion), channel_id=1, source_target_pairs={{0,1},{1,0},{2,3},{3,2},{4,5},{5,4},{6,7},{7,6},{8,9},{9,8},{10,11... | collective-permute-start | bytes 442376 | tf_op jit(solution)/shard_map/ppermute | solution.py:35
  17.1 5.6 %copy-start.7 = (s32[6,4]{0,1:T(4,128)S(1)}, s32[6,4]{0,1:T(4,128)}, u32[]{:S(2)}) copy-start(s32[6,4]{0,1:T(4,128)} %param.7) | copy-start | bytes 292
  17.1 1.2 %collective-permute-start.7 = (f32[3,8,128]{2,1,0:T(8,128)S(1)}, f32[3,8,128]{2,1,0:T(8,128)S(1)}, u32[]{:S(2)}, u32[]{:S(2)}) collective-permute-start(f32[3,8,128]{2,1,0:T(8,128)S(1)} %shard_map.46), channel_id=1, source_target_pairs={{0,1},{1,0},{2,3},{3,2},{4,5},{5,4},{6,7},{7,6},{8,9},{9,8},{10,11... | collective-permute-start | bytes 36872 | tf_op jit(solution)/shard_map/ppermute | solution.py:35
  18.3 8.2 %copy-start.3 = (f32[3,8,128]{2,1,0:T(8,128)}, f32[3,8,128]{2,1,0:T(8,128)S(1)}, u32[]{:S(2)}) copy-start(f32[3,8,128]{2,1,0:T(8,128)S(1)} %add.3.refs_0_) | copy-start | bytes 36868
  18.3 5.5 %collective-permute-start.10 = (f32[3,8,128]{2,1,0:T(8,128)S(1)}, f32[3,8,128]{2,1,0:T(8,128)S(1)}, u32[]{:S(2)}, u32[]{:S(2)}) collective-permute-start(f32[3,8,128]{2,1,0:T(8,128)S(1)} %add.3.refs_0_), channel_id=1, source_target_pairs={{0,6},{1,7},{2,4},{3,5},{4,2},{5,3},{6,0},{7,1},{8,14},{9,15},{10,... | collective-permute-start | bytes 36872 | tf_op jit(solution)/shard_map/ppermute | solution.py:27
  21.9 3.7 %collective-permute-start.8 = (f32[3,8,128]{2,1,0:T(8,128)S(1)}, f32[3,8,128]{2,1,0:T(8,128)S(1)}, u32[]{:S(2)}, u32[]{:S(2)}) collective-permute-start(f32[3,8,128]{2,1,0:T(8,128)S(1)} %add.3.refs_0_), channel_id=1, source_target_pairs={{0,2},{1,3},{2,0},{3,1},{4,6},{5,7},{6,4},{7,5},{8,10},{9,11},{10,... | collective-permute-start | bytes 36872 | tf_op jit(solution)/shard_map/ppermute | solution.py:27
  21.9 4.6 %collective-permute-start.9 = (f32[3,8,128]{2,1,0:T(8,128)S(1)}, f32[3,8,128]{2,1,0:T(8,128)S(1)}, u32[]{:S(2)}, u32[]{:S(2)}) collective-permute-start(f32[3,8,128]{2,1,0:T(8,128)S(1)} %add.3.refs_0_), channel_id=1, source_target_pairs={{0,4},{1,5},{2,6},{3,7},{4,0},{5,1},{6,2},{7,3},{8,12},{9,13},{10,... | collective-permute-start | bytes 36872 | tf_op jit(solution)/shard_map/ppermute | solution.py:27
  23.8 2.7 %copy-start.4 = (f32[3,8,128]{2,1,0:T(8,128)}, f32[3,8,128]{2,1,0:T(8,128)S(1)}, u32[]{:S(2)}) copy-start(f32[3,8,128]{2,1,0:T(8,128)S(1)} %collective-permute-done.10.refs_3_) | copy-start | bytes 36868
  25.6 0.9 %copy-start.5 = (f32[3,8,128]{2,1,0:T(8,128)}, f32[3,8,128]{2,1,0:T(8,128)S(1)}, u32[]{:S(2)}) copy-start(f32[3,8,128]{2,1,0:T(8,128)S(1)} %collective-permute-done.8.refs_1_) | copy-start | bytes 36868
  26.5 0.6 %copy-start.6 = (f32[3,8,128]{2,1,0:T(8,128)}, f32[3,8,128]{2,1,0:T(8,128)S(1)}, u32[]{:S(2)}) copy-start(f32[3,8,128]{2,1,0:T(8,128)S(1)} %collective-permute-done.9.refs_2_) | copy-start | bytes 36868

commit v2 on v1

--- a/solution.py
+++ b/solution.py
@@ -1,4 +1,5 @@
 import functools
+import math
 
 import jax
 import jax.numpy as jnp
@@ -9,6 +10,7 @@
 
 CORES = 2
 LANES = 128
+VMEM_LIMIT = 24 * 2**20
 
 
 def partner(i, s, n):
@@ -31,6 +33,44 @@
     )
 
 
+def chip_stages(nz):
+    stages, stride = [], nz
+    while stride > 1:
+        size = next(f for f in range(2, stride + 1) if stride % f == 0)
+        stride //= size
+        stages.append((stride, size))
+    return stages
+
+
+def shift_digit(i, s, stride, size):
+    digit = i // stride % size
+    return i + ((digit + s) % size - digit) * stride
+
+
+def gather_chips(x, nz):
+    shifts, parts = [()], [x[None]]
+    for stride, size in chip_stages(nz):
+        held = parts[0] if len(parts) == 1 else jnp.concatenate(parts)
+        parts = [held]
+        old = shifts
+        for s in range(1, size):
+            pairs = [
+                (i * CORES + c, shift_digit(i, s, stride, size) * CORES + c)
+                for i in range(nz)
+                for c in range(CORES)
+            ]
+            parts.append(lax.ppermute(held, "ga", pairs))
+            shifts = shifts + [was + ((stride, size, size - s),) for was in old]
+    return parts, shifts
+
+
+def apply_shifts(z, path):
+    for stride, size, s in path:
+        digit = lax.rem(lax.div(z, stride), size)
+        z = z + (lax.rem(digit + s, size) - digit) * stride
+    return z
+
+
 def send_core(x, nz):
     return lax.ppermute(
         x, "ga", [(i * CORES + c, i * CORES + 1 - c) for i in range(nz) for c in range(CORES)]
@@ -41,30 +81,66 @@
     return lax.dot_general(a, b, (((1,), (1,)), ((), ())), preferred_element_type=jnp.float32)
 
 
-def partial_kernel(npb, nz, *refs):
-    w_refs, mine_refs = refs[:npb], refs[npb : npb + nz]
-    other_ref, val_ref, out_ref, slab_ref, full_ref = refs[npb + nz :]
-    nk, nq, nc, ng = mine_refs[0].shape
-    nv = val_ref.shape[2]
+def pack_kernel(con_ref, out_ref):
+    nk, nq, nc, ng = con_ref.shape
+    for q in range(nq):
+        rows = con_ref[:, q].astype(jnp.float32).reshape(nk * nc, ng)
+        out_ref[:, q * ng : (q + 1) * ng] = rows.astype(jnp.bfloat16)
+
+
+def join_slabs(shifts, core, part_refs, slab_ref, full_ref):
+    nz = len(shifts)
+    ng = full_ref.shape[2] // (nz * CORES)
+    z = lax.div(lax.axis_index("ga"), CORES)
+    pieces = [ref.at[i] for ref in part_refs for i in range(ref.shape[0])]
+    for path, piece in zip(shifts, pieces):
+        first = apply_shifts(z, path) * CORES
+        slab_ref[first + core] = piece[...]
+        slab_ref[first + 1 - core] = jnp.zeros(slab_ref.shape[1:], jnp.bfloat16)
+    n_slabs, nq = nz * CORES, full_ref.shape[0]
+    group = LANES // math.gcd(ng, LANES)
+    slab_group = group if n_slabs % group == 0 else n_slabs
+    q_group = group if nq % group == 0 else nq
+    n_steps = (n_slabs // slab_group) * (nq // q_group)
+
+    def join(step, _):
+        p0 = lax.rem(step, n_slabs // slab_group) * slab_group
+        q0 = lax.div(step, n_slabs // slab_group) * q_group
+        loaded = [
+            slab_ref[p0 + p, :, pl.ds(pl.multiple_of(q0 * ng, q_group * ng), q_group * ng)]
+            for p in range(slab_group)
+        ]
+        for q in range(q_group):
+            row = [x[:, q * ng : (q + 1) * ng] for x in loaded]
+            full_ref[
+                q0 + q, :, pl.ds(pl.multiple_of(p0 * ng, slab_group * ng), slab_group * ng)
+            ] = jnp.concatenate(row, axis=1)
+
+    lax.fori_loop(0, n_steps, join, None, unroll=n_steps <= 4)
+
+
+def near_kernel(npb, shifts, *refs):
+    w_refs, part_refs = refs[:npb], refs[npb:-3]
+    out_ref, slab_ref, full_ref = refs[-3:]
+    pb, ga = lax.axis_index("pb"), lax.axis_index("ga")
+    join_slabs(shifts, lax.rem(ga, CORES), part_refs, slab_ref, full_ref)
+    for s in range(npb):
+        out_ref[s] = dot_nt(full_ref[source(pb, s, npb)], w_refs[s][0])
+
+
+def partial_kernel(npb, shifts, *refs):
+    w_refs, part_refs = refs[:npb], refs[npb:-5]
+    near_ref, val_ref, out_ref, slab_ref, full_ref = refs[-5:]
+    nk, _, nv, ng = val_ref.shape
+    nc = near_ref.shape[1] // nk
     per_tile = LANES // nv
     pb, ga = lax.axis_index("pb"), lax.axis_index("ga")
-    z, core = lax.div(ga, CORES), lax.rem(ga, CORES)
-    for s in range(nz):
-        first = source(z, s, nz) * CORES
-        slab_ref[first + core] = mine_refs[s][...]
-        slab_ref[first + 1 - core] = other_ref[s]
+    join_slabs(shifts, 1 - lax.rem(ga, CORES), part_refs, slab_ref, full_ref)
     lane_block = lax.broadcasted_iota(jnp.int32, (nc, LANES), 1) // nv
     tiles = [jnp.zeros((nc, LANES), jnp.float32) for _ in range(out_ref.shape[0])]
-
-    def join(q, _):
-        for p in range(nz * CORES):
-            piece = slab_ref[p, :, q].astype(jnp.float32).reshape(nk * nc, ng)
-            full_ref[q, :, p * ng : (p + 1) * ng] = piece.astype(jnp.bfloat16)
-
-    lax.fori_loop(0, nq, join, None, unroll=min(nq, 4))
     for s in range(npb):
         q = source(pb, s, npb)
-        applied = dot_nt(full_ref[q], w_refs[s][0])
+        applied = near_ref[s] + dot_nt(full_ref[q], w_refs[s][0])
         high = applied.astype(jnp.bfloat16)
         low = (applied - high.astype(jnp.float32)).astype(jnp.bfloat16)
         val = val_ref[:, q].astype(jnp.float32).reshape(nk * nv, ng).astype(jnp.bfloat16)
@@ -92,7 +168,7 @@
         q = source(pb, s, npb)
         for k in range(nk):
             tile, place = divmod(k * npb + s, per_tile)
-            out_ref[k, kq_ref[k, q]] = total[tile, :, place * nv : (place + 1) * nv]
+            out_ref[k, kq_ref[q, k]] = total[tile, :, place * nv : (place + 1) * nv]
 
 
 def per_device(npb, nz, valence, conduction, screened, kq_table):
@@ -100,22 +176,43 @@
     nc = conduction.shape[2]
     vmem = pl.BlockSpec(memory_space=pltpu.VMEM)
     smem = pl.BlockSpec(memory_space=pltpu.SMEM)
+    params = pltpu.CompilerParams(vmem_limit_bytes=VMEM_LIMIT)
+    join_scratch = [
+        pltpu.VMEM((nz * CORES, nk * nc, nq * ng), jnp.bfloat16),
+        pltpu.VMEM((nq, nk * nc, nz * CORES * ng), jnp.bfloat16),
+    ]
 
     w_parts = [screened] + [send_pb(screened, s, npb) for s in range(1, npb)]
-    mine = [conduction] + [send_chip(conduction, s, nz) for s in range(1, nz)]
-    other = send_core(jnp.stack(mine), nz)
+    packed = pl.pallas_call(
+        pack_kernel,
+        out_shape=jax.ShapeDtypeStruct((nk * nc, nq * ng), jnp.bfloat16),
+        in_specs=[vmem],
+        out_specs=vmem,
+        compiler_params=params,
+        cost_estimate=pl.CostEstimate(flops=0, bytes_accessed=1000000, transcendentals=0),
+    )(conduction)
+    mine, shifts = gather_chips(packed, nz)
+    other = [send_core(part, nz) for part in mine]
+    near = pl.pallas_call(
+        functools.partial(near_kernel, npb, shifts),
+        out_shape=jax.ShapeDtypeStruct((npb, nk * nc, ng), jnp.float32),
+        in_specs=[vmem] * (npb + len(mine)),
+        out_specs=vmem,
+        scratch_shapes=join_scratch,
+        compiler_params=params,
+        cost_estimate=pl.CostEstimate(
+            flops=2 * nk * nq * nc * ng * ng * nz, bytes_accessed=3000000, transcendentals=0
+        ),
+    )(*w_parts, *mine)
     n_tiles = -(-nk * nq * nv // LANES)
     partial_value = pl.pallas_call(
-        functools.partial(partial_kernel, npb, nz),
+        functools.partial(partial_kernel, npb, shifts),
         out_shape=jax.ShapeDtypeStruct((n_tiles, nc, LANES), jnp.float32),
-        in_specs=[vmem] * (npb + nz + 2),
-        out_specs=vmem,
-        scratch_shapes=[
-            pltpu.VMEM((nz * CORES, nk, nq, nc, ng), jnp.bfloat16),
-            pltpu.VMEM((nq, nk * nc, nz * CORES * ng), jnp.bfloat16),
-        ],
-        compiler_params=pltpu.CompilerParams(vmem_limit_bytes=48 * 2**20),
-    )(*w_parts, *mine, other, valence)
+        in_specs=[vmem] * (npb + len(mine) + 2),
+        out_specs=vmem,
+        scratch_shapes=join_scratch,
+        compiler_params=params,
+    )(*w_parts, *other, near, valence)
     chip_value = partial_value + send_core(partial_value, nz)
     shares = [chip_value] + [send_chip(chip_value, s, nz) for s in range(1, nz)]
     return pl.pallas_call(
@@ -123,7 +220,8 @@
         out_shape=jax.ShapeDtypeStruct((nk, nq, nc, nv), jnp.float32),
         in_specs=[vmem] * nz + [smem],
         out_specs=vmem,
-    )(*shares, kq_table)
+        compiler_params=params,
+    )(*shares, kq_table.T)
 
 
 def solution(mesh):

time: 28.9 us -> 25.5 us (0.88)
  waiting for transfers between devices: 9.93 us -> 7.87 us
  other arithmetic: 0.92 us -> 0.02 us
  local copies, waits for them, and re-layouts: 1.29 us -> 0.85 us
    ppermute x0 -> x2, starting transfers between devices: none -> 5.74 us  [gather_chips(): parts.append(lax.ppermute(held, 'ga', pairs))]
    ppermute x6 -> x3, starting transfers between devices: 10 us -> 4.39 us  [send_chip(): lax.ppermute(x, 'ga', [(i * CORES + c, partner(i, s, nz) * CORES + c) for...]
    ppermute x6 -> x3, waiting for transfers between devices: 5.69 us -> 1.86 us  [send_chip(): lax.ppermute(x, 'ga', [(i * CORES + c, partner(i, s, nz) * CORES + c) for...]
    ppermute x0 -> x2, waiting for transfers between devices: none -> 2.78 us  [gather_chips(): parts.append(lax.ppermute(held, 'ga', pairs))]
    ppermute x3, waiting for transfers between devices: 3.07 us -> 2.06 us  [send_pb(): return lax.ppermute(x, 'pb', [(i, partner(i, s, npb)) for i in range(npb)])]
    another operation x1 -> x0, other arithmetic: 0.92 us -> none  [per_device(): other = send_core(jnp.stack(mine), nz)]
    unnamed x17 -> x8, local copies, waits for them, and re-layouts: 1.29 us -> 0.85 us
    pallas_call x1 -> x3, Pallas kernels: 1.26 us -> 1.63 us  [the longest x1 1.05 us: per_device(): pl.pallas_call(functools.partial(partial_kernel, npb, shifts), out_shape=...]
  transfers between devices with their start and end apart: 11 -> 11, of which waited for: 6 -> 5; matrix products, arithmetic and copies ran while one was open for 6% -> 0% of each run, Pallas kernels for 0% -> 2%
where the time goes in v2:
time: 25.5 us; the launch traced here: 25.4 us
  starting transfers between devices  13.7 us (54%)
  waiting for transfers between devices  7.87 us (31%)
  Pallas kernels  2.93 us (11%)
  local copies, waits for them, and re-layouts  0.85 us (3%)
    ppermute x2, starting transfers between devices, gather_chips(): parts.append(lax.ppermute(held, 'ga', pairs))  5.74 us
    ppermute x3, starting transfers between devices, send_chip(): lax.ppermute(x, 'ga', [(i * CORES + c, partner(i, s, nz) * CORES + c) for...  4.39 us
    ppermute x3, starting transfers between devices, send_pb(): return lax.ppermute(x, 'pb', [(i, partner(i, s, npb)) for i in range(npb)])  3.49 us
    ppermute x2, waiting for transfers between devices, gather_chips(): parts.append(lax.ppermute(held, 'ga', pairs))  2.78 us
    ppermute x3, waiting for transfers between devices, send_pb(): return lax.ppermute(x, 'pb', [(i, partner(i, s, npb)) for i in range(npb)])  2.06 us
    ppermute x3, waiting for transfers between devices, send_chip(): lax.ppermute(x, 'ga', [(i * CORES + c, partner(i, s, nz) * CORES + c) for...  1.86 us
    pallas_call x1, Pallas kernels, per_device(): pl.pallas_call(functools.partial(place_kernel, npb, nz), out_shape=jax.Sh...  1.3 us
    ppermute x3, waiting for transfers between devices, send_core(): lax.ppermute(x, 'ga', [(i * CORES + c, i * CORES + 1 - c) for i in range(...  1.17 us
  transfers between devices with their start and end apart: 11, of which 5 were waited for; matrix products, arithmetic and copies ran while one was open for 0% of the time, Pallas kernels for 2%

profile of v2, /device:TPU:0, one launch (start us, length us, event | category | flops | bytes accessed | tf_op | source)
XLA Modules:
  0.0 25.4 jit_solution(895392111954034623)
XLA Ops:
  0.0 0.8 %copy-done.2 = bf16[6,4,8,96]{3,2,1,0:T(8,128)(2,1)S(1)} copy-done((bf16[6,4,8,96]{3,2,1,0:T(8,128)(2,1)S(1)}, bf16[6,4,8,96]{3,2,1,0:T(8,128)(2,1)}, u32[]{:S(2)}) %copy-start.2) | copy-done | bytes 36888
  0.8 0.1 shard_map.46
  0.9 4.1 %collective-permute-start.3 = (bf16[1,48,384]{2,1,0:T(8,128)(2,1)S(1)}, bf16[1,48,384]{2,1,0:T(8,128)(2,1)S(1)}, u32[]{:S(2)}, u32[]{:S(2)}) collective-permute-start(bf16[1,48,384]{2,1,0:T(8,128)(2,1)S(1)} %bitcast.2), channel_id=1, source_target_pairs={{0,4},{1,5},{2,6},{3,7},{4,0},{5,1},{6,2},{7,3},{8,12},{9,13},{10,... | collective-permute-start | bytes 110600 | tf_op jit(solution)/shard_map/ppermute | solution.py:62
  5.0 1.5 %collective-permute-start = (bf16[1,96,768]{2,1,0:T(8,128)(2,1)}, bf16[1,96,768]{2,1,0:T(8,128)(2,1)S(1)}, u32[]{:S(2)}, u32[]{:S(2)}) collective-permute-start(bf16[1,96,768]{2,1,0:T(8,128)(2,1)} %refs_0_.3), channel_id=1, source_target_pairs={{0,8},{8,0},{16,24},{24,16},{1,9},{9,1},{17,25},{25,17},{2,10},{10... | collective-permute-start | bytes 442376 | tf_op jit(solution)/shard_map/ppermute | solution.py:25
  6.5 1.5 %collective-permute-start.1 = (bf16[1,96,768]{2,1,0:T(8,128)(2,1)}, bf16[1,96,768]{2,1,0:T(8,128)(2,1)S(1)}, u32[]{:S(2)}, u32[]{:S(2)}) collective-permute-start(bf16[1,96,768]{2,1,0:T(8,128)(2,1)} %refs_0_.3), channel_id=1, source_target_pairs={{0,16},{8,24},{16,0},{24,8},{1,17},{9,25},{17,1},{25,9},{2,18},{10... | collective-permute-start | bytes 442376 | tf_op jit(solution)/shard_map/ppermute | solution.py:25
  8.0 0.5 %collective-permute-start.2 = (bf16[1,96,768]{2,1,0:T(8,128)(2,1)}, bf16[1,96,768]{2,1,0:T(8,128)(2,1)S(1)}, u32[]{:S(2)}, u32[]{:S(2)}) collective-permute-start(bf16[1,96,768]{2,1,0:T(8,128)(2,1)} %refs_0_.3), channel_id=1, source_target_pairs={{0,24},{8,16},{16,8},{24,0},{1,25},{9,17},{17,9},{25,1},{2,26},{10... | collective-permute-start | bytes 442376 | tf_op jit(solution)/shard_map/ppermute | solution.py:25
  8.5 0.0 copy-start.1
  8.6 1.6 %collective-permute-start.5 = (bf16[2,48,384]{2,1,0:T(8,128)(2,1)S(1)}, bf16[2,48,384]{2,1,0:T(8,128)(2,1)S(1)}, u32[]{:S(2)}, u32[]{:S(2)}) collective-permute-start(bf16[2,48,384]{2,1,0:T(8,128)(2,1)S(1)} %pad_maximum_fusion.refs_4_), channel_id=1, source_target_pairs={{0,2},{1,3},{2,0},{3,1},{4,6},{5,7},{6,4},{7,5},{8,10},{9,11},{10,... | collective-permute-start | bytes 221192 | tf_op jit(solution)/shard_map/ppermute | solution.py:62
  10.2 0.0 collective-permute-start.4
  10.2 2.8 %collective-permute-done.5.refs_5_ = bf16[2,48,384]{2,1,0:T(8,128)(2,1)S(1)} collective-permute-done((bf16[2,48,384]{2,1,0:T(8,128)(2,1)S(1)}, bf16[2,48,384]{2,1,0:T(8,128)(2,1)S(1)}, u32[]{:S(2)}, u32[]{:S(2)}) %collective-permute-start.5) | collective-permute-done | bytes 73760 | tf_op jit(solution)/shard_map/ppermute | solution.py:62
  13.0 0.0 collective-permute-done.refs_1_
  13.0 2.1 %collective-permute-done.1.refs_2_ = bf16[1,96,768]{2,1,0:T(8,128)(2,1)S(1)} collective-permute-done((bf16[1,96,768]{2,1,0:T(8,128)(2,1)}, bf16[1,96,768]{2,1,0:T(8,128)(2,1)S(1)}, u32[]{:S(2)}, u32[]{:S(2)}) %collective-permute-start.1) | collective-permute-done | bytes 147488 | tf_op jit(solution)/shard_map/ppermute | solution.py:25
  15.0 0.0 collective-permute-done.2.refs_3_
  15.0 0.5 %shard_map.47.refs_6_ = f32[4,48,96]{2,1,0:T(8,128)S(1)} custom-call(bf16[1,96,768]{2,1,0:T(8,128)(2,1)S(1)} %copy-done, bf16[1,96,768]{2,1,0:T(8,128)(2,1)S(1)} %collective-permute-done.refs_1_, bf16[1,96,768]{2,1,0:T(8,128)(2,1)S(1)} %collective-permute-done.1.refs_2_, bf16[1,96,768]{2,1,0:T(8,128)(2,1)S(1)} %collective-permute-done.2.refs_3_, ...), custom_call_target="tpu_custom_call" | custom-call | flops 14155776 | bytes 3000000 | tf_op jit(solution)/shard_map/pallas_call | solution.py:196
  15.5 0.0 collective-permute-done.6.refs_5_
  15.6 1.1 %shard_map.48 = f32[3,8,128]{2,1,0:T(8,128)S(1)} custom-call(bf16[1,96,768]{2,1,0:T(8,128)(2,1)S(1)} %copy-done, bf16[1,96,768]{2,1,0:T(8,128)(2,1)S(1)} %collective-permute-done.refs_1_, bf16[1,96,768]{2,1,0:T(8,128)(2,1)S(1)} %collective-permute-done.1.refs_2_, bf16[1,96,768]{2,1,0:T(8,128)(2,1)S(1)} %collective-permute-done.2.refs_3_, ...), custom_call_target="tpu_custom_call" | custom-call | tf_op jit(solution)/shard_map/pallas_call | solution.py:208
  16.6 0.0 collective-permute-start.7
  16.7 1.2 %collective-permute-done.7 = f32[3,8,128]{2,1,0:T(8,128)S(1)} collective-permute-done((f32[3,8,128]{2,1,0:T(8,128)S(1)}, f32[3,8,128]{2,1,0:T(8,128)S(1)}, u32[]{:S(2)}, u32[]{:S(2)}) %collective-permute-start.7) | collective-permute-done | bytes 12320 | tf_op jit(solution)/shard_map/ppermute | solution.py:75
  17.8 1.4 %collective-permute-start.10 = (f32[3,8,128]{2,1,0:T(8,128)S(1)}, f32[3,8,128]{2,1,0:T(8,128)S(1)}, u32[]{:S(2)}, u32[]{:S(2)}) collective-permute-start(f32[3,8,128]{2,1,0:T(8,128)S(1)} %add.3.refs_0_), channel_id=1, source_target_pairs={{0,6},{1,7},{2,4},{3,5},{4,2},{5,3},{6,0},{7,1},{8,14},{9,15},{10,... | collective-permute-start | bytes 36872 | tf_op jit(solution)/shard_map/ppermute | solution.py:29
  19.2 0.3 %collective-permute-start.8 = (f32[3,8,128]{2,1,0:T(8,128)S(1)}, f32[3,8,128]{2,1,0:T(8,128)S(1)}, u32[]{:S(2)}, u32[]{:S(2)}) collective-permute-start(f32[3,8,128]{2,1,0:T(8,128)S(1)} %add.3.refs_0_), channel_id=1, source_target_pairs={{0,2},{1,3},{2,0},{3,1},{4,6},{5,7},{6,4},{7,5},{8,10},{9,11},{10,... | collective-permute-start | bytes 36872 | tf_op jit(solution)/shard_map/ppermute | solution.py:29
  19.5 2.7 %collective-permute-start.9 = (f32[3,8,128]{2,1,0:T(8,128)S(1)}, f32[3,8,128]{2,1,0:T(8,128)S(1)}, u32[]{:S(2)}, u32[]{:S(2)}) collective-permute-start(f32[3,8,128]{2,1,0:T(8,128)S(1)} %add.3.refs_0_), channel_id=1, source_target_pairs={{0,4},{1,5},{2,6},{3,7},{4,0},{5,1},{6,2},{7,3},{8,12},{9,13},{10,... | collective-permute-start | bytes 36872 | tf_op jit(solution)/shard_map/ppermute | solution.py:29
  22.2 1.1 %collective-permute-done.10.refs_3_ = f32[3,8,128]{2,1,0:T(8,128)S(1)} collective-permute-done((f32[3,8,128]{2,1,0:T(8,128)S(1)}, f32[3,8,128]{2,1,0:T(8,128)S(1)}, u32[]{:S(2)}, u32[]{:S(2)}) %collective-permute-start.10) | collective-permute-done | bytes 12320 | tf_op jit(solution)/shard_map/ppermute | solution.py:29
  23.3 0.7 %collective-permute-done.9.refs_2_ = f32[3,8,128]{2,1,0:T(8,128)S(1)} collective-permute-done((f32[3,8,128]{2,1,0:T(8,128)S(1)}, f32[3,8,128]{2,1,0:T(8,128)S(1)}, u32[]{:S(2)}, u32[]{:S(2)}) %collective-permute-start.9) | collective-permute-done | bytes 12320 | tf_op jit(solution)/shard_map/ppermute | solution.py:29
  24.1 1.3 %shard_map.49 = f32[6,4,8,16]{3,2,1,0:T(8,128)} custom-call(f32[3,8,128]{2,1,0:T(8,128)S(1)} %add.3.refs_0_, f32[3,8,128]{2,1,0:T(8,128)S(1)} %collective-permute-done.8.refs_1_, f32[3,8,128]{2,1,0:T(8,128)S(1)} %collective-permute-done.9.refs_2_, f32[3,8,128]{2,1,0:T(8,128)S(1)} %collective-permute-done.10.refs_3_, s32[4,6]{1,0:T(4,128)S(1)} %bitcast.4), custom_call_target="tpu_custom_call" | custom-call | tf_op jit(solution)/shard_map/pallas_call | solution.py:218
  (12 shorter events, 0.0 us)
Async XLA Ops:
  0.0 15.0 %copy-start = (bf16[1,96,768]{2,1,0:T(8,128)(2,1)S(1)}, bf16[1,96,768]{2,1,0:T(8,128)(2,1)}, u32[]{:S(2)}) copy-start(bf16[1,96,768]{2,1,0:T(8,128)(2,1)} %refs_0_.3) | copy-start | bytes 442372
  0.0 0.8 %copy-start.2 = (bf16[6,4,8,96]{3,2,1,0:T(8,128)(2,1)S(1)}, bf16[6,4,8,96]{3,2,1,0:T(8,128)(2,1)}, u32[]{:S(2)}) copy-start(bf16[6,4,8,96]{3,2,1,0:T(8,128)(2,1)} %con_ref.1) | copy-start | bytes 110596
  0.9 7.6 %collective-permute-start.3 = (bf16[1,48,384]{2,1,0:T(8,128)(2,1)S(1)}, bf16[1,48,384]{2,1,0:T(8,128)(2,1)S(1)}, u32[]{:S(2)}, u32[]{:S(2)}) collective-permute-start(bf16[1,48,384]{2,1,0:T(8,128)(2,1)S(1)} %bitcast.2), channel_id=1, source_target_pairs={{0,4},{1,5},{2,6},{3,7},{4,0},{5,1},{6,2},{7,3},{8,12},{9,13},{10,... | collective-permute-start | bytes 110600 | tf_op jit(solution)/shard_map/ppermute | solution.py:62
  5.0 7.9 %collective-permute-start = (bf16[1,96,768]{2,1,0:T(8,128)(2,1)}, bf16[1,96,768]{2,1,0:T(8,128)(2,1)S(1)}, u32[]{:S(2)}, u32[]{:S(2)}) collective-permute-start(bf16[1,96,768]{2,1,0:T(8,128)(2,1)} %refs_0_.3), channel_id=1, source_target_pairs={{0,8},{8,0},{16,24},{24,16},{1,9},{9,1},{17,25},{25,17},{2,10},{10... | collective-permute-start | bytes 442376 | tf_op jit(solution)/shard_map/ppermute | solution.py:25
  6.5 8.5 %collective-permute-start.1 = (bf16[1,96,768]{2,1,0:T(8,128)(2,1)}, bf16[1,96,768]{2,1,0:T(8,128)(2,1)S(1)}, u32[]{:S(2)}, u32[]{:S(2)}) collective-permute-start(bf16[1,96,768]{2,1,0:T(8,128)(2,1)} %refs_0_.3), channel_id=1, source_target_pairs={{0,16},{8,24},{16,0},{24,8},{1,17},{9,25},{17,1},{25,9},{2,18},{10... | collective-permute-start | bytes 442376 | tf_op jit(solution)/shard_map/ppermute | solution.py:25
  8.0 7.0 %collective-permute-start.2 = (bf16[1,96,768]{2,1,0:T(8,128)(2,1)}, bf16[1,96,768]{2,1,0:T(8,128)(2,1)S(1)}, u32[]{:S(2)}, u32[]{:S(2)}) collective-permute-start(bf16[1,96,768]{2,1,0:T(8,128)(2,1)} %refs_0_.3), channel_id=1, source_target_pairs={{0,24},{8,16},{16,8},{24,0},{1,25},{9,17},{17,9},{25,1},{2,26},{10... | collective-permute-start | bytes 442376 | tf_op jit(solution)/shard_map/ppermute | solution.py:25
  8.5 7.0 %copy-start.1 = (bf16[6,4,16,96]{3,2,1,0:T(8,128)(2,1)S(1)}, bf16[6,4,16,96]{3,2,1,0:T(8,128)(2,1)}, u32[]{:S(2)}) copy-start(bf16[6,4,16,96]{3,2,1,0:T(8,128)(2,1)} %refs_7_.1) | copy-start | bytes 221188
  8.6 4.4 %collective-permute-start.5 = (bf16[2,48,384]{2,1,0:T(8,128)(2,1)S(1)}, bf16[2,48,384]{2,1,0:T(8,128)(2,1)S(1)}, u32[]{:S(2)}, u32[]{:S(2)}) collective-permute-start(bf16[2,48,384]{2,1,0:T(8,128)(2,1)S(1)} %pad_maximum_fusion.refs_4_), channel_id=1, source_target_pairs={{0,2},{1,3},{2,0},{3,1},{4,6},{5,7},{6,4},{7,5},{8,10},{9,11},{10,... | collective-permute-start | bytes 221192 | tf_op jit(solution)/shard_map/ppermute | solution.py:62
  10.2 5.3 %collective-permute-start.4 = (bf16[2,48,384]{2,1,0:T(8,128)(2,1)S(1)}, bf16[2,48,384]{2,1,0:T(8,128)(2,1)S(1)}, u32[]{:S(2)}, u32[]{:S(2)}) collective-permute-start(bf16[2,48,384]{2,1,0:T(8,128)(2,1)S(1)} %pad_maximum_fusion.refs_4_), channel_id=1, source_target_pairs={{0,1},{1,0},{2,3},{3,2},{4,5},{5,4},{6,7},{7,6},{8,9},{9,8},{10,11... | collective-permute-start | bytes 221192 | tf_op jit(solution)/shard_map/ppermute | solution.py:75
  13.0 2.6 %collective-permute-start.6 = (bf16[2,48,384]{2,1,0:T(8,128)(2,1)S(1)}, bf16[2,48,384]{2,1,0:T(8,128)(2,1)S(1)}, u32[]{:S(2)}, u32[]{:S(2)}) collective-permute-start(bf16[2,48,384]{2,1,0:T(8,128)(2,1)S(1)} %collective-permute-done.5.refs_5_), channel_id=1, source_target_pairs={{0,1},{1,0},{2,3},{3,2},{4,5},{5,4},{6,7},{7,6},{8,9},{9,8},{10,11... | collective-permute-start | bytes 221192 | tf_op jit(solution)/shard_map/ppermute | solution.py:75
  16.6 1.2 %collective-permute-start.7 = (f32[3,8,128]{2,1,0:T(8,128)S(1)}, f32[3,8,128]{2,1,0:T(8,128)S(1)}, u32[]{:S(2)}, u32[]{:S(2)}) collective-permute-start(f32[3,8,128]{2,1,0:T(8,128)S(1)} %shard_map.48), channel_id=1, source_target_pairs={{0,1},{1,0},{2,3},{3,2},{4,5},{5,4},{6,7},{7,6},{8,9},{9,8},{10,11... | collective-permute-start | bytes 36872 | tf_op jit(solution)/shard_map/ppermute | solution.py:75
  17.8 6.3 %copy-start.3 = (s32[6,4]{0,1:T(4,128)S(1)}, s32[6,4]{0,1:T(4,128)}, u32[]{:S(2)}) copy-start(s32[6,4]{0,1:T(4,128)} %param.7) | copy-start | bytes 292
  17.8 5.5 %collective-permute-start.10 = (f32[3,8,128]{2,1,0:T(8,128)S(1)}, f32[3,8,128]{2,1,0:T(8,128)S(1)}, u32[]{:S(2)}, u32[]{:S(2)}) collective-permute-start(f32[3,8,128]{2,1,0:T(8,128)S(1)} %add.3.refs_0_), channel_id=1, source_target_pairs={{0,6},{1,7},{2,4},{3,5},{4,2},{5,3},{6,0},{7,1},{8,14},{9,15},{10,... | collective-permute-start | bytes 36872 | tf_op jit(solution)/shard_map/ppermute | solution.py:29
  19.2 4.1 %collective-permute-start.8 = (f32[3,8,128]{2,1,0:T(8,128)S(1)}, f32[3,8,128]{2,1,0:T(8,128)S(1)}, u32[]{:S(2)}, u32[]{:S(2)}) collective-permute-start(f32[3,8,128]{2,1,0:T(8,128)S(1)} %add.3.refs_0_), channel_id=1, source_target_pairs={{0,2},{1,3},{2,0},{3,1},{4,6},{5,7},{6,4},{7,5},{8,10},{9,11},{10,... | collective-permute-start | bytes 36872 | tf_op jit(solution)/shard_map/ppermute | solution.py:29
  19.5 4.6 %collective-permute-start.9 = (f32[3,8,128]{2,1,0:T(8,128)S(1)}, f32[3,8,128]{2,1,0:T(8,128)S(1)}, u32[]{:S(2)}, u32[]{:S(2)}) collective-permute-start(f32[3,8,128]{2,1,0:T(8,128)S(1)} %add.3.refs_0_), channel_id=1, source_target_pairs={{0,4},{1,5},{2,6},{3,7},{4,0},{5,1},{6,2},{7,3},{8,12},{9,13},{10,... | collective-permute-start | bytes 36872 | tf_op jit(solution)/shard_map/ppermute | solution.py:29

commit v3 on v2

--- a/solution.py
+++ b/solution.py
@@ -47,10 +47,12 @@
     return i + ((digit + s) % size - digit) * stride
 
 
-def gather_chips(x, nz):
-    shifts, parts = [()], [x[None]]
-    for stride, size in chip_stages(nz):
-        held = parts[0] if len(parts) == 1 else jnp.concatenate(parts)
+def gather_chips(x, nz, join):
+    shifts, parts = [()], [x]
+    for i, (stride, size) in enumerate(chip_stages(nz)):
+        held = x
+        if i:
+            held = join(*parts) if i == 1 else jnp.concatenate(parts)
         parts = [held]
         old = shifts
         for s in range(1, size):
@@ -81,11 +83,32 @@
     return lax.dot_general(a, b, (((1,), (1,)), ((), ())), preferred_element_type=jnp.float32)
 
 
-def pack_kernel(con_ref, out_ref):
+def pack(con_ref, out_ref):
     nk, nq, nc, ng = con_ref.shape
     for q in range(nq):
         rows = con_ref[:, q].astype(jnp.float32).reshape(nk * nc, ng)
         out_ref[:, q * ng : (q + 1) * ng] = rows.astype(jnp.bfloat16)
+
+
+def pack_kernel(own_ref, *refs):
+    out_ref = refs[-1]
+    out_ref[0] = own_ref[...]
+    for i, con_ref in enumerate(refs[:-1]):
+        pack(con_ref, out_ref.at[i + 1])
+
+
+def prepare_kernel(npb, held_ref, val_ref, kq_ref, sent_ref, out_ref):
+    nk, nq, nv, ng = val_ref.shape
+    per_tile = LANES // nv
+    pb = lax.axis_index("pb")
+    sent_ref[...] = held_ref[...]
+    out_ref[...] = jnp.zeros(out_ref.shape, out_ref.dtype)
+    for s in range(npb):
+        q = source(pb, s, npb)
+        for k in range(nk):
+            block = k * nq + kq_ref[q, k]
+            rows = pl.ds(pl.multiple_of(lax.rem(block, per_tile) * nv, nv), nv)
+            out_ref[lax.div(block, per_tile), rows, s * LANES : s * LANES + ng] = val_ref[k, q]
 
 
 def join_slabs(shifts, core, part_refs, slab_ref, full_ref):
@@ -131,44 +154,44 @@
 def partial_kernel(npb, shifts, *refs):
     w_refs, part_refs = refs[:npb], refs[npb:-5]
     near_ref, val_ref, out_ref, slab_ref, full_ref = refs[-5:]
-    nk, _, nv, ng = val_ref.shape
-    nc = near_ref.shape[1] // nk
-    per_tile = LANES // nv
+    n_tiles, nc, _ = out_ref.shape
+    nq, rows, ng = near_ref.shape
+    nk = rows // nc
+    blocks = nk * nq // n_tiles
     pb, ga = lax.axis_index("pb"), lax.axis_index("ga")
     join_slabs(shifts, 1 - lax.rem(ga, CORES), part_refs, slab_ref, full_ref)
-    lane_block = lax.broadcasted_iota(jnp.int32, (nc, LANES), 1) // nv
-    tiles = [jnp.zeros((nc, LANES), jnp.float32) for _ in range(out_ref.shape[0])]
+    high, low = [], []
+    fill = jnp.zeros((rows, LANES - ng), jnp.float32)
     for s in range(npb):
-        q = source(pb, s, npb)
-        applied = near_ref[s] + dot_nt(full_ref[q], w_refs[s][0])
-        high = applied.astype(jnp.bfloat16)
-        low = (applied - high.astype(jnp.float32)).astype(jnp.bfloat16)
-        val = val_ref[:, q].astype(jnp.float32).reshape(nk * nv, ng).astype(jnp.bfloat16)
-        val = jnp.concatenate([val, jnp.zeros((LANES - nk * nv, ng), jnp.bfloat16)], axis=0)
-        product = dot_nt(high, val) + dot_nt(low, val)
-        for k in range(nk):
-            tile, place = divmod(k * npb + s, per_tile)
-            moved = pltpu.roll(
-                product[k * nc : (k + 1) * nc], ((place - k) * nv) % LANES, axis=1
-            )
-            tiles[tile] = jnp.where(lane_block == place, moved, tiles[tile])
-    for t, tile in enumerate(tiles):
+        applied = near_ref[s] + dot_nt(full_ref[source(pb, s, npb)], w_refs[s][0])
+        applied = jnp.concatenate([applied, fill], axis=1)
+        high.append(applied.astype(jnp.bfloat16))
+        low.append((applied - high[-1].astype(jnp.float32)).astype(jnp.bfloat16))
+    high, low = jnp.concatenate(high, axis=1), jnp.concatenate(low, axis=1)
+    owner = lax.broadcasted_iota(jnp.int32, (nc, LANES), 1) // (LANES // blocks)
+    for t in range(n_tiles):
+        first, last = t * blocks // nq, ((t + 1) * blocks - 1) // nq + 1
+        both = jnp.concatenate([high[first * nc : last * nc], low[first * nc : last * nc]])
+        product = dot_nt(both, val_ref[t])
+        product = product[: (last - first) * nc] + product[(last - first) * nc :]
+        tile = product[:nc]
+        for k in range(first + 1, last):
+            mine = (owner + t * blocks) // nq == k
+            tile = jnp.where(mine, product[(k - first) * nc : (k - first + 1) * nc], tile)
         out_ref[t] = tile
 
 
-def place_kernel(npb, nz, *refs):
-    share_refs, (kq_ref, out_ref) = refs[:nz], refs[nz:]
-    nk, _, _, nv = out_ref.shape
+def place_kernel(nz, *refs):
+    share_refs, out_ref = refs[:nz], refs[nz]
+    nk, nq, _, nv = out_ref.shape
     per_tile = LANES // nv
-    pb = lax.axis_index("pb")
     total = share_refs[0][...]
     for share_ref in share_refs[1:]:
         total = total + share_ref[...]
-    for s in range(npb):
-        q = source(pb, s, npb)
-        for k in range(nk):
-            tile, place = divmod(k * npb + s, per_tile)
-            out_ref[k, kq_ref[q, k]] = total[tile, :, place * nv : (place + 1) * nv]
+    for k in range(nk):
+        for j in range(nq):
+            tile, place = divmod(k * nq + j, per_tile)
+            out_ref[k, j] = total[tile, :, place * nv : (place + 1) * nv]
 
 
 def per_device(npb, nz, valence, conduction, screened, kq_table):
@@ -182,17 +205,36 @@
         pltpu.VMEM((nq, nk * nc, nz * CORES * ng), jnp.bfloat16),
     ]
 
-    w_parts = [screened] + [send_pb(screened, s, npb) for s in range(1, npb)]
-    packed = pl.pallas_call(
-        pack_kernel,
+    n_tiles = -(-nk * nq * nv // LANES)
+    own = pl.pallas_call(
+        pack,
         out_shape=jax.ShapeDtypeStruct((nk * nc, nq * ng), jnp.bfloat16),
         in_specs=[vmem],
         out_specs=vmem,
         compiler_params=params,
-        cost_estimate=pl.CostEstimate(flops=0, bytes_accessed=1000000, transcendentals=0),
     )(conduction)
-    mine, shifts = gather_chips(packed, nz)
-    other = [send_core(part, nz) for part in mine]
+    def join(_, *parts):
+        return pl.pallas_call(
+            pack_kernel,
+            out_shape=jax.ShapeDtypeStruct((len(parts) + 1, nk * nc, nq * ng), jnp.bfloat16),
+            in_specs=[vmem] * (len(parts) + 1),
+            out_specs=vmem,
+            compiler_params=params,
+        )(own, *parts)
+
+    w_parts = [screened] + [send_pb(screened, s, npb) for s in range(1, npb)]
+    mine, shifts = gather_chips(conduction, nz, join)
+    sent, prepared = pl.pallas_call(
+        functools.partial(prepare_kernel, npb),
+        out_shape=(
+            jax.ShapeDtypeStruct(mine[0].shape, jnp.bfloat16),
+            jax.ShapeDtypeStruct((n_tiles, LANES, npb * LANES), jnp.bfloat16),
+        ),
+        in_specs=[vmem, vmem, smem],
+        out_specs=(vmem, vmem),
+        compiler_params=params,
+    )(mine[0], valence, kq_table.T)
+    other = [send_core(part, nz) for part in [sent] + mine[1:]]
     near = pl.pallas_call(
         functools.partial(near_kernel, npb, shifts),
         out_shape=jax.ShapeDtypeStruct((npb, nk * nc, ng), jnp.float32),
@@ -204,7 +246,6 @@
             flops=2 * nk * nq * nc * ng * ng * nz, bytes_accessed=3000000, transcendentals=0
         ),
     )(*w_parts, *mine)
-    n_tiles = -(-nk * nq * nv // LANES)
     partial_value = pl.pallas_call(
         functools.partial(partial_kernel, npb, shifts),
         out_shape=jax.ShapeDtypeStruct((n_tiles, nc, LANES), jnp.float32),
@@ -212,16 +253,16 @@
         out_specs=vmem,
         scratch_shapes=join_scratch,
         compiler_params=params,
-    )(*w_parts, *other, near, valence)
+    )(*w_parts, *other, near, prepared)
     chip_value = partial_value + send_core(partial_value, nz)
     shares = [chip_value] + [send_chip(chip_value, s, nz) for s in range(1, nz)]
     return pl.pallas_call(
-        functools.partial(place_kernel, npb, nz),
+        functools.partial(place_kernel, nz),
         out_shape=jax.ShapeDtypeStruct((nk, nq, nc, nv), jnp.float32),
-        in_specs=[vmem] * nz + [smem],
-        out_specs=vmem,
-        compiler_params=params,
-    )(*shares, kq_table.T)
+        in_specs=[vmem] * nz,
+        out_specs=vmem,
+        compiler_params=params,
+    )(*shares)
 
 
 def solution(mesh):

time: 25.5 us -> 23.8 us (0.933)
  waiting for transfers between devices: 7.87 us -> 6.24 us
    ppermute x3, waiting for transfers between devices: 2.06 us -> 0.72 us  [send_pb(): return lax.ppermute(x, 'pb', [(i, partner(i, s, npb)) for i in range(npb)])]
    ppermute x2, waiting for transfers between devices: 2.78 us -> 1.98 us  [gather_chips(): parts.append(lax.ppermute(held, 'ga', pairs))]
    ppermute x3, waiting for transfers between devices: 1.86 us -> 2.48 us  [send_chip(): lax.ppermute(x, 'ga', [(i * CORES + c, partner(i, s, nz) * CORES + c) for...]
    pallas_call x1, Pallas kernels: 1.05 us -> 0.64 us  [per_device(): pl.pallas_call(functools.partial(partial_kernel, npb, shifts), out_shape=...]
    pallas_call x2 -> x4, Pallas kernels: 1.38 us -> 1.6 us  [the longest x1 0.73 us: per_device(): pl.pallas_call(functools.partial(place_kernel, nz), out_shape=jax.ShapeDt...]
  transfers between devices with their start and end apart: 11 -> 11, of which waited for: 5 -> 6; matrix products, arithmetic and copies ran while one was open for 0% -> 0% of each run, Pallas kernels for 2% -> 6%
where the time goes in v3:
time: 23.8 us; the launch traced here: 23.7 us
  starting transfers between devices  13.8 us (58%)
  waiting for transfers between devices  6.24 us (26%)
  Pallas kernels  2.74 us (12%)
  local copies, waits for them, and re-layouts  0.81 us (3%)
    ppermute x2, starting transfers between devices, gather_chips(): parts.append(lax.ppermute(held, 'ga', pairs))  5.68 us
    ppermute x3, starting transfers between devices, send_chip(): lax.ppermute(x, 'ga', [(i * CORES + c, partner(i, s, nz) * CORES + c) for...  4.39 us
    ppermute x3, starting transfers between devices, send_pb(): return lax.ppermute(x, 'pb', [(i, partner(i, s, npb)) for i in range(npb)])  3.49 us
    ppermute x3, waiting for transfers between devices, send_chip(): lax.ppermute(x, 'ga', [(i * CORES + c, partner(i, s, nz) * CORES + c) for...  2.48 us
    ppermute x2, waiting for transfers between devices, gather_chips(): parts.append(lax.ppermute(held, 'ga', pairs))  1.98 us
    ppermute x3, waiting for transfers between devices, send_core(): lax.ppermute(x, 'ga', [(i * CORES + c, i * CORES + 1 - c) for i in range(...  1.06 us
    unnamed x8, local copies, waits for them, and re-layouts  0.81 us
    pallas_call x1, Pallas kernels, per_device(): pl.pallas_call(functools.partial(place_kernel, nz), out_shape=jax.ShapeDt...  0.73 us
  transfers between devices with their start and end apart: 11, of which 6 were waited for; matrix products, arithmetic and copies ran while one was open for 0% of the time, Pallas kernels for 6%

profile of v3, /device:TPU:0, one launch (start us, length us, event | category | flops | bytes accessed | tf_op | source)
XLA Modules:
  0.0 23.7 jit_solution(5639123835108013776)
XLA Ops:
  0.0 4.0 %collective-permute-start.3 = (bf16[6,4,8,96]{3,2,1,0:T(8,128)(2,1)}, bf16[6,4,8,96]{3,2,1,0:T(8,128)(2,1)S(1)}, u32[]{:S(2)}, u32[]{:S(2)}) collective-permute-start(bf16[6,4,8,96]{3,2,1,0:T(8,128)(2,1)} %con_ref.1), channel_id=1, source_target_pairs={{0,4},{1,5},{2,6},{3,7},{4,0},{5,1},{6,2},{7,3},{8,12},{9,13},{10,... | collective-permute-start | bytes 110600 | tf_op jit(solution)/shard_map/ppermute | solution.py:64
  4.0 2.4 %collective-permute-start.2 = (bf16[1,96,768]{2,1,0:T(8,128)(2,1)}, bf16[1,96,768]{2,1,0:T(8,128)(2,1)S(1)}, u32[]{:S(2)}, u32[]{:S(2)}) collective-permute-start(bf16[1,96,768]{2,1,0:T(8,128)(2,1)} %refs_0_.3), channel_id=1, source_target_pairs={{0,24},{8,16},{16,8},{24,0},{1,25},{9,17},{17,9},{25,1},{2,26},{10... | collective-permute-start | bytes 442376 | tf_op jit(solution)/shard_map/ppermute | solution.py:25
  6.5 0.5 %collective-permute-start.1 = (bf16[1,96,768]{2,1,0:T(8,128)(2,1)}, bf16[1,96,768]{2,1,0:T(8,128)(2,1)S(1)}, u32[]{:S(2)}, u32[]{:S(2)}) collective-permute-start(bf16[1,96,768]{2,1,0:T(8,128)(2,1)} %refs_0_.3), channel_id=1, source_target_pairs={{0,16},{8,24},{16,0},{24,8},{1,17},{9,25},{17,1},{25,9},{2,18},{10... | collective-permute-start | bytes 442376 | tf_op jit(solution)/shard_map/ppermute | solution.py:25
  7.0 0.5 %collective-permute-start = (bf16[1,96,768]{2,1,0:T(8,128)(2,1)}, bf16[1,96,768]{2,1,0:T(8,128)(2,1)S(1)}, u32[]{:S(2)}, u32[]{:S(2)}) collective-permute-start(bf16[1,96,768]{2,1,0:T(8,128)(2,1)} %refs_0_.3), channel_id=1, source_target_pairs={{0,8},{8,0},{16,24},{24,16},{1,9},{9,1},{17,25},{25,17},{2,10},{10... | collective-permute-start | bytes 442376 | tf_op jit(solution)/shard_map/ppermute | solution.py:25
  7.5 0.8 %copy-done.2 = bf16[6,4,8,96]{3,2,1,0:T(8,128)(2,1)S(1)} copy-done((bf16[6,4,8,96]{3,2,1,0:T(8,128)(2,1)S(1)}, bf16[6,4,8,96]{3,2,1,0:T(8,128)(2,1)}, u32[]{:S(2)}) %copy-start.2) | copy-done | bytes 36888
  8.3 0.1 shard_map.46.own_ref
  8.4 0.1 shard_map.47.held_ref.refs_4_
  8.5 1.6 %collective-permute-start.5 = (bf16[2,48,384]{2,1,0:T(8,128)(2,1)S(1)}, bf16[2,48,384]{2,1,0:T(8,128)(2,1)S(1)}, u32[]{:S(2)}, u32[]{:S(2)}) collective-permute-start(bf16[2,48,384]{2,1,0:T(8,128)(2,1)S(1)} %shard_map.47.held_ref.refs_4_), channel_id=1, source_target_pairs={{0,2},{1,3},{2,0},{3,1},{4,6},{5,7},{6,4},{7,5},{8,10},{9,11},{10,... | collective-permute-start | bytes 221192 | tf_op jit(solution)/shard_map/ppermute | solution.py:64
  10.2 0.7 %shard_map.48 = (bf16[2,48,384]{2,1,0:T(8,128)(2,1)S(1)}, bf16[3,128,512]{2,1,0:T(8,128)(2,1)S(1)}) custom-call(bf16[2,48,384]{2,1,0:T(8,128)(2,1)S(1)} %shard_map.47.held_ref.refs_4_, bf16[6,4,16,96]{3,2,1,0:T(8,128)(2,1)S(1)} %copy-done.1, s32[4,6]{1,0:T(4,128)S(1)} %bitcast.1), custom_call_target="tpu_custom_call" | custom-call | tf_op jit(solution)/shard_map/pallas_call | solution.py:227
  10.9 0.1 collective-permute-start.4
  11.0 2.0 %collective-permute-done.5.refs_5_ = bf16[2,48,384]{2,1,0:T(8,128)(2,1)S(1)} collective-permute-done((bf16[2,48,384]{2,1,0:T(8,128)(2,1)S(1)}, bf16[2,48,384]{2,1,0:T(8,128)(2,1)S(1)}, u32[]{:S(2)}, u32[]{:S(2)}) %collective-permute-start.5) | collective-permute-done | bytes 73760 | tf_op jit(solution)/shard_map/ppermute | solution.py:64
  13.0 0.7 %collective-permute-done.1.refs_2_ = bf16[1,96,768]{2,1,0:T(8,128)(2,1)S(1)} collective-permute-done((bf16[1,96,768]{2,1,0:T(8,128)(2,1)}, bf16[1,96,768]{2,1,0:T(8,128)(2,1)S(1)}, u32[]{:S(2)}, u32[]{:S(2)}) %collective-permute-start.1) | collective-permute-done | bytes 147488 | tf_op jit(solution)/shard_map/ppermute | solution.py:25
  13.6 0.1 collective-permute-done.refs_1_
  13.7 0.5 %shard_map.49.refs_6_ = f32[4,48,96]{2,1,0:T(8,128)S(1)} custom-call(bf16[1,96,768]{2,1,0:T(8,128)(2,1)S(1)} %copy-done, bf16[1,96,768]{2,1,0:T(8,128)(2,1)S(1)} %collective-permute-done.refs_1_, bf16[1,96,768]{2,1,0:T(8,128)(2,1)S(1)} %collective-permute-done.1.refs_2_, bf16[1,96,768]{2,1,0:T(8,128)(2,1)S(1)} %collective-permute-done.2.refs_3_, ...), custom_call_target="tpu_custom_call" | custom-call | flops 14155776 | bytes 3000000 | tf_op jit(solution)/shard_map/pallas_call | solution.py:238
  14.2 0.0 collective-permute-done.6.refs_5_
  14.2 0.6 %shard_map.50 = f32[3,8,128]{2,1,0:T(8,128)S(1)} custom-call(bf16[1,96,768]{2,1,0:T(8,128)(2,1)S(1)} %copy-done, bf16[1,96,768]{2,1,0:T(8,128)(2,1)S(1)} %collective-permute-done.refs_1_, bf16[1,96,768]{2,1,0:T(8,128)(2,1)S(1)} %collective-permute-done.1.refs_2_, bf16[1,96,768]{2,1,0:T(8,128)(2,1)S(1)} %collective-permute-done.2.refs_3_, ...), custom_call_target="tpu_custom_call" | custom-call | tf_op jit(solution)/shard_map/pallas_call | solution.py:249
  14.9 0.2 collective-permute-start.7
  15.0 1.0 %collective-permute-done.7 = f32[3,8,128]{2,1,0:T(8,128)S(1)} collective-permute-done((f32[3,8,128]{2,1,0:T(8,128)S(1)}, f32[3,8,128]{2,1,0:T(8,128)S(1)}, u32[]{:S(2)}, u32[]{:S(2)}) %collective-permute-start.7) | collective-permute-done | bytes 12320 | tf_op jit(solution)/shard_map/ppermute | solution.py:77
  16.1 2.2 %collective-permute-start.10 = (f32[3,8,128]{2,1,0:T(8,128)S(1)}, f32[3,8,128]{2,1,0:T(8,128)S(1)}, u32[]{:S(2)}, u32[]{:S(2)}) collective-permute-start(f32[3,8,128]{2,1,0:T(8,128)S(1)} %add.3.refs_0_), channel_id=1, source_target_pairs={{0,6},{1,7},{2,4},{3,5},{4,2},{5,3},{6,0},{7,1},{8,14},{9,15},{10,... | collective-permute-start | bytes 36872 | tf_op jit(solution)/shard_map/ppermute | solution.py:29
  18.3 0.8 %collective-permute-start.9 = (f32[3,8,128]{2,1,0:T(8,128)S(1)}, f32[3,8,128]{2,1,0:T(8,128)S(1)}, u32[]{:S(2)}, u32[]{:S(2)}) collective-permute-start(f32[3,8,128]{2,1,0:T(8,128)S(1)} %add.3.refs_0_), channel_id=1, source_target_pairs={{0,4},{1,5},{2,6},{3,7},{4,0},{5,1},{6,2},{7,3},{8,12},{9,13},{10,... | collective-permute-start | bytes 36872 | tf_op jit(solution)/shard_map/ppermute | solution.py:29
  19.1 1.3 %collective-permute-start.8 = (f32[3,8,128]{2,1,0:T(8,128)S(1)}, f32[3,8,128]{2,1,0:T(8,128)S(1)}, u32[]{:S(2)}, u32[]{:S(2)}) collective-permute-start(f32[3,8,128]{2,1,0:T(8,128)S(1)} %add.3.refs_0_), channel_id=1, source_target_pairs={{0,2},{1,3},{2,0},{3,1},{4,6},{5,7},{6,4},{7,5},{8,10},{9,11},{10,... | collective-permute-start | bytes 36872 | tf_op jit(solution)/shard_map/ppermute | solution.py:29
  20.5 1.1 %collective-permute-done.10.refs_3_ = f32[3,8,128]{2,1,0:T(8,128)S(1)} collective-permute-done((f32[3,8,128]{2,1,0:T(8,128)S(1)}, f32[3,8,128]{2,1,0:T(8,128)S(1)}, u32[]{:S(2)}, u32[]{:S(2)}) %collective-permute-start.10) | collective-permute-done | bytes 12320 | tf_op jit(solution)/shard_map/ppermute | solution.py:29
  21.6 1.4 %collective-permute-done.9.refs_2_ = f32[3,8,128]{2,1,0:T(8,128)S(1)} collective-permute-done((f32[3,8,128]{2,1,0:T(8,128)S(1)}, f32[3,8,128]{2,1,0:T(8,128)S(1)}, u32[]{:S(2)}, u32[]{:S(2)}) %collective-permute-start.9) | collective-permute-done | bytes 12320 | tf_op jit(solution)/shard_map/ppermute | solution.py:29
  22.9 0.7 %shard_map.51 = f32[6,4,8,16]{3,2,1,0:T(8,128)} custom-call(f32[3,8,128]{2,1,0:T(8,128)S(1)} %add.3.refs_0_, f32[3,8,128]{2,1,0:T(8,128)S(1)} %collective-permute-done.8.refs_1_, f32[3,8,128]{2,1,0:T(8,128)S(1)} %collective-permute-done.9.refs_2_, f32[3,8,128]{2,1,0:T(8,128)S(1)} %collective-permute-done.10.refs_3_), custom_call_target="tpu_custom_call" | custom-call | tf_op jit(solution)/shard_map/pallas_call | solution.py:259
  (13 shorter events, 0.0 us)
Async XLA Ops:
  0.0 8.4 %collective-permute-start.3 = (bf16[6,4,8,96]{3,2,1,0:T(8,128)(2,1)}, bf16[6,4,8,96]{3,2,1,0:T(8,128)(2,1)S(1)}, u32[]{:S(2)}, u32[]{:S(2)}) collective-permute-start(bf16[6,4,8,96]{3,2,1,0:T(8,128)(2,1)} %con_ref.1), channel_id=1, source_target_pairs={{0,4},{1,5},{2,6},{3,7},{4,0},{5,1},{6,2},{7,3},{8,12},{9,13},{10,... | collective-permute-start | bytes 110600 | tf_op jit(solution)/shard_map/ppermute | solution.py:64
  4.0 8.9 %collective-permute-start.2 = (bf16[1,96,768]{2,1,0:T(8,128)(2,1)}, bf16[1,96,768]{2,1,0:T(8,128)(2,1)S(1)}, u32[]{:S(2)}, u32[]{:S(2)}) collective-permute-start(bf16[1,96,768]{2,1,0:T(8,128)(2,1)} %refs_0_.3), channel_id=1, source_target_pairs={{0,24},{8,16},{16,8},{24,0},{1,25},{9,17},{17,9},{25,1},{2,26},{10... | collective-permute-start | bytes 442376 | tf_op jit(solution)/shard_map/ppermute | solution.py:25
  6.5 7.1 %collective-permute-start.1 = (bf16[1,96,768]{2,1,0:T(8,128)(2,1)}, bf16[1,96,768]{2,1,0:T(8,128)(2,1)S(1)}, u32[]{:S(2)}, u32[]{:S(2)}) collective-permute-start(bf16[1,96,768]{2,1,0:T(8,128)(2,1)} %refs_0_.3), channel_id=1, source_target_pairs={{0,16},{8,24},{16,0},{24,8},{1,17},{9,25},{17,1},{25,9},{2,18},{10... | collective-permute-start | bytes 442376 | tf_op jit(solution)/shard_map/ppermute | solution.py:25
  7.0 6.7 %collective-permute-start = (bf16[1,96,768]{2,1,0:T(8,128)(2,1)}, bf16[1,96,768]{2,1,0:T(8,128)(2,1)S(1)}, u32[]{:S(2)}, u32[]{:S(2)}) collective-permute-start(bf16[1,96,768]{2,1,0:T(8,128)(2,1)} %refs_0_.3), channel_id=1, source_target_pairs={{0,8},{8,0},{16,24},{24,16},{1,9},{9,1},{17,25},{25,17},{2,10},{10... | collective-permute-start | bytes 442376 | tf_op jit(solution)/shard_map/ppermute | solution.py:25
  7.5 0.8 %copy-start.2 = (bf16[6,4,8,96]{3,2,1,0:T(8,128)(2,1)S(1)}, bf16[6,4,8,96]{3,2,1,0:T(8,128)(2,1)}, u32[]{:S(2)}) copy-start(bf16[6,4,8,96]{3,2,1,0:T(8,128)(2,1)} %con_ref.1) | copy-start | bytes 110596
  8.3 1.9 %copy-start.1 = (bf16[6,4,16,96]{3,2,1,0:T(8,128)(2,1)S(1)}, bf16[6,4,16,96]{3,2,1,0:T(8,128)(2,1)}, u32[]{:S(2)}) copy-start(bf16[6,4,16,96]{3,2,1,0:T(8,128)(2,1)} %val_ref.1) | copy-start | bytes 221188
  8.3 1.9 %copy-start.3 = (s32[6,4]{0,1:T(4,128)S(1)}, s32[6,4]{0,1:T(4,128)}, u32[]{:S(2)}) copy-start(s32[6,4]{0,1:T(4,128)} %param.7) | copy-start | bytes 292
  8.4 5.3 %copy-start = (bf16[1,96,768]{2,1,0:T(8,128)(2,1)S(1)}, bf16[1,96,768]{2,1,0:T(8,128)(2,1)}, u32[]{:S(2)}) copy-start(bf16[1,96,768]{2,1,0:T(8,128)(2,1)} %refs_0_.3) | copy-start | bytes 442372
  8.5 4.4 %collective-permute-start.5 = (bf16[2,48,384]{2,1,0:T(8,128)(2,1)S(1)}, bf16[2,48,384]{2,1,0:T(8,128)(2,1)S(1)}, u32[]{:S(2)}, u32[]{:S(2)}) collective-permute-start(bf16[2,48,384]{2,1,0:T(8,128)(2,1)S(1)} %shard_map.47.held_ref.refs_4_), channel_id=1, source_target_pairs={{0,2},{1,3},{2,0},{3,1},{4,6},{5,7},{6,4},{7,5},{8,10},{9,11},{10,... | collective-permute-start | bytes 221192 | tf_op jit(solution)/shard_map/ppermute | solution.py:64
  10.9 3.3 %collective-permute-start.4 = (bf16[2,48,384]{2,1,0:T(8,128)(2,1)S(1)}, bf16[2,48,384]{2,1,0:T(8,128)(2,1)S(1)}, u32[]{:S(2)}, u32[]{:S(2)}) collective-permute-start(bf16[2,48,384]{2,1,0:T(8,128)(2,1)S(1)} %get-tuple-element.7), channel_id=1, source_target_pairs={{0,1},{1,0},{2,3},{3,2},{4,5},{5,4},{6,7},{7,6},{8,9},{9,8},{10,11... | collective-permute-start | bytes 221192 | tf_op jit(solution)/shard_map/ppermute | solution.py:77
  13.0 1.3 %collective-permute-start.6 = (bf16[2,48,384]{2,1,0:T(8,128)(2,1)S(1)}, bf16[2,48,384]{2,1,0:T(8,128)(2,1)S(1)}, u32[]{:S(2)}, u32[]{:S(2)}) collective-permute-start(bf16[2,48,384]{2,1,0:T(8,128)(2,1)S(1)} %collective-permute-done.5.refs_5_), channel_id=1, source_target_pairs={{0,1},{1,0},{2,3},{3,2},{4,5},{5,4},{6,7},{7,6},{8,9},{9,8},{10,11... | collective-permute-start | bytes 221192 | tf_op jit(solution)/shard_map/ppermute | solution.py:77
  14.9 1.2 %collective-permute-start.7 = (f32[3,8,128]{2,1,0:T(8,128)S(1)}, f32[3,8,128]{2,1,0:T(8,128)S(1)}, u32[]{:S(2)}, u32[]{:S(2)}) collective-permute-start(f32[3,8,128]{2,1,0:T(8,128)S(1)} %shard_map.50), channel_id=1, source_target_pairs={{0,1},{1,0},{2,3},{3,2},{4,5},{5,4},{6,7},{7,6},{8,9},{9,8},{10,11... | collective-permute-start | bytes 36872 | tf_op jit(solution)/shard_map/ppermute | solution.py:77
  16.1 5.5 %collective-permute-start.10 = (f32[3,8,128]{2,1,0:T(8,128)S(1)}, f32[3,8,128]{2,1,0:T(8,128)S(1)}, u32[]{:S(2)}, u32[]{:S(2)}) collective-permute-start(f32[3,8,128]{2,1,0:T(8,128)S(1)} %add.3.refs_0_), channel_id=1, source_target_pairs={{0,6},{1,7},{2,4},{3,5},{4,2},{5,3},{6,0},{7,1},{8,14},{9,15},{10,... | collective-permute-start | bytes 36872 | tf_op jit(solution)/shard_map/ppermute | solution.py:29
  18.3 4.7 %collective-permute-start.9 = (f32[3,8,128]{2,1,0:T(8,128)S(1)}, f32[3,8,128]{2,1,0:T(8,128)S(1)}, u32[]{:S(2)}, u32[]{:S(2)}) collective-permute-start(f32[3,8,128]{2,1,0:T(8,128)S(1)} %add.3.refs_0_), channel_id=1, source_target_pairs={{0,4},{1,5},{2,6},{3,7},{4,0},{5,1},{6,2},{7,3},{8,12},{9,13},{10,... | collective-permute-start | bytes 36872 | tf_op jit(solution)/shard_map/ppermute | solution.py:29
  19.1 3.8 %collective-permute-start.8 = (f32[3,8,128]{2,1,0:T(8,128)S(1)}, f32[3,8,128]{2,1,0:T(8,128)S(1)}, u32[]{:S(2)}, u32[]{:S(2)}) collective-permute-start(f32[3,8,128]{2,1,0:T(8,128)S(1)} %add.3.refs_0_), channel_id=1, source_target_pairs={{0,2},{1,3},{2,0},{3,1},{4,6},{5,7},{6,4},{7,5},{8,10},{9,11},{10,... | collective-permute-start | bytes 36872 | tf_op jit(solution)/shard_map/ppermute | solution.py:29

commit v4 on v3

--- a/solution.py
+++ b/solution.py
@@ -47,23 +47,23 @@
     return i + ((digit + s) % size - digit) * stride
 
 
-def gather_chips(x, nz, join):
-    shifts, parts = [()], [x]
-    for i, (stride, size) in enumerate(chip_stages(nz)):
-        held = x
-        if i:
-            held = join(*parts) if i == 1 else jnp.concatenate(parts)
-        parts = [held]
-        old = shifts
+def gather_chips(x, nz, pack):
+    groups = [([()], x[None])]
+    for stride, size in chip_stages(nz):
+        if len(groups) > 1:
+            paths = [path for paths, _ in groups[1:] for path in paths]
+            groups[1:] = [(paths, pack(*[array for _, array in groups[1:]], flops=1000000000))]
+        old = list(groups)
         for s in range(1, size):
             pairs = [
                 (i * CORES + c, shift_digit(i, s, stride, size) * CORES + c)
                 for i in range(nz)
                 for c in range(CORES)
             ]
-            parts.append(lax.ppermute(held, "ga", pairs))
-            shifts = shifts + [was + ((stride, size, size - s),) for was in old]
-    return parts, shifts
+            for paths, array in old:
+                moved = [path + ((stride, size, size - s),) for path in paths]
+                groups.append((moved, lax.ppermute(array, "ga", pairs)))
+    return groups
 
 
 def apply_shifts(z, path):
@@ -90,18 +90,27 @@
         out_ref[:, q * ng : (q + 1) * ng] = rows.astype(jnp.bfloat16)
 
 
-def pack_kernel(own_ref, *refs):
-    out_ref = refs[-1]
-    out_ref[0] = own_ref[...]
-    for i, con_ref in enumerate(refs[:-1]):
-        pack(con_ref, out_ref.at[i + 1])
-
-
-def prepare_kernel(npb, held_ref, val_ref, kq_ref, sent_ref, out_ref):
+def pack_groups(refs, out_ref):
+    n = 0
+    for ref in refs:
+        for i in range(ref.shape[0]):
+            if len(ref.shape) == 3:
+                out_ref[n] = ref[i]
+            else:
+                pack(ref.at[i], out_ref.at[n])
+            n += 1
+
+
+def pack_kernel(*refs):
+    pack_groups(refs[:-1], refs[-1])
+
+
+def prepare_kernel(npb, *refs):
+    val_ref, kq_ref, packed_ref, out_ref = refs[-4:]
     nk, nq, nv, ng = val_ref.shape
     per_tile = LANES // nv
     pb = lax.axis_index("pb")
-    sent_ref[...] = held_ref[...]
+    pack_groups(refs[:-4], packed_ref)
     out_ref[...] = jnp.zeros(out_ref.shape, out_ref.dtype)
     for s in range(npb):
         q = source(pb, s, npb)
@@ -206,35 +215,34 @@
     ]
 
     n_tiles = -(-nk * nq * nv // LANES)
-    own = pl.pallas_call(
-        pack,
-        out_shape=jax.ShapeDtypeStruct((nk * nc, nq * ng), jnp.bfloat16),
-        in_specs=[vmem],
-        out_specs=vmem,
-        compiler_params=params,
-    )(conduction)
-    def join(_, *parts):
+    def pack_all(*parts, flops=0):
+        n = sum(part.shape[0] for part in parts)
         return pl.pallas_call(
             pack_kernel,
-            out_shape=jax.ShapeDtypeStruct((len(parts) + 1, nk * nc, nq * ng), jnp.bfloat16),
-            in_specs=[vmem] * (len(parts) + 1),
+            out_shape=jax.ShapeDtypeStruct((n, nk * nc, nq * ng), jnp.bfloat16),
+            in_specs=[vmem] * len(parts),
             out_specs=vmem,
             compiler_params=params,
-        )(own, *parts)
+            cost_estimate=pl.CostEstimate(flops=flops, bytes_accessed=0, transcendentals=0),
+        )(*parts)
 
     w_parts = [screened] + [send_pb(screened, s, npb) for s in range(1, npb)]
-    mine, shifts = gather_chips(conduction, nz, join)
-    sent, prepared = pl.pallas_call(
+    groups = gather_chips(conduction, nz, pack_all)
+    shifts = [path for paths, _ in groups for path in paths]
+    last = groups[-1][1]
+    held = [pack_all(groups[0][1])] + [array for _, array in groups[1:-1]]
+    packed, prepared = pl.pallas_call(
         functools.partial(prepare_kernel, npb),
         out_shape=(
-            jax.ShapeDtypeStruct(mine[0].shape, jnp.bfloat16),
+            jax.ShapeDtypeStruct((nz - last.shape[0], nk * nc, nq * ng), jnp.bfloat16),
             jax.ShapeDtypeStruct((n_tiles, LANES, npb * LANES), jnp.bfloat16),
         ),
-        in_specs=[vmem, vmem, smem],
+        in_specs=[vmem] * (len(held) + 1) + [smem],
         out_specs=(vmem, vmem),
         compiler_params=params,
-    )(mine[0], valence, kq_table.T)
-    other = [send_core(part, nz) for part in [sent] + mine[1:]]
+    )(*held, valence, kq_table.T)
+    mine = [packed, last]
+    other = [send_core(part, nz) for part in mine]
     near = pl.pallas_call(
         functools.partial(near_kernel, npb, shifts),
         out_shape=jax.ShapeDtypeStruct((npb, nk * nc, ng), jnp.float32),
@@ -243,7 +251,7 @@
         scratch_shapes=join_scratch,
         compiler_params=params,
         cost_estimate=pl.CostEstimate(
-            flops=2 * nk * nq * nc * ng * ng * nz, bytes_accessed=3000000, transcendentals=0
+            flops=1000000000, bytes_accessed=3000000, transcendentals=0
         ),
     )(*w_parts, *mine)
     partial_value = pl.pallas_call(

time: 23.8 us -> 23.7 us (level)
  local copies, waits for them, and re-layouts: 0.81 us -> 0.02 us
  starting transfers between devices: 13.8 us -> 14.3 us
    unnamed x8, local copies, waits for them, and re-layouts: 0.81 us -> 0.02 us
    ppermute x2 -> x3, waiting for transfers between devices: 1.98 us -> 2.62 us  [gather_chips(): groups.append((moved, lax.ppermute(array, 'ga', pairs)))]
    ppermute x2 -> x3, starting transfers between devices: 5.68 us -> 6.13 us  [gather_chips(): groups.append((moved, lax.ppermute(array, 'ga', pairs)))]
    ppermute x3, waiting for transfers between devices: 2.48 us -> 2.08 us  [send_chip(): lax.ppermute(x, 'ga', [(i * CORES + c, partner(i, s, nz) * CORES + c) for...]
    ppermute x3, waiting for transfers between devices: 0.72 us -> 0.43 us  [send_pb(): return lax.ppermute(x, 'pb', [(i, partner(i, s, npb)) for i in range(npb)])]
  transfers between devices with their start and end apart: 11 -> 12, of which waited for: 6 -> 9; matrix products, arithmetic and copies ran while one was open for 0% -> 0% of each run, Pallas kernels for 6% -> 6%
where the time goes in v4:
time: 23.7 us; the launch traced here: 23.5 us
  starting transfers between devices  14.3 us (60%)
  waiting for transfers between devices  6.43 us (27%)
  Pallas kernels  2.74 us (12%)
    ppermute x3, starting transfers between devices, gather_chips(): groups.append((moved, lax.ppermute(array, 'ga', pairs)))  6.13 us
    ppermute x3, starting transfers between devices, send_chip(): lax.ppermute(x, 'ga', [(i * CORES + c, partner(i, s, nz) * CORES + c) for...  4.39 us
    ppermute x3, starting transfers between devices, send_pb(): return lax.ppermute(x, 'pb', [(i, partner(i, s, npb)) for i in range(npb)])  3.49 us
    ppermute x3, waiting for transfers between devices, gather_chips(): groups.append((moved, lax.ppermute(array, 'ga', pairs)))  2.62 us
    ppermute x3, waiting for transfers between devices, send_chip(): lax.ppermute(x, 'ga', [(i * CORES + c, partner(i, s, nz) * CORES + c) for...  2.08 us
    ppermute x3, waiting for transfers between devices, send_core(): lax.ppermute(x, 'ga', [(i * CORES + c, i * CORES + 1 - c) for i in range(...  1.3 us
    pallas_call x1, Pallas kernels, per_device(): pl.pallas_call(functools.partial(place_kernel, nz), out_shape=jax.ShapeDt...  0.73 us
    pallas_call x1, Pallas kernels, per_device(): pl.pallas_call(functools.partial(prepare_kernel, npb), out_shape=(jax.Sha...  0.7 us
  transfers between devices with their start and end apart: 12, of which 9 were waited for; matrix products, arithmetic and copies ran while one was open for 0% of the time, Pallas kernels for 6%

profile of v4, /device:TPU:0, one launch (start us, length us, event | category | flops | bytes accessed | tf_op | source)
XLA Modules:
  0.0 23.5 jit_solution(4061279389153371879)
XLA Ops:
  0.0 4.0 %collective-permute-start.3 = (bf16[1,6,4,8,96]{4,3,2,1,0:T(8,128)(2,1)}, bf16[1,6,4,8,96]{4,3,2,1,0:T(8,128)(2,1)S(1)}, u32[]{:S(2)}, u32[]{:S(2)}) collective-permute-start(bf16[1,6,4,8,96]{4,3,2,1,0:T(8,128)(2,1)} %bitcast.2), channel_id=1, source_target_pairs={{0,4},{1,5},{2,6},{3,7},{4,0},{5,1},{6,2},{7,3},{8,12},{9,13},{10,... | collective-permute-start | bytes 110600 | tf_op jit(solution)/shard_map/ppermute | solution.py:65
  4.0 2.4 %collective-permute-start.2 = (bf16[1,96,768]{2,1,0:T(8,128)(2,1)}, bf16[1,96,768]{2,1,0:T(8,128)(2,1)S(1)}, u32[]{:S(2)}, u32[]{:S(2)}) collective-permute-start(bf16[1,96,768]{2,1,0:T(8,128)(2,1)} %refs_0_.3), channel_id=1, source_target_pairs={{0,24},{8,16},{16,8},{24,0},{1,25},{9,17},{17,9},{25,1},{2,26},{10... | collective-permute-start | bytes 442376 | tf_op jit(solution)/shard_map/ppermute | solution.py:25
  6.5 0.5 %collective-permute-start.1 = (bf16[1,96,768]{2,1,0:T(8,128)(2,1)}, bf16[1,96,768]{2,1,0:T(8,128)(2,1)S(1)}, u32[]{:S(2)}, u32[]{:S(2)}) collective-permute-start(bf16[1,96,768]{2,1,0:T(8,128)(2,1)} %refs_0_.3), channel_id=1, source_target_pairs={{0,16},{8,24},{16,0},{24,8},{1,17},{9,25},{17,1},{25,9},{2,18},{10... | collective-permute-start | bytes 442376 | tf_op jit(solution)/shard_map/ppermute | solution.py:25
  7.0 0.5 %collective-permute-start = (bf16[1,96,768]{2,1,0:T(8,128)(2,1)}, bf16[1,96,768]{2,1,0:T(8,128)(2,1)S(1)}, u32[]{:S(2)}, u32[]{:S(2)}) collective-permute-start(bf16[1,96,768]{2,1,0:T(8,128)(2,1)} %refs_0_.3), channel_id=1, source_target_pairs={{0,8},{8,0},{16,24},{24,16},{1,9},{9,1},{17,25},{25,17},{2,10},{10... | collective-permute-start | bytes 442376 | tf_op jit(solution)/shard_map/ppermute | solution.py:25
  7.5 1.6 %collective-permute-start.4 = (bf16[1,6,4,8,96]{4,3,2,1,0:T(8,128)(2,1)}, bf16[1,6,4,8,96]{4,3,2,1,0:T(8,128)(2,1)S(1)}, u32[]{:S(2)}, u32[]{:S(2)}) collective-permute-start(bf16[1,6,4,8,96]{4,3,2,1,0:T(8,128)(2,1)} %bitcast.3), channel_id=1, source_target_pairs={{0,2},{1,3},{2,0},{3,1},{4,6},{5,7},{6,4},{7,5},{8,10},{9,11},{10,... | collective-permute-start | bytes 110600 | tf_op jit(solution)/shard_map/ppermute | solution.py:65
  9.1 0.1 shard_map.47.refs_1_
  9.2 0.5 %collective-permute-start.6 = (bf16[1,48,384]{2,1,0:T(8,128)(2,1)S(1)}, bf16[1,48,384]{2,1,0:T(8,128)(2,1)S(1)}, u32[]{:S(2)}, u32[]{:S(2)}) collective-permute-start(bf16[1,48,384]{2,1,0:T(8,128)(2,1)S(1)} %shard_map.47.refs_1_), channel_id=1, source_target_pairs={{0,2},{1,3},{2,0},{3,1},{4,6},{5,7},{6,4},{7,5},{8,10},{9,11},{10,... | collective-permute-start | bytes 110600 | tf_op jit(solution)/shard_map/ppermute | solution.py:65
  9.7 0.1 shard_map.46.refs_0_
  9.8 2.0 %collective-permute-done.4.refs_2_ = bf16[1,6,4,8,96]{4,3,2,1,0:T(8,128)(2,1)S(1)} collective-permute-done((bf16[1,6,4,8,96]{4,3,2,1,0:T(8,128)(2,1)}, bf16[1,6,4,8,96]{4,3,2,1,0:T(8,128)(2,1)S(1)}, u32[]{:S(2)}, u32[]{:S(2)}) %collective-permute-start.4) | collective-permute-done | bytes 36896 | tf_op jit(solution)/shard_map/ppermute | solution.py:65
  11.8 0.7 %shard_map.48 = (bf16[3,48,384]{2,1,0:T(8,128)(2,1)S(1)}, bf16[3,128,512]{2,1,0:T(8,128)(2,1)S(1)}) custom-call(bf16[1,48,384]{2,1,0:T(8,128)(2,1)S(1)} %shard_map.46.refs_0_, bf16[1,48,384]{2,1,0:T(8,128)(2,1)S(1)} %shard_map.47.refs_1_, bf16[1,6,4,8,96]{4,3,2,1,0:T(8,128)(2,1)S(1)} %collective-permute-done.4.refs_2_, bf16[6,4,16,96]{3,2,1,0:T(8,128)(2,1)S(1)} %copy-done.1, ...), custom_call_target="tpu_custom_call" | custom-call | tf_op jit(solution)/shard_map/pallas_call | solution.py:234
  12.6 0.6 %collective-permute-done.6.refs_5_ = bf16[1,48,384]{2,1,0:T(8,128)(2,1)S(1)} collective-permute-done((bf16[1,48,384]{2,1,0:T(8,128)(2,1)S(1)}, bf16[1,48,384]{2,1,0:T(8,128)(2,1)S(1)}, u32[]{:S(2)}, u32[]{:S(2)}) %collective-permute-start.6) | collective-permute-done | bytes 36896 | tf_op jit(solution)/shard_map/ppermute | solution.py:65
  13.2 0.4 %collective-permute-done.1.refs_2_ = bf16[1,96,768]{2,1,0:T(8,128)(2,1)S(1)} collective-permute-done((bf16[1,96,768]{2,1,0:T(8,128)(2,1)}, bf16[1,96,768]{2,1,0:T(8,128)(2,1)S(1)}, u32[]{:S(2)}, u32[]{:S(2)}) %collective-permute-start.1) | collective-permute-done | bytes 147488 | tf_op jit(solution)/shard_map/ppermute | solution.py:25
  13.7 0.5 %shard_map.49.refs_6_ = f32[4,48,96]{2,1,0:T(8,128)S(1)} custom-call(bf16[1,96,768]{2,1,0:T(8,128)(2,1)S(1)} %copy-done, bf16[1,96,768]{2,1,0:T(8,128)(2,1)S(1)} %collective-permute-done.refs_1_, bf16[1,96,768]{2,1,0:T(8,128)(2,1)S(1)} %collective-permute-done.1.refs_2_, bf16[1,96,768]{2,1,0:T(8,128)(2,1)S(1)} %collective-permute-done.2.refs_3_, ...), custom_call_target="tpu_custom_call" | custom-call | flops 1000000000 | bytes 3000000 | tf_op jit(solution)/shard_map/pallas_call | solution.py:246
  14.2 0.3 %collective-permute-done.7.refs_5_ = bf16[1,48,384]{2,1,0:T(8,128)(2,1)S(1)} collective-permute-done((bf16[1,48,384]{2,1,0:T(8,128)(2,1)S(1)}, bf16[1,48,384]{2,1,0:T(8,128)(2,1)S(1)}, u32[]{:S(2)}, u32[]{:S(2)}) %collective-permute-start.7) | collective-permute-done | bytes 36896 | tf_op jit(solution)/shard_map/ppermute | solution.py:77
  14.5 0.6 %shard_map.50 = f32[3,8,128]{2,1,0:T(8,128)S(1)} custom-call(bf16[1,96,768]{2,1,0:T(8,128)(2,1)S(1)} %copy-done, bf16[1,96,768]{2,1,0:T(8,128)(2,1)S(1)} %collective-permute-done.refs_1_, bf16[1,96,768]{2,1,0:T(8,128)(2,1)S(1)} %collective-permute-done.1.refs_2_, bf16[1,96,768]{2,1,0:T(8,128)(2,1)S(1)} %collective-permute-done.2.refs_3_, ...), custom_call_target="tpu_custom_call" | custom-call | tf_op jit(solution)/shard_map/pallas_call | solution.py:257
  15.1 0.2 collective-permute-start.8
  15.3 1.0 %collective-permute-done.8 = f32[3,8,128]{2,1,0:T(8,128)S(1)} collective-permute-done((f32[3,8,128]{2,1,0:T(8,128)S(1)}, f32[3,8,128]{2,1,0:T(8,128)S(1)}, u32[]{:S(2)}, u32[]{:S(2)}) %collective-permute-start.8) | collective-permute-done | bytes 12320 | tf_op jit(solution)/shard_map/ppermute | solution.py:77
  16.3 1.6 %collective-permute-start.11 = (f32[3,8,128]{2,1,0:T(8,128)S(1)}, f32[3,8,128]{2,1,0:T(8,128)S(1)}, u32[]{:S(2)}, u32[]{:S(2)}) collective-permute-start(f32[3,8,128]{2,1,0:T(8,128)S(1)} %add.3.refs_0_), channel_id=1, source_target_pairs={{0,6},{1,7},{2,4},{3,5},{4,2},{5,3},{6,0},{7,1},{8,14},{9,15},{10,... | collective-permute-start | bytes 36872 | tf_op jit(solution)/shard_map/ppermute | solution.py:29
  17.9 1.2 %collective-permute-start.10 = (f32[3,8,128]{2,1,0:T(8,128)S(1)}, f32[3,8,128]{2,1,0:T(8,128)S(1)}, u32[]{:S(2)}, u32[]{:S(2)}) collective-permute-start(f32[3,8,128]{2,1,0:T(8,128)S(1)} %add.3.refs_0_), channel_id=1, source_target_pairs={{0,4},{1,5},{2,6},{3,7},{4,0},{5,1},{6,2},{7,3},{8,12},{9,13},{10,... | collective-permute-start | bytes 36872 | tf_op jit(solution)/shard_map/ppermute | solution.py:29
  19.1 1.6 %collective-permute-start.9 = (f32[3,8,128]{2,1,0:T(8,128)S(1)}, f32[3,8,128]{2,1,0:T(8,128)S(1)}, u32[]{:S(2)}, u32[]{:S(2)}) collective-permute-start(f32[3,8,128]{2,1,0:T(8,128)S(1)} %add.3.refs_0_), channel_id=1, source_target_pairs={{0,2},{1,3},{2,0},{3,1},{4,6},{5,7},{6,4},{7,5},{8,10},{9,11},{10,... | collective-permute-start | bytes 36872 | tf_op jit(solution)/shard_map/ppermute | solution.py:29
  20.7 1.1 %collective-permute-done.11.refs_3_ = f32[3,8,128]{2,1,0:T(8,128)S(1)} collective-permute-done((f32[3,8,128]{2,1,0:T(8,128)S(1)}, f32[3,8,128]{2,1,0:T(8,128)S(1)}, u32[]{:S(2)}, u32[]{:S(2)}) %collective-permute-start.11) | collective-permute-done | bytes 12320 | tf_op jit(solution)/shard_map/ppermute | solution.py:29
  21.8 0.7 %collective-permute-done.10.refs_2_ = f32[3,8,128]{2,1,0:T(8,128)S(1)} collective-permute-done((f32[3,8,128]{2,1,0:T(8,128)S(1)}, f32[3,8,128]{2,1,0:T(8,128)S(1)}, u32[]{:S(2)}, u32[]{:S(2)}) %collective-permute-start.10) | collective-permute-done | bytes 12320 | tf_op jit(solution)/shard_map/ppermute | solution.py:29
  22.5 0.3 %collective-permute-done.9.refs_1_ = f32[3,8,128]{2,1,0:T(8,128)S(1)} collective-permute-done((f32[3,8,128]{2,1,0:T(8,128)S(1)}, f32[3,8,128]{2,1,0:T(8,128)S(1)}, u32[]{:S(2)}, u32[]{:S(2)}) %collective-permute-start.9) | collective-permute-done | bytes 12320 | tf_op jit(solution)/shard_map/ppermute | solution.py:29
  22.8 0.7 %shard_map.51 = f32[6,4,8,16]{3,2,1,0:T(8,128)} custom-call(f32[3,8,128]{2,1,0:T(8,128)S(1)} %add.3.refs_0_, f32[3,8,128]{2,1,0:T(8,128)S(1)} %collective-permute-done.9.refs_1_, f32[3,8,128]{2,1,0:T(8,128)S(1)} %collective-permute-done.10.refs_2_, f32[3,8,128]{2,1,0:T(8,128)S(1)} %collective-permute-done.11.refs_3_), custom_call_target="tpu_custom_call" | custom-call | tf_op jit(solution)/shard_map/pallas_call | solution.py:267
  (15 shorter events, 0.2 us)
Async XLA Ops:
  0.0 9.7 %copy-start.2 = (bf16[6,4,8,96]{3,2,1,0:T(8,128)(2,1)S(1)}, bf16[6,4,8,96]{3,2,1,0:T(8,128)(2,1)}, u32[]{:S(2)}) copy-start(bf16[6,4,8,96]{3,2,1,0:T(8,128)(2,1)} %param.5) | copy-start | bytes 110596
  0.0 9.1 %collective-permute-start.3 = (bf16[1,6,4,8,96]{4,3,2,1,0:T(8,128)(2,1)}, bf16[1,6,4,8,96]{4,3,2,1,0:T(8,128)(2,1)S(1)}, u32[]{:S(2)}, u32[]{:S(2)}) collective-permute-start(bf16[1,6,4,8,96]{4,3,2,1,0:T(8,128)(2,1)} %bitcast.2), channel_id=1, source_target_pairs={{0,4},{1,5},{2,6},{3,7},{4,0},{5,1},{6,2},{7,3},{8,12},{9,13},{10,... | collective-permute-start | bytes 110600 | tf_op jit(solution)/shard_map/ppermute | solution.py:65
  4.0 9.2 %collective-permute-start.2 = (bf16[1,96,768]{2,1,0:T(8,128)(2,1)}, bf16[1,96,768]{2,1,0:T(8,128)(2,1)S(1)}, u32[]{:S(2)}, u32[]{:S(2)}) collective-permute-start(bf16[1,96,768]{2,1,0:T(8,128)(2,1)} %refs_0_.3), channel_id=1, source_target_pairs={{0,24},{8,16},{16,8},{24,0},{1,25},{9,17},{17,9},{25,1},{2,26},{10... | collective-permute-start | bytes 442376 | tf_op jit(solution)/shard_map/ppermute | solution.py:25
  6.5 7.1 %collective-permute-start.1 = (bf16[1,96,768]{2,1,0:T(8,128)(2,1)}, bf16[1,96,768]{2,1,0:T(8,128)(2,1)S(1)}, u32[]{:S(2)}, u32[]{:S(2)}) collective-permute-start(bf16[1,96,768]{2,1,0:T(8,128)(2,1)} %refs_0_.3), channel_id=1, source_target_pairs={{0,16},{8,24},{16,0},{24,8},{1,17},{9,25},{17,1},{25,9},{2,18},{10... | collective-permute-start | bytes 442376 | tf_op jit(solution)/shard_map/ppermute | solution.py:25
  7.0 6.7 %collective-permute-start = (bf16[1,96,768]{2,1,0:T(8,128)(2,1)}, bf16[1,96,768]{2,1,0:T(8,128)(2,1)S(1)}, u32[]{:S(2)}, u32[]{:S(2)}) collective-permute-start(bf16[1,96,768]{2,1,0:T(8,128)(2,1)} %refs_0_.3), channel_id=1, source_target_pairs={{0,8},{8,0},{16,24},{24,16},{1,9},{9,1},{17,25},{25,17},{2,10},{10... | collective-permute-start | bytes 442376 | tf_op jit(solution)/shard_map/ppermute | solution.py:25
  7.5 4.3 %collective-permute-start.4 = (bf16[1,6,4,8,96]{4,3,2,1,0:T(8,128)(2,1)}, bf16[1,6,4,8,96]{4,3,2,1,0:T(8,128)(2,1)S(1)}, u32[]{:S(2)}, u32[]{:S(2)}) collective-permute-start(bf16[1,6,4,8,96]{4,3,2,1,0:T(8,128)(2,1)} %bitcast.3), channel_id=1, source_target_pairs={{0,2},{1,3},{2,0},{3,1},{4,6},{5,7},{6,4},{7,5},{8,10},{9,11},{10,... | collective-permute-start | bytes 110600 | tf_op jit(solution)/shard_map/ppermute | solution.py:65
  9.1 2.7 %copy-start.1 = (bf16[6,4,16,96]{3,2,1,0:T(8,128)(2,1)S(1)}, bf16[6,4,16,96]{3,2,1,0:T(8,128)(2,1)}, u32[]{:S(2)}) copy-start(bf16[6,4,16,96]{3,2,1,0:T(8,128)(2,1)} %refs_3_.1) | copy-start | bytes 221188
  9.1 2.7 %copy-start.3 = (s32[6,4]{0,1:T(4,128)S(1)}, s32[6,4]{0,1:T(4,128)}, u32[]{:S(2)}) copy-start(s32[6,4]{0,1:T(4,128)} %param.7) | copy-start | bytes 292
  9.2 4.5 %copy-start = (bf16[1,96,768]{2,1,0:T(8,128)(2,1)S(1)}, bf16[1,96,768]{2,1,0:T(8,128)(2,1)}, u32[]{:S(2)}) copy-start(bf16[1,96,768]{2,1,0:T(8,128)(2,1)} %refs_0_.3) | copy-start | bytes 442372
  9.2 4.0 %collective-permute-start.6 = (bf16[1,48,384]{2,1,0:T(8,128)(2,1)S(1)}, bf16[1,48,384]{2,1,0:T(8,128)(2,1)S(1)}, u32[]{:S(2)}, u32[]{:S(2)}) collective-permute-start(bf16[1,48,384]{2,1,0:T(8,128)(2,1)S(1)} %shard_map.47.refs_1_), channel_id=1, source_target_pairs={{0,2},{1,3},{2,0},{3,1},{4,6},{5,7},{6,4},{7,5},{8,10},{9,11},{10,... | collective-permute-start | bytes 110600 | tf_op jit(solution)/shard_map/ppermute | solution.py:65
  12.5 1.9 %collective-permute-start.5 = (bf16[3,48,384]{2,1,0:T(8,128)(2,1)S(1)}, bf16[3,48,384]{2,1,0:T(8,128)(2,1)S(1)}, u32[]{:S(2)}, u32[]{:S(2)}) collective-permute-start(bf16[3,48,384]{2,1,0:T(8,128)(2,1)S(1)} %get-tuple-element.7.refs_4_), channel_id=1, source_target_pairs={{0,1},{1,0},{2,3},{3,2},{4,5},{5,4},{6,7},{7,6},{8,9},{9,8},{10,11... | collective-permute-start | bytes 331784 | tf_op jit(solution)/shard_map/ppermute | solution.py:77
  13.2 1.2 %collective-permute-start.7 = (bf16[1,48,384]{2,1,0:T(8,128)(2,1)S(1)}, bf16[1,48,384]{2,1,0:T(8,128)(2,1)S(1)}, u32[]{:S(2)}, u32[]{:S(2)}) collective-permute-start(bf16[1,48,384]{2,1,0:T(8,128)(2,1)S(1)} %collective-permute-done.6.refs_5_), channel_id=1, source_target_pairs={{0,1},{1,0},{2,3},{3,2},{4,5},{5,4},{6,7},{7,6},{8,9},{9,8},{10,11... | collective-permute-start | bytes 110600 | tf_op jit(solution)/shard_map/ppermute | solution.py:77
  15.1 1.2 %collective-permute-start.8 = (f32[3,8,128]{2,1,0:T(8,128)S(1)}, f32[3,8,128]{2,1,0:T(8,128)S(1)}, u32[]{:S(2)}, u32[]{:S(2)}) collective-permute-start(f32[3,8,128]{2,1,0:T(8,128)S(1)} %shard_map.50), channel_id=1, source_target_pairs={{0,1},{1,0},{2,3},{3,2},{4,5},{5,4},{6,7},{7,6},{8,9},{9,8},{10,11... | collective-permute-start | bytes 36872 | tf_op jit(solution)/shard_map/ppermute | solution.py:77
  16.3 5.5 %collective-permute-start.11 = (f32[3,8,128]{2,1,0:T(8,128)S(1)}, f32[3,8,128]{2,1,0:T(8,128)S(1)}, u32[]{:S(2)}, u32[]{:S(2)}) collective-permute-start(f32[3,8,128]{2,1,0:T(8,128)S(1)} %add.3.refs_0_), channel_id=1, source_target_pairs={{0,6},{1,7},{2,4},{3,5},{4,2},{5,3},{6,0},{7,1},{8,14},{9,15},{10,... | collective-permute-start | bytes 36872 | tf_op jit(solution)/shard_map/ppermute | solution.py:29
  17.9 4.6 %collective-permute-start.10 = (f32[3,8,128]{2,1,0:T(8,128)S(1)}, f32[3,8,128]{2,1,0:T(8,128)S(1)}, u32[]{:S(2)}, u32[]{:S(2)}) collective-permute-start(f32[3,8,128]{2,1,0:T(8,128)S(1)} %add.3.refs_0_), channel_id=1, source_target_pairs={{0,4},{1,5},{2,6},{3,7},{4,0},{5,1},{6,2},{7,3},{8,12},{9,13},{10,... | collective-permute-start | bytes 36872 | tf_op jit(solution)/shard_map/ppermute | solution.py:29
  19.1 3.7 %collective-permute-start.9 = (f32[3,8,128]{2,1,0:T(8,128)S(1)}, f32[3,8,128]{2,1,0:T(8,128)S(1)}, u32[]{:S(2)}, u32[]{:S(2)}) collective-permute-start(f32[3,8,128]{2,1,0:T(8,128)S(1)} %add.3.refs_0_), channel_id=1, source_target_pairs={{0,2},{1,3},{2,0},{3,1},{4,6},{5,7},{6,4},{7,5},{8,10},{9,11},{10,... | collective-permute-start | bytes 36872 | tf_op jit(solution)/shard_map/ppermute | solution.py:29

commit v5 on v4

--- a/solution.py
+++ b/solution.py
@@ -71,6 +71,10 @@
         digit = lax.rem(lax.div(z, stride), size)
         z = z + (lax.rem(digit + s, size) - digit) * stride
     return z
+
+
+def chip_order(nz):
+    return [2, 1] + list(range(3, nz)) if nz > 2 else list(range(1, nz))
 
 
 def send_core(x, nz):
@@ -262,12 +266,14 @@
         scratch_shapes=join_scratch,
         compiler_params=params,
     )(*w_parts, *other, near, prepared)
-    chip_value = partial_value + send_core(partial_value, nz)
-    shares = [chip_value] + [send_chip(chip_value, s, nz) for s in range(1, nz)]
+    core_value = partial_value
+    for s in chip_order(nz):
+        core_value = core_value + send_chip(partial_value, s, nz)
+    shares = [core_value, send_core(core_value, nz)]
     return pl.pallas_call(
-        functools.partial(place_kernel, nz),
+        functools.partial(place_kernel, CORES),
         out_shape=jax.ShapeDtypeStruct((nk, nq, nc, nv), jnp.float32),
-        in_specs=[vmem] * nz,
+        in_specs=[vmem] * CORES,
         out_specs=vmem,
         compiler_params=params,
     )(*shares)

time: 23.7 us -> 23.4 us (0.987)
    ppermute x3, waiting for transfers between devices: 2.08 us -> 1.8 us  [send_chip(): lax.ppermute(x, 'ga', [(i * CORES + c, partner(i, s, nz) * CORES + c) for...]
  transfers between devices with their start and end apart: 12 -> 12, of which waited for: 9 -> 8; matrix products, arithmetic and copies ran while one was open for 0% -> 0% of each run, Pallas kernels for 6% -> 6%
where the time goes in v5:
time: 23.4 us; the launch traced here: 23.2 us
  starting transfers between devices  14.1 us (60%)
  waiting for transfers between devices  6.31 us (27%)
  Pallas kernels  2.73 us (12%)
    ppermute x3, starting transfers between devices, gather_chips(): groups.append((moved, lax.ppermute(array, 'ga', pairs)))  6.13 us
    ppermute x3, starting transfers between devices, send_chip(): lax.ppermute(x, 'ga', [(i * CORES + c, partner(i, s, nz) * CORES + c) for...  4.42 us
    ppermute x3, starting transfers between devices, send_pb(): return lax.ppermute(x, 'pb', [(i, partner(i, s, npb)) for i in range(npb)])  3.49 us
    ppermute x3, waiting for transfers between devices, gather_chips(): groups.append((moved, lax.ppermute(array, 'ga', pairs)))  2.62 us
    ppermute x3, waiting for transfers between devices, send_chip(): lax.ppermute(x, 'ga', [(i * CORES + c, partner(i, s, nz) * CORES + c) for...  1.8 us
    ppermute x3, waiting for transfers between devices, send_core(): lax.ppermute(x, 'ga', [(i * CORES + c, i * CORES + 1 - c) for i in range(...  1.46 us
    pallas_call x1, Pallas kernels, per_device(): pl.pallas_call(functools.partial(place_kernel, CORES), out_shape=jax.Shap...  0.73 us
    pallas_call x1, Pallas kernels, per_device(): pl.pallas_call(functools.partial(prepare_kernel, npb), out_shape=(jax.Sha...  0.7 us
  transfers between devices with their start and end apart: 12, of which 8 were waited for; matrix products, arithmetic and copies ran while one was open for 0% of the time, Pallas kernels for 6%

profile of v5, /device:TPU:0, one launch (start us, length us, event | category | flops | bytes accessed | tf_op | source)
XLA Modules:
  0.0 23.2 jit_solution(5720700357290448725)
XLA Ops:
  0.0 4.0 %collective-permute-start.3 = (bf16[1,6,4,8,96]{4,3,2,1,0:T(8,128)(2,1)}, bf16[1,6,4,8,96]{4,3,2,1,0:T(8,128)(2,1)S(1)}, u32[]{:S(2)}, u32[]{:S(2)}) collective-permute-start(bf16[1,6,4,8,96]{4,3,2,1,0:T(8,128)(2,1)} %bitcast.2), channel_id=1, source_target_pairs={{0,4},{1,5},{2,6},{3,7},{4,0},{5,1},{6,2},{7,3},{8,12},{9,13},{10,... | collective-permute-start | bytes 110600 | tf_op jit(solution)/shard_map/ppermute | solution.py:65
  4.0 2.4 %collective-permute-start.2 = (bf16[1,96,768]{2,1,0:T(8,128)(2,1)}, bf16[1,96,768]{2,1,0:T(8,128)(2,1)S(1)}, u32[]{:S(2)}, u32[]{:S(2)}) collective-permute-start(bf16[1,96,768]{2,1,0:T(8,128)(2,1)} %refs_0_.3), channel_id=1, source_target_pairs={{0,24},{8,16},{16,8},{24,0},{1,25},{9,17},{17,9},{25,1},{2,26},{10... | collective-permute-start | bytes 442376 | tf_op jit(solution)/shard_map/ppermute | solution.py:25
  6.5 0.5 %collective-permute-start.1 = (bf16[1,96,768]{2,1,0:T(8,128)(2,1)}, bf16[1,96,768]{2,1,0:T(8,128)(2,1)S(1)}, u32[]{:S(2)}, u32[]{:S(2)}) collective-permute-start(bf16[1,96,768]{2,1,0:T(8,128)(2,1)} %refs_0_.3), channel_id=1, source_target_pairs={{0,16},{8,24},{16,0},{24,8},{1,17},{9,25},{17,1},{25,9},{2,18},{10... | collective-permute-start | bytes 442376 | tf_op jit(solution)/shard_map/ppermute | solution.py:25
  7.0 0.5 %collective-permute-start = (bf16[1,96,768]{2,1,0:T(8,128)(2,1)}, bf16[1,96,768]{2,1,0:T(8,128)(2,1)S(1)}, u32[]{:S(2)}, u32[]{:S(2)}) collective-permute-start(bf16[1,96,768]{2,1,0:T(8,128)(2,1)} %refs_0_.3), channel_id=1, source_target_pairs={{0,8},{8,0},{16,24},{24,16},{1,9},{9,1},{17,25},{25,17},{2,10},{10... | collective-permute-start | bytes 442376 | tf_op jit(solution)/shard_map/ppermute | solution.py:25
  7.5 1.6 %collective-permute-start.4 = (bf16[1,6,4,8,96]{4,3,2,1,0:T(8,128)(2,1)}, bf16[1,6,4,8,96]{4,3,2,1,0:T(8,128)(2,1)S(1)}, u32[]{:S(2)}, u32[]{:S(2)}) collective-permute-start(bf16[1,6,4,8,96]{4,3,2,1,0:T(8,128)(2,1)} %bitcast.3), channel_id=1, source_target_pairs={{0,2},{1,3},{2,0},{3,1},{4,6},{5,7},{6,4},{7,5},{8,10},{9,11},{10,... | collective-permute-start | bytes 110600 | tf_op jit(solution)/shard_map/ppermute | solution.py:65
  9.1 0.1 shard_map.47.refs_1_
  9.2 0.0 copy-start
  9.2 0.5 %collective-permute-start.6 = (bf16[1,48,384]{2,1,0:T(8,128)(2,1)S(1)}, bf16[1,48,384]{2,1,0:T(8,128)(2,1)S(1)}, u32[]{:S(2)}, u32[]{:S(2)}) collective-permute-start(bf16[1,48,384]{2,1,0:T(8,128)(2,1)S(1)} %shard_map.47.refs_1_), channel_id=1, source_target_pairs={{0,2},{1,3},{2,0},{3,1},{4,6},{5,7},{6,4},{7,5},{8,10},{9,11},{10,... | collective-permute-start | bytes 110600 | tf_op jit(solution)/shard_map/ppermute | solution.py:65
  9.7 0.1 shard_map.46.refs_0_
  9.8 2.0 %collective-permute-done.4.refs_2_ = bf16[1,6,4,8,96]{4,3,2,1,0:T(8,128)(2,1)S(1)} collective-permute-done((bf16[1,6,4,8,96]{4,3,2,1,0:T(8,128)(2,1)}, bf16[1,6,4,8,96]{4,3,2,1,0:T(8,128)(2,1)S(1)}, u32[]{:S(2)}, u32[]{:S(2)}) %collective-permute-start.4) | collective-permute-done | bytes 36896 | tf_op jit(solution)/shard_map/ppermute | solution.py:65
  11.8 0.7 %shard_map.48 = (bf16[3,48,384]{2,1,0:T(8,128)(2,1)S(1)}, bf16[3,128,512]{2,1,0:T(8,128)(2,1)S(1)}) custom-call(bf16[1,48,384]{2,1,0:T(8,128)(2,1)S(1)} %shard_map.46.refs_0_, bf16[1,48,384]{2,1,0:T(8,128)(2,1)S(1)} %shard_map.47.refs_1_, bf16[1,6,4,8,96]{4,3,2,1,0:T(8,128)(2,1)S(1)} %collective-permute-done.4.refs_2_, bf16[6,4,16,96]{3,2,1,0:T(8,128)(2,1)S(1)} %copy-done.1, ...), custom_call_target="tpu_custom_call" | custom-call | tf_op jit(solution)/shard_map/pallas_call | solution.py:238
  12.5 0.1 collective-permute-start.5
  12.6 0.6 %collective-permute-done.6.refs_5_ = bf16[1,48,384]{2,1,0:T(8,128)(2,1)S(1)} collective-permute-done((bf16[1,48,384]{2,1,0:T(8,128)(2,1)S(1)}, bf16[1,48,384]{2,1,0:T(8,128)(2,1)S(1)}, u32[]{:S(2)}, u32[]{:S(2)}) %collective-permute-start.6) | collective-permute-done | bytes 36896 | tf_op jit(solution)/shard_map/ppermute | solution.py:65
  13.2 0.4 %collective-permute-done.1.refs_2_ = bf16[1,96,768]{2,1,0:T(8,128)(2,1)S(1)} collective-permute-done((bf16[1,96,768]{2,1,0:T(8,128)(2,1)}, bf16[1,96,768]{2,1,0:T(8,128)(2,1)S(1)}, u32[]{:S(2)}, u32[]{:S(2)}) %collective-permute-start.1) | collective-permute-done | bytes 147488 | tf_op jit(solution)/shard_map/ppermute | solution.py:25
  13.6 0.1 collective-permute-done.refs_1_
  13.7 0.5 %shard_map.49.refs_6_ = f32[4,48,96]{2,1,0:T(8,128)S(1)} custom-call(bf16[1,96,768]{2,1,0:T(8,128)(2,1)S(1)} %copy-done, bf16[1,96,768]{2,1,0:T(8,128)(2,1)S(1)} %collective-permute-done.refs_1_, bf16[1,96,768]{2,1,0:T(8,128)(2,1)S(1)} %collective-permute-done.1.refs_2_, bf16[1,96,768]{2,1,0:T(8,128)(2,1)S(1)} %collective-permute-done.2.refs_3_, ...), custom_call_target="tpu_custom_call" | custom-call | flops 1000000000 | bytes 3000000 | tf_op jit(solution)/shard_map/pallas_call | solution.py:250
  14.2 0.3 %collective-permute-done.7.refs_5_ = bf16[1,48,384]{2,1,0:T(8,128)(2,1)S(1)} collective-permute-done((bf16[1,48,384]{2,1,0:T(8,128)(2,1)S(1)}, bf16[1,48,384]{2,1,0:T(8,128)(2,1)S(1)}, u32[]{:S(2)}, u32[]{:S(2)}) %collective-permute-start.7) | collective-permute-done | bytes 36896 | tf_op jit(solution)/shard_map/ppermute | solution.py:81
  14.5 0.6 %shard_map.50 = f32[3,8,128]{2,1,0:T(8,128)S(1)} custom-call(bf16[1,96,768]{2,1,0:T(8,128)(2,1)S(1)} %copy-done, bf16[1,96,768]{2,1,0:T(8,128)(2,1)S(1)} %collective-permute-done.refs_1_, bf16[1,96,768]{2,1,0:T(8,128)(2,1)S(1)} %collective-permute-done.1.refs_2_, bf16[1,96,768]{2,1,0:T(8,128)(2,1)S(1)} %collective-permute-done.2.refs_3_, ...), custom_call_target="tpu_custom_call" | custom-call | tf_op jit(solution)/shard_map/pallas_call | solution.py:261
  15.1 1.6 %collective-permute-start.10 = (f32[3,8,128]{2,1,0:T(8,128)S(1)}, f32[3,8,128]{2,1,0:T(8,128)S(1)}, u32[]{:S(2)}, u32[]{:S(2)}) collective-permute-start(f32[3,8,128]{2,1,0:T(8,128)S(1)} %shard_map.50), channel_id=1, source_target_pairs={{0,6},{1,7},{2,4},{3,5},{4,2},{5,3},{6,0},{7,1},{8,14},{9,15},{10,... | collective-permute-start | bytes 36872 | tf_op jit(solution)/shard_map/ppermute | solution.py:29
  16.7 2.8 %collective-permute-start.8 = (f32[3,8,128]{2,1,0:T(8,128)S(1)}, f32[3,8,128]{2,1,0:T(8,128)S(1)}, u32[]{:S(2)}, u32[]{:S(2)}) collective-permute-start(f32[3,8,128]{2,1,0:T(8,128)S(1)} %shard_map.50), channel_id=1, source_target_pairs={{0,4},{1,5},{2,6},{3,7},{4,0},{5,1},{6,2},{7,3},{8,12},{9,13},{10,... | collective-permute-start | bytes 36872 | tf_op jit(solution)/shard_map/ppermute | solution.py:29
  19.5 1.1 %collective-permute-done.10 = f32[3,8,128]{2,1,0:T(8,128)S(1)} collective-permute-done((f32[3,8,128]{2,1,0:T(8,128)S(1)}, f32[3,8,128]{2,1,0:T(8,128)S(1)}, u32[]{:S(2)}, u32[]{:S(2)}) %collective-permute-start.10) | collective-permute-done | bytes 12320 | tf_op jit(solution)/shard_map/ppermute | solution.py:29
  20.6 0.7 %collective-permute-done.8 = f32[3,8,128]{2,1,0:T(8,128)S(1)} collective-permute-done((f32[3,8,128]{2,1,0:T(8,128)S(1)}, f32[3,8,128]{2,1,0:T(8,128)S(1)}, u32[]{:S(2)}, u32[]{:S(2)}) %collective-permute-start.8) | collective-permute-done | bytes 12320 | tf_op jit(solution)/shard_map/ppermute | solution.py:29
  21.3 1.2 %collective-permute-done.11.refs_1_ = f32[3,8,128]{2,1,0:T(8,128)S(1)} collective-permute-done((f32[3,8,128]{2,1,0:T(8,128)S(1)}, f32[3,8,128]{2,1,0:T(8,128)S(1)}, u32[]{:S(2)}, u32[]{:S(2)}) %collective-permute-start.11) | collective-permute-done | bytes 12320 | tf_op jit(solution)/shard_map/ppermute | solution.py:81
  22.5 0.7 %shard_map.51 = f32[6,4,8,16]{3,2,1,0:T(8,128)} custom-call(f32[3,8,128]{2,1,0:T(8,128)S(1)} %add_add_fusion.refs_0_, f32[3,8,128]{2,1,0:T(8,128)S(1)} %collective-permute-done.11.refs_1_), custom_call_target="tpu_custom_call" | custom-call | tf_op jit(solution)/shard_map/pallas_call | solution.py:273
  (15 shorter events, 0.0 us)
Async XLA Ops:
  0.0 9.7 %copy-start.2 = (bf16[6,4,8,96]{3,2,1,0:T(8,128)(2,1)S(1)}, bf16[6,4,8,96]{3,2,1,0:T(8,128)(2,1)}, u32[]{:S(2)}) copy-start(bf16[6,4,8,96]{3,2,1,0:T(8,128)(2,1)} %param.5) | copy-start | bytes 110596
  0.0 9.1 %collective-permute-start.3 = (bf16[1,6,4,8,96]{4,3,2,1,0:T(8,128)(2,1)}, bf16[1,6,4,8,96]{4,3,2,1,0:T(8,128)(2,1)S(1)}, u32[]{:S(2)}, u32[]{:S(2)}) collective-permute-start(bf16[1,6,4,8,96]{4,3,2,1,0:T(8,128)(2,1)} %bitcast.2), channel_id=1, source_target_pairs={{0,4},{1,5},{2,6},{3,7},{4,0},{5,1},{6,2},{7,3},{8,12},{9,13},{10,... | collective-permute-start | bytes 110600 | tf_op jit(solution)/shard_map/ppermute | solution.py:65
  4.0 9.2 %collective-permute-start.2 = (bf16[1,96,768]{2,1,0:T(8,128)(2,1)}, bf16[1,96,768]{2,1,0:T(8,128)(2,1)S(1)}, u32[]{:S(2)}, u32[]{:S(2)}) collective-permute-start(bf16[1,96,768]{2,1,0:T(8,128)(2,1)} %refs_0_.3), channel_id=1, source_target_pairs={{0,24},{8,16},{16,8},{24,0},{1,25},{9,17},{17,9},{25,1},{2,26},{10... | collective-permute-start | bytes 442376 | tf_op jit(solution)/shard_map/ppermute | solution.py:25
  6.5 7.1 %collective-permute-start.1 = (bf16[1,96,768]{2,1,0:T(8,128)(2,1)}, bf16[1,96,768]{2,1,0:T(8,128)(2,1)S(1)}, u32[]{:S(2)}, u32[]{:S(2)}) collective-permute-start(bf16[1,96,768]{2,1,0:T(8,128)(2,1)} %refs_0_.3), channel_id=1, source_target_pairs={{0,16},{8,24},{16,0},{24,8},{1,17},{9,25},{17,1},{25,9},{2,18},{10... | collective-permute-start | bytes 442376 | tf_op jit(solution)/shard_map/ppermute | solution.py:25
  7.0 6.7 %collective-permute-start = (bf16[1,96,768]{2,1,0:T(8,128)(2,1)}, bf16[1,96,768]{2,1,0:T(8,128)(2,1)S(1)}, u32[]{:S(2)}, u32[]{:S(2)}) collective-permute-start(bf16[1,96,768]{2,1,0:T(8,128)(2,1)} %refs_0_.3), channel_id=1, source_target_pairs={{0,8},{8,0},{16,24},{24,16},{1,9},{9,1},{17,25},{25,17},{2,10},{10... | collective-permute-start | bytes 442376 | tf_op jit(solution)/shard_map/ppermute | solution.py:25
  7.5 4.3 %collective-permute-start.4 = (bf16[1,6,4,8,96]{4,3,2,1,0:T(8,128)(2,1)}, bf16[1,6,4,8,96]{4,3,2,1,0:T(8,128)(2,1)S(1)}, u32[]{:S(2)}, u32[]{:S(2)}) collective-permute-start(bf16[1,6,4,8,96]{4,3,2,1,0:T(8,128)(2,1)} %bitcast.3), channel_id=1, source_target_pairs={{0,2},{1,3},{2,0},{3,1},{4,6},{5,7},{6,4},{7,5},{8,10},{9,11},{10,... | collective-permute-start | bytes 110600 | tf_op jit(solution)/shard_map/ppermute | solution.py:65
  9.1 2.7 %copy-start.1 = (bf16[6,4,16,96]{3,2,1,0:T(8,128)(2,1)S(1)}, bf16[6,4,16,96]{3,2,1,0:T(8,128)(2,1)}, u32[]{:S(2)}) copy-start(bf16[6,4,16,96]{3,2,1,0:T(8,128)(2,1)} %refs_3_.1) | copy-start | bytes 221188
  9.1 2.7 %copy-start.3 = (s32[6,4]{0,1:T(4,128)S(1)}, s32[6,4]{0,1:T(4,128)}, u32[]{:S(2)}) copy-start(s32[6,4]{0,1:T(4,128)} %param.7) | copy-start | bytes 292
  9.2 4.5 %copy-start = (bf16[1,96,768]{2,1,0:T(8,128)(2,1)S(1)}, bf16[1,96,768]{2,1,0:T(8,128)(2,1)}, u32[]{:S(2)}) copy-start(bf16[1,96,768]{2,1,0:T(8,128)(2,1)} %refs_0_.3) | copy-start | bytes 442372
  9.2 4.0 %collective-permute-start.6 = (bf16[1,48,384]{2,1,0:T(8,128)(2,1)S(1)}, bf16[1,48,384]{2,1,0:T(8,128)(2,1)S(1)}, u32[]{:S(2)}, u32[]{:S(2)}) collective-permute-start(bf16[1,48,384]{2,1,0:T(8,128)(2,1)S(1)} %shard_map.47.refs_1_), channel_id=1, source_target_pairs={{0,2},{1,3},{2,0},{3,1},{4,6},{5,7},{6,4},{7,5},{8,10},{9,11},{10,... | collective-permute-start | bytes 110600 | tf_op jit(solution)/shard_map/ppermute | solution.py:65
  12.5 1.9 %collective-permute-start.5 = (bf16[3,48,384]{2,1,0:T(8,128)(2,1)S(1)}, bf16[3,48,384]{2,1,0:T(8,128)(2,1)S(1)}, u32[]{:S(2)}, u32[]{:S(2)}) collective-permute-start(bf16[3,48,384]{2,1,0:T(8,128)(2,1)S(1)} %get-tuple-element.7.refs_4_), channel_id=1, source_target_pairs={{0,1},{1,0},{2,3},{3,2},{4,5},{5,4},{6,7},{7,6},{8,9},{9,8},{10,11... | collective-permute-start | bytes 331784 | tf_op jit(solution)/shard_map/ppermute | solution.py:81
  13.2 1.2 %collective-permute-start.7 = (bf16[1,48,384]{2,1,0:T(8,128)(2,1)S(1)}, bf16[1,48,384]{2,1,0:T(8,128)(2,1)S(1)}, u32[]{:S(2)}, u32[]{:S(2)}) collective-permute-start(bf16[1,48,384]{2,1,0:T(8,128)(2,1)S(1)} %collective-permute-done.6.refs_5_), channel_id=1, source_target_pairs={{0,1},{1,0},{2,3},{3,2},{4,5},{5,4},{6,7},{7,6},{8,9},{9,8},{10,11... | collective-permute-start | bytes 110600 | tf_op jit(solution)/shard_map/ppermute | solution.py:81
  15.1 5.5 %collective-permute-start.10 = (f32[3,8,128]{2,1,0:T(8,128)S(1)}, f32[3,8,128]{2,1,0:T(8,128)S(1)}, u32[]{:S(2)}, u32[]{:S(2)}) collective-permute-start(f32[3,8,128]{2,1,0:T(8,128)S(1)} %shard_map.50), channel_id=1, source_target_pairs={{0,6},{1,7},{2,4},{3,5},{4,2},{5,3},{6,0},{7,1},{8,14},{9,15},{10,... | collective-permute-start | bytes 36872 | tf_op jit(solution)/shard_map/ppermute | solution.py:29
  16.7 3.9 %collective-permute-start.9 = (f32[3,8,128]{2,1,0:T(8,128)S(1)}, f32[3,8,128]{2,1,0:T(8,128)S(1)}, u32[]{:S(2)}, u32[]{:S(2)}) collective-permute-start(f32[3,8,128]{2,1,0:T(8,128)S(1)} %shard_map.50), channel_id=1, source_target_pairs={{0,2},{1,3},{2,0},{3,1},{4,6},{5,7},{6,4},{7,5},{8,10},{9,11},{10,... | collective-permute-start | bytes 36872 | tf_op jit(solution)/shard_map/ppermute | solution.py:29
  16.7 4.6 %collective-permute-start.8 = (f32[3,8,128]{2,1,0:T(8,128)S(1)}, f32[3,8,128]{2,1,0:T(8,128)S(1)}, u32[]{:S(2)}, u32[]{:S(2)}) collective-permute-start(f32[3,8,128]{2,1,0:T(8,128)S(1)} %shard_map.50), channel_id=1, source_target_pairs={{0,4},{1,5},{2,6},{3,7},{4,0},{5,1},{6,2},{7,3},{8,12},{9,13},{10,... | collective-permute-start | bytes 36872 | tf_op jit(solution)/shard_map/ppermute | solution.py:29
  21.3 1.2 %collective-permute-start.11 = (f32[3,8,128]{2,1,0:T(8,128)S(1)}, f32[3,8,128]{2,1,0:T(8,128)S(1)}, u32[]{:S(2)}, u32[]{:S(2)}) collective-permute-start(f32[3,8,128]{2,1,0:T(8,128)S(1)} %add_add_fusion.refs_0_), channel_id=1, source_target_pairs={{0,1},{1,0},{2,3},{3,2},{4,5},{5,4},{6,7},{7,6},{8,9},{9,8},{10,11... | collective-permute-start | bytes 36872 | tf_op jit(solution)/shard_map/ppermute | solution.py:81

commit v6 on v4

--- a/solution.py
+++ b/solution.py
@@ -71,6 +71,10 @@
         digit = lax.rem(lax.div(z, stride), size)
         z = z + (lax.rem(digit + s, size) - digit) * stride
     return z
+
+
+def chip_order(nz):
+    return [2, 1] + list(range(3, nz)) if nz > 2 else list(range(1, nz))
 
 
 def send_core(x, nz):
@@ -263,7 +267,7 @@
         compiler_params=params,
     )(*w_parts, *other, near, prepared)
     chip_value = partial_value + send_core(partial_value, nz)
-    shares = [chip_value] + [send_chip(chip_value, s, nz) for s in range(1, nz)]
+    shares = [chip_value] + [send_chip(chip_value, s, nz) for s in chip_order(nz)]
     return pl.pallas_call(
         functools.partial(place_kernel, nz),
         out_shape=jax.ShapeDtypeStruct((nk, nq, nc, nv), jnp.float32),

time: 23.7 us -> 23.4 us (0.987)
  waiting for transfers between devices: 6.43 us -> 6.15 us
    ppermute x3, waiting for transfers between devices: 2.08 us -> 1.8 us  [send_chip(): lax.ppermute(x, 'ga', [(i * CORES + c, partner(i, s, nz) * CORES + c) for...]
  transfers between devices with their start and end apart: 12 -> 12, of which waited for: 9 -> 8; matrix products, arithmetic and copies ran while one was open for 0% -> 0% of each run, Pallas kernels for 6% -> 6%
where the time goes in v6:
time: 23.4 us; the launch traced here: 23.2 us
  starting transfers between devices  14.3 us (61%)
  waiting for transfers between devices  6.15 us (26%)
  Pallas kernels  2.74 us (12%)
    ppermute x3, starting transfers between devices, gather_chips(): groups.append((moved, lax.ppermute(array, 'ga', pairs)))  6.13 us
    ppermute x3, starting transfers between devices, send_chip(): lax.ppermute(x, 'ga', [(i * CORES + c, partner(i, s, nz) * CORES + c) for...  4.39 us
    ppermute x3, starting transfers between devices, send_pb(): return lax.ppermute(x, 'pb', [(i, partner(i, s, npb)) for i in range(npb)])  3.49 us
    ppermute x3, waiting for transfers between devices, gather_chips(): groups.append((moved, lax.ppermute(array, 'ga', pairs)))  2.62 us
    ppermute x3, waiting for transfers between devices, send_chip(): lax.ppermute(x, 'ga', [(i * CORES + c, partner(i, s, nz) * CORES + c) for...  1.8 us
    ppermute x3, waiting for transfers between devices, send_core(): lax.ppermute(x, 'ga', [(i * CORES + c, i * CORES + 1 - c) for i in range(...  1.3 us
    pallas_call x1, Pallas kernels, per_device(): pl.pallas_call(functools.partial(place_kernel, nz), out_shape=jax.ShapeDt...  0.73 us
    pallas_call x1, Pallas kernels, per_device(): pl.pallas_call(functools.partial(prepare_kernel, npb), out_shape=(jax.Sha...  0.7 us
  transfers between devices with their start and end apart: 12, of which 8 were waited for; matrix products, arithmetic and copies ran while one was open for 0% of the time, Pallas kernels for 6%

profile of v6, /device:TPU:0, one launch (start us, length us, event | category | flops | bytes accessed | tf_op | source)
XLA Modules:
  0.0 23.2 jit_solution(7588915514289483462)
XLA Ops:
  0.0 4.0 %collective-permute-start.3 = (bf16[1,6,4,8,96]{4,3,2,1,0:T(8,128)(2,1)}, bf16[1,6,4,8,96]{4,3,2,1,0:T(8,128)(2,1)S(1)}, u32[]{:S(2)}, u32[]{:S(2)}) collective-permute-start(bf16[1,6,4,8,96]{4,3,2,1,0:T(8,128)(2,1)} %bitcast.2), channel_id=1, source_target_pairs={{0,4},{1,5},{2,6},{3,7},{4,0},{5,1},{6,2},{7,3},{8,12},{9,13},{10,... | collective-permute-start | bytes 110600 | tf_op jit(solution)/shard_map/ppermute | solution.py:65
  4.0 2.4 %collective-permute-start.2 = (bf16[1,96,768]{2,1,0:T(8,128)(2,1)}, bf16[1,96,768]{2,1,0:T(8,128)(2,1)S(1)}, u32[]{:S(2)}, u32[]{:S(2)}) collective-permute-start(bf16[1,96,768]{2,1,0:T(8,128)(2,1)} %refs_0_.3), channel_id=1, source_target_pairs={{0,24},{8,16},{16,8},{24,0},{1,25},{9,17},{17,9},{25,1},{2,26},{10... | collective-permute-start | bytes 442376 | tf_op jit(solution)/shard_map/ppermute | solution.py:25
  6.5 0.5 %collective-permute-start.1 = (bf16[1,96,768]{2,1,0:T(8,128)(2,1)}, bf16[1,96,768]{2,1,0:T(8,128)(2,1)S(1)}, u32[]{:S(2)}, u32[]{:S(2)}) collective-permute-start(bf16[1,96,768]{2,1,0:T(8,128)(2,1)} %refs_0_.3), channel_id=1, source_target_pairs={{0,16},{8,24},{16,0},{24,8},{1,17},{9,25},{17,1},{25,9},{2,18},{10... | collective-permute-start | bytes 442376 | tf_op jit(solution)/shard_map/ppermute | solution.py:25
  7.0 0.5 %collective-permute-start = (bf16[1,96,768]{2,1,0:T(8,128)(2,1)}, bf16[1,96,768]{2,1,0:T(8,128)(2,1)S(1)}, u32[]{:S(2)}, u32[]{:S(2)}) collective-permute-start(bf16[1,96,768]{2,1,0:T(8,128)(2,1)} %refs_0_.3), channel_id=1, source_target_pairs={{0,8},{8,0},{16,24},{24,16},{1,9},{9,1},{17,25},{25,17},{2,10},{10... | collective-permute-start | bytes 442376 | tf_op jit(solution)/shard_map/ppermute | solution.py:25
  7.5 1.6 %collective-permute-start.4 = (bf16[1,6,4,8,96]{4,3,2,1,0:T(8,128)(2,1)}, bf16[1,6,4,8,96]{4,3,2,1,0:T(8,128)(2,1)S(1)}, u32[]{:S(2)}, u32[]{:S(2)}) collective-permute-start(bf16[1,6,4,8,96]{4,3,2,1,0:T(8,128)(2,1)} %bitcast.3), channel_id=1, source_target_pairs={{0,2},{1,3},{2,0},{3,1},{4,6},{5,7},{6,4},{7,5},{8,10},{9,11},{10,... | collective-permute-start | bytes 110600 | tf_op jit(solution)/shard_map/ppermute | solution.py:65
  9.1 0.1 shard_map.47.refs_1_
  9.2 0.5 %collective-permute-start.6 = (bf16[1,48,384]{2,1,0:T(8,128)(2,1)S(1)}, bf16[1,48,384]{2,1,0:T(8,128)(2,1)S(1)}, u32[]{:S(2)}, u32[]{:S(2)}) collective-permute-start(bf16[1,48,384]{2,1,0:T(8,128)(2,1)S(1)} %shard_map.47.refs_1_), channel_id=1, source_target_pairs={{0,2},{1,3},{2,0},{3,1},{4,6},{5,7},{6,4},{7,5},{8,10},{9,11},{10,... | collective-permute-start | bytes 110600 | tf_op jit(solution)/shard_map/ppermute | solution.py:65
  9.7 0.1 shard_map.46.refs_0_
  9.8 2.0 %collective-permute-done.4.refs_2_ = bf16[1,6,4,8,96]{4,3,2,1,0:T(8,128)(2,1)S(1)} collective-permute-done((bf16[1,6,4,8,96]{4,3,2,1,0:T(8,128)(2,1)}, bf16[1,6,4,8,96]{4,3,2,1,0:T(8,128)(2,1)S(1)}, u32[]{:S(2)}, u32[]{:S(2)}) %collective-permute-start.4) | collective-permute-done | bytes 36896 | tf_op jit(solution)/shard_map/ppermute | solution.py:65
  11.8 0.7 %shard_map.48 = (bf16[3,48,384]{2,1,0:T(8,128)(2,1)S(1)}, bf16[3,128,512]{2,1,0:T(8,128)(2,1)S(1)}) custom-call(bf16[1,48,384]{2,1,0:T(8,128)(2,1)S(1)} %shard_map.46.refs_0_, bf16[1,48,384]{2,1,0:T(8,128)(2,1)S(1)} %shard_map.47.refs_1_, bf16[1,6,4,8,96]{4,3,2,1,0:T(8,128)(2,1)S(1)} %collective-permute-done.4.refs_2_, bf16[6,4,16,96]{3,2,1,0:T(8,128)(2,1)S(1)} %copy-done.1, ...), custom_call_target="tpu_custom_call" | custom-call | tf_op jit(solution)/shard_map/pallas_call | solution.py:238
  12.5 0.1 collective-permute-start.5
  12.6 0.6 %collective-permute-done.6.refs_5_ = bf16[1,48,384]{2,1,0:T(8,128)(2,1)S(1)} collective-permute-done((bf16[1,48,384]{2,1,0:T(8,128)(2,1)S(1)}, bf16[1,48,384]{2,1,0:T(8,128)(2,1)S(1)}, u32[]{:S(2)}, u32[]{:S(2)}) %collective-permute-start.6) | collective-permute-done | bytes 36896 | tf_op jit(solution)/shard_map/ppermute | solution.py:65
  13.2 0.4 %collective-permute-done.1.refs_2_ = bf16[1,96,768]{2,1,0:T(8,128)(2,1)S(1)} collective-permute-done((bf16[1,96,768]{2,1,0:T(8,128)(2,1)}, bf16[1,96,768]{2,1,0:T(8,128)(2,1)S(1)}, u32[]{:S(2)}, u32[]{:S(2)}) %collective-permute-start.1) | collective-permute-done | bytes 147488 | tf_op jit(solution)/shard_map/ppermute | solution.py:25
  13.6 0.1 collective-permute-done.refs_1_
  13.7 0.5 %shard_map.49.refs_6_ = f32[4,48,96]{2,1,0:T(8,128)S(1)} custom-call(bf16[1,96,768]{2,1,0:T(8,128)(2,1)S(1)} %copy-done, bf16[1,96,768]{2,1,0:T(8,128)(2,1)S(1)} %collective-permute-done.refs_1_, bf16[1,96,768]{2,1,0:T(8,128)(2,1)S(1)} %collective-permute-done.1.refs_2_, bf16[1,96,768]{2,1,0:T(8,128)(2,1)S(1)} %collective-permute-done.2.refs_3_, ...), custom_call_target="tpu_custom_call" | custom-call | flops 1000000000 | bytes 3000000 | tf_op jit(solution)/shard_map/pallas_call | solution.py:250
  14.2 0.3 %collective-permute-done.7.refs_5_ = bf16[1,48,384]{2,1,0:T(8,128)(2,1)S(1)} collective-permute-done((bf16[1,48,384]{2,1,0:T(8,128)(2,1)S(1)}, bf16[1,48,384]{2,1,0:T(8,128)(2,1)S(1)}, u32[]{:S(2)}, u32[]{:S(2)}) %collective-permute-start.7) | collective-permute-done | bytes 36896 | tf_op jit(solution)/shard_map/ppermute | solution.py:81
  14.5 0.6 %shard_map.50 = f32[3,8,128]{2,1,0:T(8,128)S(1)} custom-call(bf16[1,96,768]{2,1,0:T(8,128)(2,1)S(1)} %copy-done, bf16[1,96,768]{2,1,0:T(8,128)(2,1)S(1)} %collective-permute-done.refs_1_, bf16[1,96,768]{2,1,0:T(8,128)(2,1)S(1)} %collective-permute-done.1.refs_2_, bf16[1,96,768]{2,1,0:T(8,128)(2,1)S(1)} %collective-permute-done.2.refs_3_, ...), custom_call_target="tpu_custom_call" | custom-call | tf_op jit(solution)/shard_map/pallas_call | solution.py:261
  15.1 0.2 collective-permute-start.8
  15.3 1.0 %collective-permute-done.8 = f32[3,8,128]{2,1,0:T(8,128)S(1)} collective-permute-done((f32[3,8,128]{2,1,0:T(8,128)S(1)}, f32[3,8,128]{2,1,0:T(8,128)S(1)}, u32[]{:S(2)}, u32[]{:S(2)}) %collective-permute-start.8) | collective-permute-done | bytes 12320 | tf_op jit(solution)/shard_map/ppermute | solution.py:81
  16.3 1.6 %collective-permute-start.11 = (f32[3,8,128]{2,1,0:T(8,128)S(1)}, f32[3,8,128]{2,1,0:T(8,128)S(1)}, u32[]{:S(2)}, u32[]{:S(2)}) collective-permute-start(f32[3,8,128]{2,1,0:T(8,128)S(1)} %add.3.refs_0_), channel_id=1, source_target_pairs={{0,6},{1,7},{2,4},{3,5},{4,2},{5,3},{6,0},{7,1},{8,14},{9,15},{10,... | collective-permute-start | bytes 36872 | tf_op jit(solution)/shard_map/ppermute | solution.py:29
  17.9 2.8 %collective-permute-start.9 = (f32[3,8,128]{2,1,0:T(8,128)S(1)}, f32[3,8,128]{2,1,0:T(8,128)S(1)}, u32[]{:S(2)}, u32[]{:S(2)}) collective-permute-start(f32[3,8,128]{2,1,0:T(8,128)S(1)} %add.3.refs_0_), channel_id=1, source_target_pairs={{0,4},{1,5},{2,6},{3,7},{4,0},{5,1},{6,2},{7,3},{8,12},{9,13},{10,... | collective-permute-start | bytes 36872 | tf_op jit(solution)/shard_map/ppermute | solution.py:29
  20.7 1.1 %collective-permute-done.11.refs_3_ = f32[3,8,128]{2,1,0:T(8,128)S(1)} collective-permute-done((f32[3,8,128]{2,1,0:T(8,128)S(1)}, f32[3,8,128]{2,1,0:T(8,128)S(1)}, u32[]{:S(2)}, u32[]{:S(2)}) %collective-permute-start.11) | collective-permute-done | bytes 12320 | tf_op jit(solution)/shard_map/ppermute | solution.py:29
  21.8 0.7 %collective-permute-done.9.refs_1_ = f32[3,8,128]{2,1,0:T(8,128)S(1)} collective-permute-done((f32[3,8,128]{2,1,0:T(8,128)S(1)}, f32[3,8,128]{2,1,0:T(8,128)S(1)}, u32[]{:S(2)}, u32[]{:S(2)}) %collective-permute-start.9) | collective-permute-done | bytes 12320 | tf_op jit(solution)/shard_map/ppermute | solution.py:29
  22.5 0.7 %shard_map.51 = f32[6,4,8,16]{3,2,1,0:T(8,128)} custom-call(f32[3,8,128]{2,1,0:T(8,128)S(1)} %add.3.refs_0_, f32[3,8,128]{2,1,0:T(8,128)S(1)} %collective-permute-done.9.refs_1_, f32[3,8,128]{2,1,0:T(8,128)S(1)} %collective-permute-done.10.refs_2_, f32[3,8,128]{2,1,0:T(8,128)S(1)} %collective-permute-done.11.refs_3_), custom_call_target="tpu_custom_call" | custom-call | tf_op jit(solution)/shard_map/pallas_call | solution.py:271
  (15 shorter events, 0.0 us)
Async XLA Ops:
  0.0 9.7 %copy-start.2 = (bf16[6,4,8,96]{3,2,1,0:T(8,128)(2,1)S(1)}, bf16[6,4,8,96]{3,2,1,0:T(8,128)(2,1)}, u32[]{:S(2)}) copy-start(bf16[6,4,8,96]{3,2,1,0:T(8,128)(2,1)} %param.5) | copy-start | bytes 110596
  0.0 9.1 %collective-permute-start.3 = (bf16[1,6,4,8,96]{4,3,2,1,0:T(8,128)(2,1)}, bf16[1,6,4,8,96]{4,3,2,1,0:T(8,128)(2,1)S(1)}, u32[]{:S(2)}, u32[]{:S(2)}) collective-permute-start(bf16[1,6,4,8,96]{4,3,2,1,0:T(8,128)(2,1)} %bitcast.2), channel_id=1, source_target_pairs={{0,4},{1,5},{2,6},{3,7},{4,0},{5,1},{6,2},{7,3},{8,12},{9,13},{10,... | collective-permute-start | bytes 110600 | tf_op jit(solution)/shard_map/ppermute | solution.py:65
  4.0 9.2 %collective-permute-start.2 = (bf16[1,96,768]{2,1,0:T(8,128)(2,1)}, bf16[1,96,768]{2,1,0:T(8,128)(2,1)S(1)}, u32[]{:S(2)}, u32[]{:S(2)}) collective-permute-start(bf16[1,96,768]{2,1,0:T(8,128)(2,1)} %refs_0_.3), channel_id=1, source_target_pairs={{0,24},{8,16},{16,8},{24,0},{1,25},{9,17},{17,9},{25,1},{2,26},{10... | collective-permute-start | bytes 442376 | tf_op jit(solution)/shard_map/ppermute | solution.py:25
  6.5 7.1 %collective-permute-start.1 = (bf16[1,96,768]{2,1,0:T(8,128)(2,1)}, bf16[1,96,768]{2,1,0:T(8,128)(2,1)S(1)}, u32[]{:S(2)}, u32[]{:S(2)}) collective-permute-start(bf16[1,96,768]{2,1,0:T(8,128)(2,1)} %refs_0_.3), channel_id=1, source_target_pairs={{0,16},{8,24},{16,0},{24,8},{1,17},{9,25},{17,1},{25,9},{2,18},{10... | collective-permute-start | bytes 442376 | tf_op jit(solution)/shard_map/ppermute | solution.py:25
  7.0 6.7 %collective-permute-start = (bf16[1,96,768]{2,1,0:T(8,128)(2,1)}, bf16[1,96,768]{2,1,0:T(8,128)(2,1)S(1)}, u32[]{:S(2)}, u32[]{:S(2)}) collective-permute-start(bf16[1,96,768]{2,1,0:T(8,128)(2,1)} %refs_0_.3), channel_id=1, source_target_pairs={{0,8},{8,0},{16,24},{24,16},{1,9},{9,1},{17,25},{25,17},{2,10},{10... | collective-permute-start | bytes 442376 | tf_op jit(solution)/shard_map/ppermute | solution.py:25
  7.5 4.3 %collective-permute-start.4 = (bf16[1,6,4,8,96]{4,3,2,1,0:T(8,128)(2,1)}, bf16[1,6,4,8,96]{4,3,2,1,0:T(8,128)(2,1)S(1)}, u32[]{:S(2)}, u32[]{:S(2)}) collective-permute-start(bf16[1,6,4,8,96]{4,3,2,1,0:T(8,128)(2,1)} %bitcast.3), channel_id=1, source_target_pairs={{0,2},{1,3},{2,0},{3,1},{4,6},{5,7},{6,4},{7,5},{8,10},{9,11},{10,... | collective-permute-start | bytes 110600 | tf_op jit(solution)/shard_map/ppermute | solution.py:65
  9.1 2.7 %copy-start.1 = (bf16[6,4,16,96]{3,2,1,0:T(8,128)(2,1)S(1)}, bf16[6,4,16,96]{3,2,1,0:T(8,128)(2,1)}, u32[]{:S(2)}) copy-start(bf16[6,4,16,96]{3,2,1,0:T(8,128)(2,1)} %refs_3_.1) | copy-start | bytes 221188
  9.1 2.7 %copy-start.3 = (s32[6,4]{0,1:T(4,128)S(1)}, s32[6,4]{0,1:T(4,128)}, u32[]{:S(2)}) copy-start(s32[6,4]{0,1:T(4,128)} %param.7) | copy-start | bytes 292
  9.2 4.5 %copy-start = (bf16[1,96,768]{2,1,0:T(8,128)(2,1)S(1)}, bf16[1,96,768]{2,1,0:T(8,128)(2,1)}, u32[]{:S(2)}) copy-start(bf16[1,96,768]{2,1,0:T(8,128)(2,1)} %refs_0_.3) | copy-start | bytes 442372
  9.2 4.0 %collective-permute-start.6 = (bf16[1,48,384]{2,1,0:T(8,128)(2,1)S(1)}, bf16[1,48,384]{2,1,0:T(8,128)(2,1)S(1)}, u32[]{:S(2)}, u32[]{:S(2)}) collective-permute-start(bf16[1,48,384]{2,1,0:T(8,128)(2,1)S(1)} %shard_map.47.refs_1_), channel_id=1, source_target_pairs={{0,2},{1,3},{2,0},{3,1},{4,6},{5,7},{6,4},{7,5},{8,10},{9,11},{10,... | collective-permute-start | bytes 110600 | tf_op jit(solution)/shard_map/ppermute | solution.py:65
  12.5 1.9 %collective-permute-start.5 = (bf16[3,48,384]{2,1,0:T(8,128)(2,1)S(1)}, bf16[3,48,384]{2,1,0:T(8,128)(2,1)S(1)}, u32[]{:S(2)}, u32[]{:S(2)}) collective-permute-start(bf16[3,48,384]{2,1,0:T(8,128)(2,1)S(1)} %get-tuple-element.7.refs_4_), channel_id=1, source_target_pairs={{0,1},{1,0},{2,3},{3,2},{4,5},{5,4},{6,7},{7,6},{8,9},{9,8},{10,11... | collective-permute-start | bytes 331784 | tf_op jit(solution)/shard_map/ppermute | solution.py:81
  13.2 1.2 %collective-permute-start.7 = (bf16[1,48,384]{2,1,0:T(8,128)(2,1)S(1)}, bf16[1,48,384]{2,1,0:T(8,128)(2,1)S(1)}, u32[]{:S(2)}, u32[]{:S(2)}) collective-permute-start(bf16[1,48,384]{2,1,0:T(8,128)(2,1)S(1)} %collective-permute-done.6.refs_5_), channel_id=1, source_target_pairs={{0,1},{1,0},{2,3},{3,2},{4,5},{5,4},{6,7},{7,6},{8,9},{9,8},{10,11... | collective-permute-start | bytes 110600 | tf_op jit(solution)/shard_map/ppermute | solution.py:81
  15.1 1.2 %collective-permute-start.8 = (f32[3,8,128]{2,1,0:T(8,128)S(1)}, f32[3,8,128]{2,1,0:T(8,128)S(1)}, u32[]{:S(2)}, u32[]{:S(2)}) collective-permute-start(f32[3,8,128]{2,1,0:T(8,128)S(1)} %shard_map.50), channel_id=1, source_target_pairs={{0,1},{1,0},{2,3},{3,2},{4,5},{5,4},{6,7},{7,6},{8,9},{9,8},{10,11... | collective-permute-start | bytes 36872 | tf_op jit(solution)/shard_map/ppermute | solution.py:81
  16.3 5.5 %collective-permute-start.11 = (f32[3,8,128]{2,1,0:T(8,128)S(1)}, f32[3,8,128]{2,1,0:T(8,128)S(1)}, u32[]{:S(2)}, u32[]{:S(2)}) collective-permute-start(f32[3,8,128]{2,1,0:T(8,128)S(1)} %add.3.refs_0_), channel_id=1, source_target_pairs={{0,6},{1,7},{2,4},{3,5},{4,2},{5,3},{6,0},{7,1},{8,14},{9,15},{10,... | collective-permute-start | bytes 36872 | tf_op jit(solution)/shard_map/ppermute | solution.py:29
  17.9 3.9 %collective-permute-start.10 = (f32[3,8,128]{2,1,0:T(8,128)S(1)}, f32[3,8,128]{2,1,0:T(8,128)S(1)}, u32[]{:S(2)}, u32[]{:S(2)}) collective-permute-start(f32[3,8,128]{2,1,0:T(8,128)S(1)} %add.3.refs_0_), channel_id=1, source_target_pairs={{0,2},{1,3},{2,0},{3,1},{4,6},{5,7},{6,4},{7,5},{8,10},{9,11},{10,... | collective-permute-start | bytes 36872 | tf_op jit(solution)/shard_map/ppermute | solution.py:29
  17.9 4.6 %collective-permute-start.9 = (f32[3,8,128]{2,1,0:T(8,128)S(1)}, f32[3,8,128]{2,1,0:T(8,128)S(1)}, u32[]{:S(2)}, u32[]{:S(2)}) collective-permute-start(f32[3,8,128]{2,1,0:T(8,128)S(1)} %add.3.refs_0_), channel_id=1, source_target_pairs={{0,4},{1,5},{2,6},{3,7},{4,0},{5,1},{6,2},{7,3},{8,12},{9,13},{10,... | collective-permute-start | bytes 36872 | tf_op jit(solution)/shard_map/ppermute | solution.py:29

commit v7 on v6

--- a/solution.py
+++ b/solution.py
@@ -156,7 +156,7 @@
 
 
 def near_kernel(npb, shifts, *refs):
-    w_refs, part_refs = refs[:npb], refs[npb:-3]
+    w_refs, part_refs = [refs[([0] + chip_order(npb)).index(s)] for s in range(npb)], refs[npb:-3]
     out_ref, slab_ref, full_ref = refs[-3:]
     pb, ga = lax.axis_index("pb"), lax.axis_index("ga")
     join_slabs(shifts, lax.rem(ga, CORES), part_refs, slab_ref, full_ref)
@@ -165,7 +165,7 @@
 
 
 def partial_kernel(npb, shifts, *refs):
-    w_refs, part_refs = refs[:npb], refs[npb:-5]
+    w_refs, part_refs = [refs[([0] + chip_order(npb)).index(s)] for s in range(npb)], refs[npb:-5]
     near_ref, val_ref, out_ref, slab_ref, full_ref = refs[-5:]
     n_tiles, nc, _ = out_ref.shape
     nq, rows, ng = near_ref.shape
@@ -257,7 +257,7 @@
         cost_estimate=pl.CostEstimate(
             flops=1000000000, bytes_accessed=3000000, transcendentals=0
         ),
-    )(*w_parts, *mine)
+    )(*[w_parts[s] for s in [0] + chip_order(npb)], *mine)
     partial_value = pl.pallas_call(
         functools.partial(partial_kernel, npb, shifts),
         out_shape=jax.ShapeDtypeStruct((n_tiles, nc, LANES), jnp.float32),
@@ -265,7 +265,7 @@
         out_specs=vmem,
         scratch_shapes=join_scratch,
         compiler_params=params,
-    )(*w_parts, *other, near, prepared)
+    )(*[w_parts[s] for s in [0] + chip_order(npb)], *other, near, prepared)
     chip_value = partial_value + send_core(partial_value, nz)
     shares = [chip_value] + [send_chip(chip_value, s, nz) for s in chip_order(nz)]
     return pl.pallas_call(

time: 23.4 us -> 23.4 us (level)
  transfers between devices with their start and end apart: 12 -> 12, of which waited for: 8 -> 7; matrix products, arithmetic and copies ran while one was open for 0% -> 0% of each run, Pallas kernels for 6% -> 6%
where the time goes in v7:
time: 23.4 us; the launch traced here: 23.2 us
  starting transfers between devices  14.3 us (61%)
  waiting for transfers between devices  6.15 us (26%)
  Pallas kernels  2.74 us (12%)
    ppermute x3, starting transfers between devices, gather_chips(): groups.append((moved, lax.ppermute(array, 'ga', pairs)))  6.13 us
    ppermute x3, starting transfers between devices, send_chip(): lax.ppermute(x, 'ga', [(i * CORES + c, partner(i, s, nz) * CORES + c) for...  4.39 us
    ppermute x3, starting transfers between devices, send_pb(): return lax.ppermute(x, 'pb', [(i, partner(i, s, npb)) for i in range(npb)])  3.49 us
    ppermute x3, waiting for transfers between devices, gather_chips(): groups.append((moved, lax.ppermute(array, 'ga', pairs)))  2.62 us
    ppermute x3, waiting for transfers between devices, send_chip(): lax.ppermute(x, 'ga', [(i * CORES + c, partner(i, s, nz) * CORES + c) for...  1.8 us
    ppermute x3, waiting for transfers between devices, send_core(): lax.ppermute(x, 'ga', [(i * CORES + c, i * CORES + 1 - c) for i in range(...  1.29 us
    pallas_call x1, Pallas kernels, per_device(): pl.pallas_call(functools.partial(place_kernel, nz), out_shape=jax.ShapeDt...  0.73 us
    pallas_call x1, Pallas kernels, per_device(): pl.pallas_call(functools.partial(prepare_kernel, npb), out_shape=(jax.Sha...  0.7 us
  transfers between devices with their start and end apart: 12, of which 7 were waited for; matrix products, arithmetic and copies ran while one was open for 0% of the time, Pallas kernels for 6%

profile of v7, /device:TPU:0, one launch (start us, length us, event | category | flops | bytes accessed | tf_op | source)
XLA Modules:
  0.0 23.2 jit_solution(11896296023321705510)
XLA Ops:
  0.0 4.0 %collective-permute-start.3 = (bf16[1,6,4,8,96]{4,3,2,1,0:T(8,128)(2,1)}, bf16[1,6,4,8,96]{4,3,2,1,0:T(8,128)(2,1)S(1)}, u32[]{:S(2)}, u32[]{:S(2)}) collective-permute-start(bf16[1,6,4,8,96]{4,3,2,1,0:T(8,128)(2,1)} %bitcast.2), channel_id=1, source_target_pairs={{0,4},{1,5},{2,6},{3,7},{4,0},{5,1},{6,2},{7,3},{8,12},{9,13},{10,... | collective-permute-start | bytes 110600 | tf_op jit(solution)/shard_map/ppermute | solution.py:65
  4.0 2.4 %collective-permute-start.2 = (bf16[1,96,768]{2,1,0:T(8,128)(2,1)}, bf16[1,96,768]{2,1,0:T(8,128)(2,1)S(1)}, u32[]{:S(2)}, u32[]{:S(2)}) collective-permute-start(bf16[1,96,768]{2,1,0:T(8,128)(2,1)} %refs_0_.3), channel_id=1, source_target_pairs={{0,24},{8,16},{16,8},{24,0},{1,25},{9,17},{17,9},{25,1},{2,26},{10... | collective-permute-start | bytes 442376 | tf_op jit(solution)/shard_map/ppermute | solution.py:25
  6.5 0.5 %collective-permute-start.1 = (bf16[1,96,768]{2,1,0:T(8,128)(2,1)}, bf16[1,96,768]{2,1,0:T(8,128)(2,1)S(1)}, u32[]{:S(2)}, u32[]{:S(2)}) collective-permute-start(bf16[1,96,768]{2,1,0:T(8,128)(2,1)} %refs_0_.3), channel_id=1, source_target_pairs={{0,8},{8,0},{16,24},{24,16},{1,9},{9,1},{17,25},{25,17},{2,10},{10... | collective-permute-start | bytes 442376 | tf_op jit(solution)/shard_map/ppermute | solution.py:25
  7.0 0.5 %collective-permute-start = (bf16[1,96,768]{2,1,0:T(8,128)(2,1)}, bf16[1,96,768]{2,1,0:T(8,128)(2,1)S(1)}, u32[]{:S(2)}, u32[]{:S(2)}) collective-permute-start(bf16[1,96,768]{2,1,0:T(8,128)(2,1)} %refs_0_.3), channel_id=1, source_target_pairs={{0,16},{8,24},{16,0},{24,8},{1,17},{9,25},{17,1},{25,9},{2,18},{10... | collective-permute-start | bytes 442376 | tf_op jit(solution)/shard_map/ppermute | solution.py:25
  7.5 1.6 %collective-permute-start.4 = (bf16[1,6,4,8,96]{4,3,2,1,0:T(8,128)(2,1)}, bf16[1,6,4,8,96]{4,3,2,1,0:T(8,128)(2,1)S(1)}, u32[]{:S(2)}, u32[]{:S(2)}) collective-permute-start(bf16[1,6,4,8,96]{4,3,2,1,0:T(8,128)(2,1)} %bitcast.3), channel_id=1, source_target_pairs={{0,2},{1,3},{2,0},{3,1},{4,6},{5,7},{6,4},{7,5},{8,10},{9,11},{10,... | collective-permute-start | bytes 110600 | tf_op jit(solution)/shard_map/ppermute | solution.py:65
  9.1 0.1 shard_map.47.refs_1_
  9.2 0.0 copy-start
  9.2 0.5 %collective-permute-start.6 = (bf16[1,48,384]{2,1,0:T(8,128)(2,1)S(1)}, bf16[1,48,384]{2,1,0:T(8,128)(2,1)S(1)}, u32[]{:S(2)}, u32[]{:S(2)}) collective-permute-start(bf16[1,48,384]{2,1,0:T(8,128)(2,1)S(1)} %shard_map.47.refs_1_), channel_id=1, source_target_pairs={{0,2},{1,3},{2,0},{3,1},{4,6},{5,7},{6,4},{7,5},{8,10},{9,11},{10,... | collective-permute-start | bytes 110600 | tf_op jit(solution)/shard_map/ppermute | solution.py:65
  9.7 0.1 shard_map.46.refs_0_
  9.8 2.0 %collective-permute-done.4.refs_2_ = bf16[1,6,4,8,96]{4,3,2,1,0:T(8,128)(2,1)S(1)} collective-permute-done((bf16[1,6,4,8,96]{4,3,2,1,0:T(8,128)(2,1)}, bf16[1,6,4,8,96]{4,3,2,1,0:T(8,128)(2,1)S(1)}, u32[]{:S(2)}, u32[]{:S(2)}) %collective-permute-start.4) | collective-permute-done | bytes 36896 | tf_op jit(solution)/shard_map/ppermute | solution.py:65
  11.8 0.7 %shard_map.48 = (bf16[3,48,384]{2,1,0:T(8,128)(2,1)S(1)}, bf16[3,128,512]{2,1,0:T(8,128)(2,1)S(1)}) custom-call(bf16[1,48,384]{2,1,0:T(8,128)(2,1)S(1)} %shard_map.46.refs_0_, bf16[1,48,384]{2,1,0:T(8,128)(2,1)S(1)} %shard_map.47.refs_1_, bf16[1,6,4,8,96]{4,3,2,1,0:T(8,128)(2,1)S(1)} %collective-permute-done.4.refs_2_, bf16[6,4,16,96]{3,2,1,0:T(8,128)(2,1)S(1)} %copy-done.1, ...), custom_call_target="tpu_custom_call" | custom-call | tf_op jit(solution)/shard_map/pallas_call | solution.py:238
  12.5 0.1 collective-permute-start.5
  12.6 0.6 %collective-permute-done.6.refs_5_ = bf16[1,48,384]{2,1,0:T(8,128)(2,1)S(1)} collective-permute-done((bf16[1,48,384]{2,1,0:T(8,128)(2,1)S(1)}, bf16[1,48,384]{2,1,0:T(8,128)(2,1)S(1)}, u32[]{:S(2)}, u32[]{:S(2)}) %collective-permute-start.6) | collective-permute-done | bytes 36896 | tf_op jit(solution)/shard_map/ppermute | solution.py:65
  13.2 0.4 %collective-permute-done.1.refs_2_ = bf16[1,96,768]{2,1,0:T(8,128)(2,1)S(1)} collective-permute-done((bf16[1,96,768]{2,1,0:T(8,128)(2,1)}, bf16[1,96,768]{2,1,0:T(8,128)(2,1)S(1)}, u32[]{:S(2)}, u32[]{:S(2)}) %collective-permute-start.1) | collective-permute-done | bytes 147488 | tf_op jit(solution)/shard_map/ppermute | solution.py:25
  13.7 0.5 %shard_map.49.refs_6_ = f32[4,48,96]{2,1,0:T(8,128)S(1)} custom-call(bf16[1,96,768]{2,1,0:T(8,128)(2,1)S(1)} %copy-done, bf16[1,96,768]{2,1,0:T(8,128)(2,1)S(1)} %collective-permute-done.refs_1_, bf16[1,96,768]{2,1,0:T(8,128)(2,1)S(1)} %collective-permute-done.1.refs_2_, bf16[1,96,768]{2,1,0:T(8,128)(2,1)S(1)} %collective-permute-done.2.refs_3_, ...), custom_call_target="tpu_custom_call" | custom-call | flops 1000000000 | bytes 3000000 | tf_op jit(solution)/shard_map/pallas_call | solution.py:250
  14.2 0.3 %collective-permute-done.7.refs_5_ = bf16[1,48,384]{2,1,0:T(8,128)(2,1)S(1)} collective-permute-done((bf16[1,48,384]{2,1,0:T(8,128)(2,1)S(1)}, bf16[1,48,384]{2,1,0:T(8,128)(2,1)S(1)}, u32[]{:S(2)}, u32[]{:S(2)}) %collective-permute-start.7) | collective-permute-done | bytes 36896 | tf_op jit(solution)/shard_map/ppermute | solution.py:81
  14.5 0.6 %shard_map.50 = f32[3,8,128]{2,1,0:T(8,128)S(1)} custom-call(bf16[1,96,768]{2,1,0:T(8,128)(2,1)S(1)} %copy-done, bf16[1,96,768]{2,1,0:T(8,128)(2,1)S(1)} %collective-permute-done.refs_1_, bf16[1,96,768]{2,1,0:T(8,128)(2,1)S(1)} %collective-permute-done.1.refs_2_, bf16[1,96,768]{2,1,0:T(8,128)(2,1)S(1)} %collective-permute-done.2.refs_3_, ...), custom_call_target="tpu_custom_call" | custom-call | tf_op jit(solution)/shard_map/pallas_call | solution.py:261
  15.1 0.2 collective-permute-start.8
  15.3 1.0 %collective-permute-done.8 = f32[3,8,128]{2,1,0:T(8,128)S(1)} collective-permute-done((f32[3,8,128]{2,1,0:T(8,128)S(1)}, f32[3,8,128]{2,1,0:T(8,128)S(1)}, u32[]{:S(2)}, u32[]{:S(2)}) %collective-permute-start.8) | collective-permute-done | bytes 12320 | tf_op jit(solution)/shard_map/ppermute | solution.py:81
  16.3 1.6 %collective-permute-start.11 = (f32[3,8,128]{2,1,0:T(8,128)S(1)}, f32[3,8,128]{2,1,0:T(8,128)S(1)}, u32[]{:S(2)}, u32[]{:S(2)}) collective-permute-start(f32[3,8,128]{2,1,0:T(8,128)S(1)} %add.3.refs_0_), channel_id=1, source_target_pairs={{0,6},{1,7},{2,4},{3,5},{4,2},{5,3},{6,0},{7,1},{8,14},{9,15},{10,... | collective-permute-start | bytes 36872 | tf_op jit(solution)/shard_map/ppermute | solution.py:29
  17.9 2.8 %collective-permute-start.9 = (f32[3,8,128]{2,1,0:T(8,128)S(1)}, f32[3,8,128]{2,1,0:T(8,128)S(1)}, u32[]{:S(2)}, u32[]{:S(2)}) collective-permute-start(f32[3,8,128]{2,1,0:T(8,128)S(1)} %add.3.refs_0_), channel_id=1, source_target_pairs={{0,4},{1,5},{2,6},{3,7},{4,0},{5,1},{6,2},{7,3},{8,12},{9,13},{10,... | collective-permute-start | bytes 36872 | tf_op jit(solution)/shard_map/ppermute | solution.py:29
  20.7 1.1 %collective-permute-done.11.refs_3_ = f32[3,8,128]{2,1,0:T(8,128)S(1)} collective-permute-done((f32[3,8,128]{2,1,0:T(8,128)S(1)}, f32[3,8,128]{2,1,0:T(8,128)S(1)}, u32[]{:S(2)}, u32[]{:S(2)}) %collective-permute-start.11) | collective-permute-done | bytes 12320 | tf_op jit(solution)/shard_map/ppermute | solution.py:29
  21.8 0.7 %collective-permute-done.9.refs_1_ = f32[3,8,128]{2,1,0:T(8,128)S(1)} collective-permute-done((f32[3,8,128]{2,1,0:T(8,128)S(1)}, f32[3,8,128]{2,1,0:T(8,128)S(1)}, u32[]{:S(2)}, u32[]{:S(2)}) %collective-permute-start.9) | collective-permute-done | bytes 12320 | tf_op jit(solution)/shard_map/ppermute | solution.py:29
  22.5 0.7 %shard_map.51 = f32[6,4,8,16]{3,2,1,0:T(8,128)} custom-call(f32[3,8,128]{2,1,0:T(8,128)S(1)} %add.3.refs_0_, f32[3,8,128]{2,1,0:T(8,128)S(1)} %collective-permute-done.9.refs_1_, f32[3,8,128]{2,1,0:T(8,128)S(1)} %collective-permute-done.10.refs_2_, f32[3,8,128]{2,1,0:T(8,128)S(1)} %collective-permute-done.11.refs_3_), custom_call_target="tpu_custom_call" | custom-call | tf_op jit(solution)/shard_map/pallas_call | solution.py:271
  (15 shorter events, 0.0 us)
Async XLA Ops:
  0.0 9.7 %copy-start.2 = (bf16[6,4,8,96]{3,2,1,0:T(8,128)(2,1)S(1)}, bf16[6,4,8,96]{3,2,1,0:T(8,128)(2,1)}, u32[]{:S(2)}) copy-start(bf16[6,4,8,96]{3,2,1,0:T(8,128)(2,1)} %param.5) | copy-start | bytes 110596
  0.0 9.1 %collective-permute-start.3 = (bf16[1,6,4,8,96]{4,3,2,1,0:T(8,128)(2,1)}, bf16[1,6,4,8,96]{4,3,2,1,0:T(8,128)(2,1)S(1)}, u32[]{:S(2)}, u32[]{:S(2)}) collective-permute-start(bf16[1,6,4,8,96]{4,3,2,1,0:T(8,128)(2,1)} %bitcast.2), channel_id=1, source_target_pairs={{0,4},{1,5},{2,6},{3,7},{4,0},{5,1},{6,2},{7,3},{8,12},{9,13},{10,... | collective-permute-start | bytes 110600 | tf_op jit(solution)/shard_map/ppermute | solution.py:65
  4.0 9.2 %collective-permute-start.2 = (bf16[1,96,768]{2,1,0:T(8,128)(2,1)}, bf16[1,96,768]{2,1,0:T(8,128)(2,1)S(1)}, u32[]{:S(2)}, u32[]{:S(2)}) collective-permute-start(bf16[1,96,768]{2,1,0:T(8,128)(2,1)} %refs_0_.3), channel_id=1, source_target_pairs={{0,24},{8,16},{16,8},{24,0},{1,25},{9,17},{17,9},{25,1},{2,26},{10... | collective-permute-start | bytes 442376 | tf_op jit(solution)/shard_map/ppermute | solution.py:25
  6.5 7.2 %collective-permute-start.1 = (bf16[1,96,768]{2,1,0:T(8,128)(2,1)}, bf16[1,96,768]{2,1,0:T(8,128)(2,1)S(1)}, u32[]{:S(2)}, u32[]{:S(2)}) collective-permute-start(bf16[1,96,768]{2,1,0:T(8,128)(2,1)} %refs_0_.3), channel_id=1, source_target_pairs={{0,8},{8,0},{16,24},{24,16},{1,9},{9,1},{17,25},{25,17},{2,10},{10... | collective-permute-start | bytes 442376 | tf_op jit(solution)/shard_map/ppermute | solution.py:25
  7.0 6.7 %collective-permute-start = (bf16[1,96,768]{2,1,0:T(8,128)(2,1)}, bf16[1,96,768]{2,1,0:T(8,128)(2,1)S(1)}, u32[]{:S(2)}, u32[]{:S(2)}) collective-permute-start(bf16[1,96,768]{2,1,0:T(8,128)(2,1)} %refs_0_.3), channel_id=1, source_target_pairs={{0,16},{8,24},{16,0},{24,8},{1,17},{9,25},{17,1},{25,9},{2,18},{10... | collective-permute-start | bytes 442376 | tf_op jit(solution)/shard_map/ppermute | solution.py:25
  7.5 4.3 %collective-permute-start.4 = (bf16[1,6,4,8,96]{4,3,2,1,0:T(8,128)(2,1)}, bf16[1,6,4,8,96]{4,3,2,1,0:T(8,128)(2,1)S(1)}, u32[]{:S(2)}, u32[]{:S(2)}) collective-permute-start(bf16[1,6,4,8,96]{4,3,2,1,0:T(8,128)(2,1)} %bitcast.3), channel_id=1, source_target_pairs={{0,2},{1,3},{2,0},{3,1},{4,6},{5,7},{6,4},{7,5},{8,10},{9,11},{10,... | collective-permute-start | bytes 110600 | tf_op jit(solution)/shard_map/ppermute | solution.py:65
  9.1 2.7 %copy-start.1 = (bf16[6,4,16,96]{3,2,1,0:T(8,128)(2,1)S(1)}, bf16[6,4,16,96]{3,2,1,0:T(8,128)(2,1)}, u32[]{:S(2)}) copy-start(bf16[6,4,16,96]{3,2,1,0:T(8,128)(2,1)} %refs_3_.1) | copy-start | bytes 221188
  9.1 2.7 %copy-start.3 = (s32[6,4]{0,1:T(4,128)S(1)}, s32[6,4]{0,1:T(4,128)}, u32[]{:S(2)}) copy-start(s32[6,4]{0,1:T(4,128)} %param.7) | copy-start | bytes 292
  9.2 4.5 %copy-start = (bf16[1,96,768]{2,1,0:T(8,128)(2,1)S(1)}, bf16[1,96,768]{2,1,0:T(8,128)(2,1)}, u32[]{:S(2)}) copy-start(bf16[1,96,768]{2,1,0:T(8,128)(2,1)} %refs_0_.3) | copy-start | bytes 442372
  9.2 4.0 %collective-permute-start.6 = (bf16[1,48,384]{2,1,0:T(8,128)(2,1)S(1)}, bf16[1,48,384]{2,1,0:T(8,128)(2,1)S(1)}, u32[]{:S(2)}, u32[]{:S(2)}) collective-permute-start(bf16[1,48,384]{2,1,0:T(8,128)(2,1)S(1)} %shard_map.47.refs_1_), channel_id=1, source_target_pairs={{0,2},{1,3},{2,0},{3,1},{4,6},{5,7},{6,4},{7,5},{8,10},{9,11},{10,... | collective-permute-start | bytes 110600 | tf_op jit(solution)/shard_map/ppermute | solution.py:65
  12.5 1.9 %collective-permute-start.5 = (bf16[3,48,384]{2,1,0:T(8,128)(2,1)S(1)}, bf16[3,48,384]{2,1,0:T(8,128)(2,1)S(1)}, u32[]{:S(2)}, u32[]{:S(2)}) collective-permute-start(bf16[3,48,384]{2,1,0:T(8,128)(2,1)S(1)} %get-tuple-element.7.refs_4_), channel_id=1, source_target_pairs={{0,1},{1,0},{2,3},{3,2},{4,5},{5,4},{6,7},{7,6},{8,9},{9,8},{10,11... | collective-permute-start | bytes 331784 | tf_op jit(solution)/shard_map/ppermute | solution.py:81
  13.2 1.2 %collective-permute-start.7 = (bf16[1,48,384]{2,1,0:T(8,128)(2,1)S(1)}, bf16[1,48,384]{2,1,0:T(8,128)(2,1)S(1)}, u32[]{:S(2)}, u32[]{:S(2)}) collective-permute-start(bf16[1,48,384]{2,1,0:T(8,128)(2,1)S(1)} %collective-permute-done.6.refs_5_), channel_id=1, source_target_pairs={{0,1},{1,0},{2,3},{3,2},{4,5},{5,4},{6,7},{7,6},{8,9},{9,8},{10,11... | collective-permute-start | bytes 110600 | tf_op jit(solution)/shard_map/ppermute | solution.py:81
  15.1 1.2 %collective-permute-start.8 = (f32[3,8,128]{2,1,0:T(8,128)S(1)}, f32[3,8,128]{2,1,0:T(8,128)S(1)}, u32[]{:S(2)}, u32[]{:S(2)}) collective-permute-start(f32[3,8,128]{2,1,0:T(8,128)S(1)} %shard_map.50), channel_id=1, source_target_pairs={{0,1},{1,0},{2,3},{3,2},{4,5},{5,4},{6,7},{7,6},{8,9},{9,8},{10,11... | collective-permute-start | bytes 36872 | tf_op jit(solution)/shard_map/ppermute | solution.py:81
  16.3 5.5 %collective-permute-start.11 = (f32[3,8,128]{2,1,0:T(8,128)S(1)}, f32[3,8,128]{2,1,0:T(8,128)S(1)}, u32[]{:S(2)}, u32[]{:S(2)}) collective-permute-start(f32[3,8,128]{2,1,0:T(8,128)S(1)} %add.3.refs_0_), channel_id=1, source_target_pairs={{0,6},{1,7},{2,4},{3,5},{4,2},{5,3},{6,0},{7,1},{8,14},{9,15},{10,... | collective-permute-start | bytes 36872 | tf_op jit(solution)/shard_map/ppermute | solution.py:29
  17.9 3.9 %collective-permute-start.10 = (f32[3,8,128]{2,1,0:T(8,128)S(1)}, f32[3,8,128]{2,1,0:T(8,128)S(1)}, u32[]{:S(2)}, u32[]{:S(2)}) collective-permute-start(f32[3,8,128]{2,1,0:T(8,128)S(1)} %add.3.refs_0_), channel_id=1, source_target_pairs={{0,2},{1,3},{2,0},{3,1},{4,6},{5,7},{6,4},{7,5},{8,10},{9,11},{10,... | collective-permute-start | bytes 36872 | tf_op jit(solution)/shard_map/ppermute | solution.py:29
  17.9 4.6 %collective-permute-start.9 = (f32[3,8,128]{2,1,0:T(8,128)S(1)}, f32[3,8,128]{2,1,0:T(8,128)S(1)}, u32[]{:S(2)}, u32[]{:S(2)}) collective-permute-start(f32[3,8,128]{2,1,0:T(8,128)S(1)} %add.3.refs_0_), channel_id=1, source_target_pairs={{0,4},{1,5},{2,6},{3,7},{4,0},{5,1},{6,2},{7,3},{8,12},{9,13},{10,... | collective-permute-start | bytes 36872 | tf_op jit(solution)/shard_map/ppermute | solution.py:29

commit v8 on v6

--- a/solution.py
+++ b/solution.py
@@ -181,12 +181,13 @@
         high.append(applied.astype(jnp.bfloat16))
         low.append((applied - high[-1].astype(jnp.float32)).astype(jnp.bfloat16))
     high, low = jnp.concatenate(high, axis=1), jnp.concatenate(low, axis=1)
+    every = val_ref[...].reshape(n_tiles * LANES, nq * LANES)
+    total = dot_nt(jnp.concatenate([high, low]), every)
+    total = total[:rows] + total[rows:]
     owner = lax.broadcasted_iota(jnp.int32, (nc, LANES), 1) // (LANES // blocks)
     for t in range(n_tiles):
         first, last = t * blocks // nq, ((t + 1) * blocks - 1) // nq + 1
-        both = jnp.concatenate([high[first * nc : last * nc], low[first * nc : last * nc]])
-        product = dot_nt(both, val_ref[t])
-        product = product[: (last - first) * nc] + product[(last - first) * nc :]
+        product = total[first * nc : last * nc, t * LANES : (t + 1) * LANES]
         tile = product[:nc]
         for k in range(first + 1, last):
             mine = (owner + t * blocks) // nq == k

time: 23.4 us -> 23.4 us (level)
  no operation moved by 1% of the time
where the time goes in v8:
time: 23.4 us; the launch traced here: 23.3 us
  starting transfers between devices  14.3 us (61%)
  waiting for transfers between devices  6.15 us (26%)
  Pallas kernels  2.73 us (12%)
    ppermute x3, starting transfers between devices, gather_chips(): groups.append((moved, lax.ppermute(array, 'ga', pairs)))  6.13 us
    ppermute x3, starting transfers between devices, send_chip(): lax.ppermute(x, 'ga', [(i * CORES + c, partner(i, s, nz) * CORES + c) for...  4.39 us
    ppermute x3, starting transfers between devices, send_pb(): return lax.ppermute(x, 'pb', [(i, partner(i, s, npb)) for i in range(npb)])  3.49 us
    ppermute x3, waiting for transfers between devices, gather_chips(): groups.append((moved, lax.ppermute(array, 'ga', pairs)))  2.62 us
    ppermute x3, waiting for transfers between devices, send_chip(): lax.ppermute(x, 'ga', [(i * CORES + c, partner(i, s, nz) * CORES + c) for...  1.8 us
    ppermute x3, waiting for transfers between devices, send_core(): lax.ppermute(x, 'ga', [(i * CORES + c, i * CORES + 1 - c) for i in range(...  1.3 us
    pallas_call x1, Pallas kernels, per_device(): pl.pallas_call(functools.partial(place_kernel, nz), out_shape=jax.ShapeDt...  0.73 us
    pallas_call x1, Pallas kernels, per_device(): pl.pallas_call(functools.partial(prepare_kernel, npb), out_shape=(jax.Sha...  0.7 us
  transfers between devices with their start and end apart: 12, of which 8 were waited for; matrix products, arithmetic and copies ran while one was open for 0% of the time, Pallas kernels for 6%

profile of v8, /device:TPU:0, one launch (start us, length us, event | category | flops | bytes accessed | tf_op | source)
XLA Modules:
  0.0 23.3 jit_solution(16751348598490465733)
XLA Ops:
  0.0 4.0 %collective-permute-start.3 = (bf16[1,6,4,8,96]{4,3,2,1,0:T(8,128)(2,1)}, bf16[1,6,4,8,96]{4,3,2,1,0:T(8,128)(2,1)S(1)}, u32[]{:S(2)}, u32[]{:S(2)}) collective-permute-start(bf16[1,6,4,8,96]{4,3,2,1,0:T(8,128)(2,1)} %bitcast.2), channel_id=1, source_target_pairs={{0,4},{1,5},{2,6},{3,7},{4,0},{5,1},{6,2},{7,3},{8,12},{9,13},{10,... | collective-permute-start | bytes 110600 | tf_op jit(solution)/shard_map/ppermute | solution.py:65
  4.0 2.4 %collective-permute-start.2 = (bf16[1,96,768]{2,1,0:T(8,128)(2,1)}, bf16[1,96,768]{2,1,0:T(8,128)(2,1)S(1)}, u32[]{:S(2)}, u32[]{:S(2)}) collective-permute-start(bf16[1,96,768]{2,1,0:T(8,128)(2,1)} %refs_0_.3), channel_id=1, source_target_pairs={{0,24},{8,16},{16,8},{24,0},{1,25},{9,17},{17,9},{25,1},{2,26},{10... | collective-permute-start | bytes 442376 | tf_op jit(solution)/shard_map/ppermute | solution.py:25
  6.5 0.5 %collective-permute-start.1 = (bf16[1,96,768]{2,1,0:T(8,128)(2,1)}, bf16[1,96,768]{2,1,0:T(8,128)(2,1)S(1)}, u32[]{:S(2)}, u32[]{:S(2)}) collective-permute-start(bf16[1,96,768]{2,1,0:T(8,128)(2,1)} %refs_0_.3), channel_id=1, source_target_pairs={{0,16},{8,24},{16,0},{24,8},{1,17},{9,25},{17,1},{25,9},{2,18},{10... | collective-permute-start | bytes 442376 | tf_op jit(solution)/shard_map/ppermute | solution.py:25
  7.0 0.5 %collective-permute-start = (bf16[1,96,768]{2,1,0:T(8,128)(2,1)}, bf16[1,96,768]{2,1,0:T(8,128)(2,1)S(1)}, u32[]{:S(2)}, u32[]{:S(2)}) collective-permute-start(bf16[1,96,768]{2,1,0:T(8,128)(2,1)} %refs_0_.3), channel_id=1, source_target_pairs={{0,8},{8,0},{16,24},{24,16},{1,9},{9,1},{17,25},{25,17},{2,10},{10... | collective-permute-start | bytes 442376 | tf_op jit(solution)/shard_map/ppermute | solution.py:25
  7.5 1.6 %collective-permute-start.4 = (bf16[1,6,4,8,96]{4,3,2,1,0:T(8,128)(2,1)}, bf16[1,6,4,8,96]{4,3,2,1,0:T(8,128)(2,1)S(1)}, u32[]{:S(2)}, u32[]{:S(2)}) collective-permute-start(bf16[1,6,4,8,96]{4,3,2,1,0:T(8,128)(2,1)} %bitcast.3), channel_id=1, source_target_pairs={{0,2},{1,3},{2,0},{3,1},{4,6},{5,7},{6,4},{7,5},{8,10},{9,11},{10,... | collective-permute-start | bytes 110600 | tf_op jit(solution)/shard_map/ppermute | solution.py:65
  9.1 0.1 shard_map.47.refs_1_
  9.2 0.5 %collective-permute-start.6 = (bf16[1,48,384]{2,1,0:T(8,128)(2,1)S(1)}, bf16[1,48,384]{2,1,0:T(8,128)(2,1)S(1)}, u32[]{:S(2)}, u32[]{:S(2)}) collective-permute-start(bf16[1,48,384]{2,1,0:T(8,128)(2,1)S(1)} %shard_map.47.refs_1_), channel_id=1, source_target_pairs={{0,2},{1,3},{2,0},{3,1},{4,6},{5,7},{6,4},{7,5},{8,10},{9,11},{10,... | collective-permute-start | bytes 110600 | tf_op jit(solution)/shard_map/ppermute | solution.py:65
  9.7 0.1 shard_map.46.refs_0_
  9.8 2.0 %collective-permute-done.4.refs_2_ = bf16[1,6,4,8,96]{4,3,2,1,0:T(8,128)(2,1)S(1)} collective-permute-done((bf16[1,6,4,8,96]{4,3,2,1,0:T(8,128)(2,1)}, bf16[1,6,4,8,96]{4,3,2,1,0:T(8,128)(2,1)S(1)}, u32[]{:S(2)}, u32[]{:S(2)}) %collective-permute-start.4) | collective-permute-done | bytes 36896 | tf_op jit(solution)/shard_map/ppermute | solution.py:65
  11.8 0.7 %shard_map.48 = (bf16[3,48,384]{2,1,0:T(8,128)(2,1)S(1)}, bf16[3,128,512]{2,1,0:T(8,128)(2,1)S(1)}) custom-call(bf16[1,48,384]{2,1,0:T(8,128)(2,1)S(1)} %shard_map.46.refs_0_, bf16[1,48,384]{2,1,0:T(8,128)(2,1)S(1)} %shard_map.47.refs_1_, bf16[1,6,4,8,96]{4,3,2,1,0:T(8,128)(2,1)S(1)} %collective-permute-done.4.refs_2_, bf16[6,4,16,96]{3,2,1,0:T(8,128)(2,1)S(1)} %copy-done.1, ...), custom_call_target="tpu_custom_call" | custom-call | tf_op jit(solution)/shard_map/pallas_call | solution.py:239
  12.5 0.1 collective-permute-start.5
  12.6 0.6 %collective-permute-done.6.refs_5_ = bf16[1,48,384]{2,1,0:T(8,128)(2,1)S(1)} collective-permute-done((bf16[1,48,384]{2,1,0:T(8,128)(2,1)S(1)}, bf16[1,48,384]{2,1,0:T(8,128)(2,1)S(1)}, u32[]{:S(2)}, u32[]{:S(2)}) %collective-permute-start.6) | collective-permute-done | bytes 36896 | tf_op jit(solution)/shard_map/ppermute | solution.py:65
  13.2 0.4 %collective-permute-done.1.refs_2_ = bf16[1,96,768]{2,1,0:T(8,128)(2,1)S(1)} collective-permute-done((bf16[1,96,768]{2,1,0:T(8,128)(2,1)}, bf16[1,96,768]{2,1,0:T(8,128)(2,1)S(1)}, u32[]{:S(2)}, u32[]{:S(2)}) %collective-permute-start.1) | collective-permute-done | bytes 147488 | tf_op jit(solution)/shard_map/ppermute | solution.py:25
  13.6 0.1 collective-permute-done.refs_1_
  13.7 0.5 %shard_map.49.refs_6_ = f32[4,48,96]{2,1,0:T(8,128)S(1)} custom-call(bf16[1,96,768]{2,1,0:T(8,128)(2,1)S(1)} %copy-done, bf16[1,96,768]{2,1,0:T(8,128)(2,1)S(1)} %collective-permute-done.refs_1_, bf16[1,96,768]{2,1,0:T(8,128)(2,1)S(1)} %collective-permute-done.1.refs_2_, bf16[1,96,768]{2,1,0:T(8,128)(2,1)S(1)} %collective-permute-done.2.refs_3_, ...), custom_call_target="tpu_custom_call" | custom-call | flops 1000000000 | bytes 3000000 | tf_op jit(solution)/shard_map/pallas_call | solution.py:251
  14.2 0.3 %collective-permute-done.7.refs_5_ = bf16[1,48,384]{2,1,0:T(8,128)(2,1)S(1)} collective-permute-done((bf16[1,48,384]{2,1,0:T(8,128)(2,1)S(1)}, bf16[1,48,384]{2,1,0:T(8,128)(2,1)S(1)}, u32[]{:S(2)}, u32[]{:S(2)}) %collective-permute-start.7) | collective-permute-done | bytes 36896 | tf_op jit(solution)/shard_map/ppermute | solution.py:81
  14.5 0.6 %shard_map.50 = f32[3,8,128]{2,1,0:T(8,128)S(1)} custom-call(bf16[1,96,768]{2,1,0:T(8,128)(2,1)S(1)} %copy-done, bf16[1,96,768]{2,1,0:T(8,128)(2,1)S(1)} %collective-permute-done.refs_1_, bf16[1,96,768]{2,1,0:T(8,128)(2,1)S(1)} %collective-permute-done.1.refs_2_, bf16[1,96,768]{2,1,0:T(8,128)(2,1)S(1)} %collective-permute-done.2.refs_3_, ...), custom_call_target="tpu_custom_call" | custom-call | tf_op jit(solution)/shard_map/pallas_call | solution.py:262
  15.1 0.2 collective-permute-start.8
  15.3 1.0 %collective-permute-done.8 = f32[3,8,128]{2,1,0:T(8,128)S(1)} collective-permute-done((f32[3,8,128]{2,1,0:T(8,128)S(1)}, f32[3,8,128]{2,1,0:T(8,128)S(1)}, u32[]{:S(2)}, u32[]{:S(2)}) %collective-permute-start.8) | collective-permute-done | bytes 12320 | tf_op jit(solution)/shard_map/ppermute | solution.py:81
  16.3 1.6 %collective-permute-start.11 = (f32[3,8,128]{2,1,0:T(8,128)S(1)}, f32[3,8,128]{2,1,0:T(8,128)S(1)}, u32[]{:S(2)}, u32[]{:S(2)}) collective-permute-start(f32[3,8,128]{2,1,0:T(8,128)S(1)} %add.3.refs_0_), channel_id=1, source_target_pairs={{0,6},{1,7},{2,4},{3,5},{4,2},{5,3},{6,0},{7,1},{8,14},{9,15},{10,... | collective-permute-start | bytes 36872 | tf_op jit(solution)/shard_map/ppermute | solution.py:29
  17.9 2.8 %collective-permute-start.9 = (f32[3,8,128]{2,1,0:T(8,128)S(1)}, f32[3,8,128]{2,1,0:T(8,128)S(1)}, u32[]{:S(2)}, u32[]{:S(2)}) collective-permute-start(f32[3,8,128]{2,1,0:T(8,128)S(1)} %add.3.refs_0_), channel_id=1, source_target_pairs={{0,4},{1,5},{2,6},{3,7},{4,0},{5,1},{6,2},{7,3},{8,12},{9,13},{10,... | collective-permute-start | bytes 36872 | tf_op jit(solution)/shard_map/ppermute | solution.py:29
  20.7 1.1 %collective-permute-done.11.refs_3_ = f32[3,8,128]{2,1,0:T(8,128)S(1)} collective-permute-done((f32[3,8,128]{2,1,0:T(8,128)S(1)}, f32[3,8,128]{2,1,0:T(8,128)S(1)}, u32[]{:S(2)}, u32[]{:S(2)}) %collective-permute-start.11) | collective-permute-done | bytes 12320 | tf_op jit(solution)/shard_map/ppermute | solution.py:29
  21.8 0.7 %collective-permute-done.9.refs_1_ = f32[3,8,128]{2,1,0:T(8,128)S(1)} collective-permute-done((f32[3,8,128]{2,1,0:T(8,128)S(1)}, f32[3,8,128]{2,1,0:T(8,128)S(1)}, u32[]{:S(2)}, u32[]{:S(2)}) %collective-permute-start.9) | collective-permute-done | bytes 12320 | tf_op jit(solution)/shard_map/ppermute | solution.py:29
  22.5 0.7 %shard_map.51 = f32[6,4,8,16]{3,2,1,0:T(8,128)} custom-call(f32[3,8,128]{2,1,0:T(8,128)S(1)} %add.3.refs_0_, f32[3,8,128]{2,1,0:T(8,128)S(1)} %collective-permute-done.9.refs_1_, f32[3,8,128]{2,1,0:T(8,128)S(1)} %collective-permute-done.10.refs_2_, f32[3,8,128]{2,1,0:T(8,128)S(1)} %collective-permute-done.11.refs_3_), custom_call_target="tpu_custom_call" | custom-call | tf_op jit(solution)/shard_map/pallas_call | solution.py:272
  (15 shorter events, 0.0 us)
Async XLA Ops:
  0.0 9.7 %copy-start.2 = (bf16[6,4,8,96]{3,2,1,0:T(8,128)(2,1)S(1)}, bf16[6,4,8,96]{3,2,1,0:T(8,128)(2,1)}, u32[]{:S(2)}) copy-start(bf16[6,4,8,96]{3,2,1,0:T(8,128)(2,1)} %param.5) | copy-start | bytes 110596
  0.0 9.1 %collective-permute-start.3 = (bf16[1,6,4,8,96]{4,3,2,1,0:T(8,128)(2,1)}, bf16[1,6,4,8,96]{4,3,2,1,0:T(8,128)(2,1)S(1)}, u32[]{:S(2)}, u32[]{:S(2)}) collective-permute-start(bf16[1,6,4,8,96]{4,3,2,1,0:T(8,128)(2,1)} %bitcast.2), channel_id=1, source_target_pairs={{0,4},{1,5},{2,6},{3,7},{4,0},{5,1},{6,2},{7,3},{8,12},{9,13},{10,... | collective-permute-start | bytes 110600 | tf_op jit(solution)/shard_map/ppermute | solution.py:65
  4.0 9.2 %collective-permute-start.2 = (bf16[1,96,768]{2,1,0:T(8,128)(2,1)}, bf16[1,96,768]{2,1,0:T(8,128)(2,1)S(1)}, u32[]{:S(2)}, u32[]{:S(2)}) collective-permute-start(bf16[1,96,768]{2,1,0:T(8,128)(2,1)} %refs_0_.3), channel_id=1, source_target_pairs={{0,24},{8,16},{16,8},{24,0},{1,25},{9,17},{17,9},{25,1},{2,26},{10... | collective-permute-start | bytes 442376 | tf_op jit(solution)/shard_map/ppermute | solution.py:25
  6.5 7.1 %collective-permute-start.1 = (bf16[1,96,768]{2,1,0:T(8,128)(2,1)}, bf16[1,96,768]{2,1,0:T(8,128)(2,1)S(1)}, u32[]{:S(2)}, u32[]{:S(2)}) collective-permute-start(bf16[1,96,768]{2,1,0:T(8,128)(2,1)} %refs_0_.3), channel_id=1, source_target_pairs={{0,16},{8,24},{16,0},{24,8},{1,17},{9,25},{17,1},{25,9},{2,18},{10... | collective-permute-start | bytes 442376 | tf_op jit(solution)/shard_map/ppermute | solution.py:25
  7.0 6.7 %collective-permute-start = (bf16[1,96,768]{2,1,0:T(8,128)(2,1)}, bf16[1,96,768]{2,1,0:T(8,128)(2,1)S(1)}, u32[]{:S(2)}, u32[]{:S(2)}) collective-permute-start(bf16[1,96,768]{2,1,0:T(8,128)(2,1)} %refs_0_.3), channel_id=1, source_target_pairs={{0,8},{8,0},{16,24},{24,16},{1,9},{9,1},{17,25},{25,17},{2,10},{10... | collective-permute-start | bytes 442376 | tf_op jit(solution)/shard_map/ppermute | solution.py:25
  7.5 4.3 %collective-permute-start.4 = (bf16[1,6,4,8,96]{4,3,2,1,0:T(8,128)(2,1)}, bf16[1,6,4,8,96]{4,3,2,1,0:T(8,128)(2,1)S(1)}, u32[]{:S(2)}, u32[]{:S(2)}) collective-permute-start(bf16[1,6,4,8,96]{4,3,2,1,0:T(8,128)(2,1)} %bitcast.3), channel_id=1, source_target_pairs={{0,2},{1,3},{2,0},{3,1},{4,6},{5,7},{6,4},{7,5},{8,10},{9,11},{10,... | collective-permute-start | bytes 110600 | tf_op jit(solution)/shard_map/ppermute | solution.py:65
  9.1 2.7 %copy-start.1 = (bf16[6,4,16,96]{3,2,1,0:T(8,128)(2,1)S(1)}, bf16[6,4,16,96]{3,2,1,0:T(8,128)(2,1)}, u32[]{:S(2)}) copy-start(bf16[6,4,16,96]{3,2,1,0:T(8,128)(2,1)} %refs_3_.1) | copy-start | bytes 221188
  9.1 2.7 %copy-start.3 = (s32[6,4]{0,1:T(4,128)S(1)}, s32[6,4]{0,1:T(4,128)}, u32[]{:S(2)}) copy-start(s32[6,4]{0,1:T(4,128)} %param.7) | copy-start | bytes 292
  9.2 4.5 %copy-start = (bf16[1,96,768]{2,1,0:T(8,128)(2,1)S(1)}, bf16[1,96,768]{2,1,0:T(8,128)(2,1)}, u32[]{:S(2)}) copy-start(bf16[1,96,768]{2,1,0:T(8,128)(2,1)} %refs_0_.3) | copy-start | bytes 442372
  9.2 4.0 %collective-permute-start.6 = (bf16[1,48,384]{2,1,0:T(8,128)(2,1)S(1)}, bf16[1,48,384]{2,1,0:T(8,128)(2,1)S(1)}, u32[]{:S(2)}, u32[]{:S(2)}) collective-permute-start(bf16[1,48,384]{2,1,0:T(8,128)(2,1)S(1)} %shard_map.47.refs_1_), channel_id=1, source_target_pairs={{0,2},{1,3},{2,0},{3,1},{4,6},{5,7},{6,4},{7,5},{8,10},{9,11},{10,... | collective-permute-start | bytes 110600 | tf_op jit(solution)/shard_map/ppermute | solution.py:65
  12.5 1.9 %collective-permute-start.5 = (bf16[3,48,384]{2,1,0:T(8,128)(2,1)S(1)}, bf16[3,48,384]{2,1,0:T(8,128)(2,1)S(1)}, u32[]{:S(2)}, u32[]{:S(2)}) collective-permute-start(bf16[3,48,384]{2,1,0:T(8,128)(2,1)S(1)} %get-tuple-element.7.refs_4_), channel_id=1, source_target_pairs={{0,1},{1,0},{2,3},{3,2},{4,5},{5,4},{6,7},{7,6},{8,9},{9,8},{10,11... | collective-permute-start | bytes 331784 | tf_op jit(solution)/shard_map/ppermute | solution.py:81
  13.2 1.2 %collective-permute-start.7 = (bf16[1,48,384]{2,1,0:T(8,128)(2,1)S(1)}, bf16[1,48,384]{2,1,0:T(8,128)(2,1)S(1)}, u32[]{:S(2)}, u32[]{:S(2)}) collective-permute-start(bf16[1,48,384]{2,1,0:T(8,128)(2,1)S(1)} %collective-permute-done.6.refs_5_), channel_id=1, source_target_pairs={{0,1},{1,0},{2,3},{3,2},{4,5},{5,4},{6,7},{7,6},{8,9},{9,8},{10,11... | collective-permute-start | bytes 110600 | tf_op jit(solution)/shard_map/ppermute | solution.py:81
  15.1 1.2 %collective-permute-start.8 = (f32[3,8,128]{2,1,0:T(8,128)S(1)}, f32[3,8,128]{2,1,0:T(8,128)S(1)}, u32[]{:S(2)}, u32[]{:S(2)}) collective-permute-start(f32[3,8,128]{2,1,0:T(8,128)S(1)} %shard_map.50), channel_id=1, source_target_pairs={{0,1},{1,0},{2,3},{3,2},{4,5},{5,4},{6,7},{7,6},{8,9},{9,8},{10,11... | collective-permute-start | bytes 36872 | tf_op jit(solution)/shard_map/ppermute | solution.py:81
  16.3 5.5 %collective-permute-start.11 = (f32[3,8,128]{2,1,0:T(8,128)S(1)}, f32[3,8,128]{2,1,0:T(8,128)S(1)}, u32[]{:S(2)}, u32[]{:S(2)}) collective-permute-start(f32[3,8,128]{2,1,0:T(8,128)S(1)} %add.3.refs_0_), channel_id=1, source_target_pairs={{0,6},{1,7},{2,4},{3,5},{4,2},{5,3},{6,0},{7,1},{8,14},{9,15},{10,... | collective-permute-start | bytes 36872 | tf_op jit(solution)/shard_map/ppermute | solution.py:29
  17.9 3.9 %collective-permute-start.10 = (f32[3,8,128]{2,1,0:T(8,128)S(1)}, f32[3,8,128]{2,1,0:T(8,128)S(1)}, u32[]{:S(2)}, u32[]{:S(2)}) collective-permute-start(f32[3,8,128]{2,1,0:T(8,128)S(1)} %add.3.refs_0_), channel_id=1, source_target_pairs={{0,2},{1,3},{2,0},{3,1},{4,6},{5,7},{6,4},{7,5},{8,10},{9,11},{10,... | collective-permute-start | bytes 36872 | tf_op jit(solution)/shard_map/ppermute | solution.py:29
  17.9 4.6 %collective-permute-start.9 = (f32[3,8,128]{2,1,0:T(8,128)S(1)}, f32[3,8,128]{2,1,0:T(8,128)S(1)}, u32[]{:S(2)}, u32[]{:S(2)}) collective-permute-start(f32[3,8,128]{2,1,0:T(8,128)S(1)} %add.3.refs_0_), channel_id=1, source_target_pairs={{0,4},{1,5},{2,6},{3,7},{4,0},{5,1},{6,2},{7,3},{8,12},{9,13},{10,... | collective-permute-start | bytes 36872 | tf_op jit(solution)/shard_map/ppermute | solution.py:29
